TPU v7x, 32 devices: a whole 2x2x4 slice. The times are simulated.
32 devices in a mesh: dp: 4 (over y, x), ctx: 2 (over core), mp: 4 (over z).
Axes of the slice: x: 2, y: 2, z: 4, core: 2. Of those that a mesh axis runs over, the one named last changes fastest.
Arguments:
- inputs: bfloat16 [2, 4, 1024, 2304], P(None, 'dp', 'ctx'), may hold values from -6 to 6
- segment_ids: int32 [2, 4, 1024], P(None, 'dp'), may hold values from 0 to 15, as said below
- positions: int32 [2, 4, 1024], P(None, 'dp', 'ctx'), may hold values from 0 to 1023, as said below
- cotangent: bfloat16 [2, 4, 1024, 2304], P(None, 'dp', 'ctx'), may hold values from -6 to 6
- w_query: float32 [2304, 2048], P(('dp', 'ctx'), 'mp'), may hold values from -0.125 to 0.125
- key_weight: float32 [2304, 1024], P(('dp', 'ctx'), 'mp'), may hold values from -0.125 to 0.125
- value_weight: float32 [2304, 1024], P(('dp', 'ctx'), 'mp'), may hold values from -0.125 to 0.125
- w_output: float32 [2304, 2048], P(('dp', 'ctx'), 'mp'), may hold values from -0.25 to 0.25
- w_gate: float32 [2304, 9216], P(('dp', 'ctx'), 'mp'), may hold values from -0.125 to 0.125
- w_up: float32 [2304, 9216], P(('dp', 'ctx'), 'mp'), may hold values from -0.125 to 0.125
- w_down: float32 [2304, 9216], P(('dp', 'ctx'), 'mp'), may hold values from -0.0625 to 0.0625
- gain_attn: float32 [2304], P(('dp', 'ctx')), may hold values from -0.7 to 1.7
- gain_post_attn: float32 [2304], P(('dp', 'ctx')), may hold values from -2.5 to 2.5
- gain_ffn: float32 [2304], P(('dp', 'ctx')), may hold values from -0.7 to 1.7
- gain_post_ffn: float32 [2304], P(('dp', 'ctx')), may hold values from -2.5 to 2.5
- m_query: float32 [2304, 2048], P(('dp', 'ctx'), 'mp'), may hold values from -0.0017089844 to 0.0017089844
- key_momentum: float32 [2304, 1024], P(('dp', 'ctx'), 'mp'), may hold values from -0.0017089844 to 0.0017089844
- value_momentum: float32 [2304, 1024], P(('dp', 'ctx'), 'mp'), may hold values from -0.0017089844 to 0.0017089844
- m_output: float32 [2304, 2048], P(('dp', 'ctx'), 'mp'), may hold values from -0.0017089844 to 0.0017089844
- m_gate: float32 [2304, 9216], P(('dp', 'ctx'), 'mp'), may hold values from -0.0017089844 to 0.0017089844
- m_up: float32 [2304, 9216], P(('dp', 'ctx'), 'mp'), may hold values from -0.0017089844 to 0.0017089844
- m_down: float32 [2304, 9216], P(('dp', 'ctx'), 'mp'), may hold values from -0.0017089844 to 0.0017089844
- m_gain_attn: float32 [2304], P(('dp', 'ctx')), may hold values from -0.0017089844 to 0.0017089844
- m_gain_post_attn: float32 [2304], P(('dp', 'ctx')), may hold values from -0.0017089844 to 0.0017089844
- m_gain_ffn: float32 [2304], P(('dp', 'ctx')), may hold values from -0.0017089844 to 0.0017089844
- m_gain_post_ffn: float32 [2304], P(('dp', 'ctx')), may hold values from -0.0017089844 to 0.0017089844
Outputs:
- output: bfloat16 [2, 4, 1024, 2304], P(None, 'dp', 'ctx')
- input_grad: bfloat16 [2, 4, 1024, 2304], P(None, 'dp', 'ctx')
- grad_norm: float32 [1], replicated
- update_query: float32 [2304, 2048], P(('dp', 'ctx'), 'mp')
- update_key: float32 [2304, 1024], P(('dp', 'ctx'), 'mp')
- update_value: float32 [2304, 1024], P(('dp', 'ctx'), 'mp')
- update_output: float32 [2304, 2048], P(('dp', 'ctx'), 'mp')
- update_gate: float32 [2304, 9216], P(('dp', 'ctx'), 'mp')
- update_up: float32 [2304, 9216], P(('dp', 'ctx'), 'mp')
- update_down: float32 [2304, 9216], P(('dp', 'ctx'), 'mp')
- mom_query: float32 [2304, 2048], P(('dp', 'ctx'), 'mp')
- mom_key: float32 [2304, 1024], P(('dp', 'ctx'), 'mp')
- mom_value: float32 [2304, 1024], P(('dp', 'ctx'), 'mp')
- mom_output: float32 [2304, 2048], P(('dp', 'ctx'), 'mp')
- mom_gate: float32 [2304, 9216], P(('dp', 'ctx'), 'mp')
- mom_up: float32 [2304, 9216], P(('dp', 'ctx'), 'mp')
- mom_down: float32 [2304, 9216], P(('dp', 'ctx'), 'mp')
- mom_gain_attn: float32 [2304], P(('dp', 'ctx'))
- mom_gain_post_attn: float32 [2304], P(('dp', 'ctx'))
- mom_gain_ffn: float32 [2304], P(('dp', 'ctx'))
- mom_gain_post_ffn: float32 [2304], P(('dp', 'ctx'))
Inputs may be any that keep to these rules, and one draw needn't show every extreme that they name: `segment_ids`: within each sequence the ids start at 0 at the first token and never fall; each new id starts a new document. `positions`: A token's offset from the first token of its document.
All inputs are finite; a program needn't handle non-finite values.
Results may differ from a plain program's by a relative error of at most 0.02.
Values may be sent and summed in bfloat16 or wider, within the bound.
A program may use at most 384 MiB of HBM per device.

v0:
```python
import math

import jax
import jax.numpy as jnp
from jax import lax
from jax.sharding import PartitionSpec as P

HEAD_SIZE = 256
STEP = 10


epsilon = 1e-06
softcap = 50.0
decay_steps = 1000.0
base_rate = 1.0


def rms_scale(value_rows, gain_vec):
    inverse = lax.rsqrt(jnp.mean(value_rows * value_rows, axis=-1, keepdims=True) + epsilon)
    return value_rows * inverse * (1.0 + gain_vec)


def rotary_embedding(vectors, token_position):
    half_dim = vectors.shape[-1] // 2
    frequency = jnp.exp(
        jnp.arange(half_dim, dtype=jnp.float32) * (-2.0 * math.log(10000.0) / vectors.shape[-1])
    )
    angles = token_position.astype(jnp.float32)[..., None, None] * frequency
    cosine = jnp.cos(angles)
    sine_part = jnp.sin(angles)
    first_half = vectors[..., :half_dim]
    second = vectors[..., half_dim:]
    return jnp.concatenate(
        [first_half * cosine - second * sine_part, second * cosine + first_half * sine_part],
        axis=-1,
    )


def soft_probs(raw_scores, allowed):
    capped = softcap * jnp.tanh(raw_scores / softcap)
    masked = jnp.where(allowed, capped, -1e30)
    return jax.nn.softmax(masked, axis=-1)


def gated(gate_pre, up_pre):
    return jax.nn.gelu(gate_pre, approximate=True) * up_pre


def project(input_activity, weight_matrix):
    return jnp.einsum(
        "qbf,fx->qbx", input_activity, weight_matrix, preferred_element_type=jnp.float32
    )


def project_back(incoming_gradient, weight_matrix):
    return jnp.einsum(
        "fam,xm->fax", incoming_gradient, weight_matrix, preferred_element_type=jnp.float32
    )


def weight_grad(left_row_block, right_row_block):
    return jnp.einsum(
        "rxo,rxm->om", left_row_block, right_row_block, preferred_element_type=jnp.float32
    )


def per_device(
    inputs,
    segment_ids,
    positions,
    cotangent,
    w_query,
    key_weight,
    value_weight,
    w_output,
    w_gate,
    w_up,
    w_down,
    gain_attn,
    gain_post_attn,
    gain_ffn,
    gain_post_ffn,
    m_query,
    key_momentum,
    value_momentum,
    m_output,
    m_gate,
    m_up,
    m_down,
    m_gain_attn,
    m_gain_post_attn,
    m_gain_ffn,
    m_gain_post_ffn,
):
    masters = (
        w_query,
        key_weight,
        value_weight,
        w_output,
        w_gate,
        w_up,
        w_down,
        gain_attn,
        gain_post_attn,
        gain_ffn,
        gain_post_ffn,
    )
    moments = (
        m_query,
        key_momentum,
        value_momentum,
        m_output,
        m_gate,
        m_up,
        m_down,
        m_gain_attn,
        m_gain_post_attn,
        m_gain_ffn,
        m_gain_post_ffn,
    )
    seq_count = inputs.shape[1]
    local_len = inputs.shape[2]
    full_len = segment_ids.shape[2]
    score_scale = HEAD_SIZE ** (-0.5)
    ctx_start = lax.axis_index("ctx") * local_len
    query_index = ctx_start + jnp.arange(local_len)
    key_index = jnp.arange(full_len)
    causal = query_index[:, None] >= key_index[None, :]

    def run_batch(micro_batch, gathered):
        query_full, key_full, value_full, output_full, gate_full, up_full, down_full = gathered[:7]
        gain_one, gain_two, gain_three, gain_four = [
            gain_low.astype(jnp.float32) for gain_low in gathered[7:]
        ]
        residual_in = inputs[micro_batch].astype(jnp.float32)
        seg_full = segment_ids[micro_batch]
        seg_local = lax.dynamic_slice_in_dim(seg_full, ctx_start, local_len, 1)
        allowed = (causal[None] & (seg_local[:, :, None] == seg_full[:, None, :]))[:, None, None]
        pos_local = positions[micro_batch]
        attn_in = rms_scale(residual_in, gain_one).astype(jnp.bfloat16)
        query_proj = project(attn_in, query_full).reshape(seq_count, local_len, -1, HEAD_SIZE)
        key_projected = project(attn_in, key_full).reshape(seq_count, local_len, -1, HEAD_SIZE)
        value_projected = project(attn_in, value_full)
        query_rows = rotary_embedding(query_proj, pos_local).astype(jnp.bfloat16)
        keys_local = rotary_embedding(key_projected, pos_local).astype(jnp.bfloat16)
        values_local = value_projected.astype(jnp.bfloat16).reshape(
            seq_count, local_len, -1, HEAD_SIZE
        )
        keys_all, values_all = (
            lax.all_gather(keys_local, "ctx", axis=1, tiled=True),
            lax.all_gather(values_local, "ctx", axis=1, tiled=True),
        )
        kv_heads = keys_all.shape[2]
        repeat = query_rows.shape[2] // kv_heads
        grouped_heads = query_rows.reshape(seq_count, local_len, kv_heads, repeat, HEAD_SIZE)
        raw_scores = (
            jnp.einsum(
                "sqkrd,stkd->skrqt", grouped_heads, keys_all, preferred_element_type=jnp.float32
            )
            * score_scale
        )
        attn_probs, soft_back = jax.vjp(lambda scores: soft_probs(scores, allowed), raw_scores)
        probs_low = attn_probs.astype(jnp.bfloat16)
        heads_out = (
            jnp.einsum(
                "skrqt,stkd->sqkrd", probs_low, values_all, preferred_element_type=jnp.float32
            )
            .astype(jnp.bfloat16)
            .reshape(seq_count, local_len, -1)
        )
        attn_sum = lax.psum(project_back(heads_out, output_full), "mp")
        attn_norm, attn_norm_back = jax.vjp(rms_scale, attn_sum, gain_two)
        middle = residual_in + attn_norm
        mid_norm, mid_norm_back = jax.vjp(rms_scale, middle, gain_three)
        ffn_in = mid_norm.astype(jnp.bfloat16)
        gate_pre = project(ffn_in, gate_full)
        up_pre = project(ffn_in, up_full)
        hidden_f, gate_back = jax.vjp(gated, gate_pre, up_pre)
        hidden = hidden_f.astype(jnp.bfloat16)
        ffn_sum = lax.psum(project_back(hidden, down_full), "mp")
        ffn_norm, ffn_norm_back = jax.vjp(rms_scale, ffn_sum, gain_four)
        final = (middle + ffn_norm).astype(jnp.bfloat16)
        grad_final = cotangent[micro_batch].astype(jnp.float32)
        grad_ffn, grad_gain_four = ffn_norm_back(grad_final)
        grad_ffn_low = grad_ffn.astype(jnp.bfloat16)
        grad_hidden = project(grad_ffn_low, down_full)
        grad_down = weight_grad(grad_ffn_low, hidden)
        grad_gate_f, grad_up_f = gate_back(grad_hidden)
        grad_gate_low = grad_gate_f.astype(jnp.bfloat16)
        grad_up_low = grad_up_f.astype(jnp.bfloat16)
        grad_ffn_in = lax.psum(
            project_back(grad_gate_low, gate_full) + project_back(grad_up_low, up_full), "mp"
        )
        grad_gate = weight_grad(ffn_in, grad_gate_low)
        grad_up = weight_grad(ffn_in, grad_up_low)
        grad_mid_norm, grad_gain_three = mid_norm_back(grad_ffn_in)
        grad_middle = grad_final + grad_mid_norm
        grad_attn, grad_gain_two = attn_norm_back(grad_middle)
        grad_attn_low = grad_attn.astype(jnp.bfloat16)
        grad_heads = project(grad_attn_low, output_full).astype(jnp.bfloat16)
        grad_output = weight_grad(grad_attn_low, heads_out)
        grad_heads_g = grad_heads.reshape(seq_count, local_len, kv_heads, repeat, HEAD_SIZE)
        grad_probs = jnp.einsum(
            "sqkrd,stkd->skrqt", grad_heads_g, values_all, preferred_element_type=jnp.float32
        )
        grad_raw = soft_back(grad_probs)[0].astype(jnp.bfloat16)
        grad_values_all = jnp.einsum(
            "skrqt,sqkrd->stkd", probs_low, grad_heads_g, preferred_element_type=jnp.float32
        )
        grad_queries = (
            jnp.einsum("skrqt,stkd->sqkrd", grad_raw, keys_all, preferred_element_type=jnp.float32)
            * score_scale
        )
        grad_keys_all = (
            jnp.einsum(
                "skrqt,sqkrd->stkd", grad_raw, grouped_heads, preferred_element_type=jnp.float32
            )
            * score_scale
        )
        grad_keys, grad_values = (
            lax.psum_scatter(
                grad_keys_all.astype(jnp.bfloat16), "ctx", scatter_dimension=1, tiled=True
            ).astype(jnp.float32),
            lax.psum_scatter(
                grad_values_all.astype(jnp.bfloat16), "ctx", scatter_dimension=1, tiled=True
            ).astype(jnp.float32),
        )
        rotate_back = jax.vjp(lambda projected: rotary_embedding(projected, pos_local), query_proj)[
            1
        ]
        grad_query_proj = (
            rotate_back(grad_queries.reshape(seq_count, local_len, -1, HEAD_SIZE))[0]
            .reshape(seq_count, local_len, -1)
            .astype(jnp.bfloat16)
        )
        key_rotate_back = jax.vjp(
            lambda projected: rotary_embedding(projected, pos_local), key_projected
        )[1]
        grad_key_proj = (
            key_rotate_back(grad_keys)[0].reshape(seq_count, local_len, -1).astype(jnp.bfloat16)
        )
        grad_value_proj = grad_values.reshape(seq_count, local_len, -1).astype(jnp.bfloat16)
        grad_attn_in = lax.psum(
            (
                project_back(grad_query_proj, query_full)
                + project_back(grad_key_proj, key_full)
                + project_back(grad_value_proj, value_full)
            ).astype(jnp.bfloat16),
            "mp",
        ).astype(jnp.float32)
        grad_query = weight_grad(attn_in, grad_query_proj)
        grad_key = weight_grad(attn_in, grad_key_proj)
        grad_value = weight_grad(attn_in, grad_value_proj)
        in_norm_back = jax.vjp(rms_scale, residual_in, gain_one)[1]
        grad_in_norm, grad_gain_one = in_norm_back(grad_attn_in)
        input_grad = (grad_middle + grad_in_norm).astype(jnp.bfloat16)
        grads = (
            grad_query,
            grad_key,
            grad_value,
            grad_output,
            grad_gate,
            grad_up,
            grad_down,
            grad_gain_one,
            grad_gain_two,
            grad_gain_three,
            grad_gain_four,
        )
        return (final, input_grad, grads)

    shared = (
        lax.all_gather(w_query.astype(jnp.bfloat16), ("dp", "ctx"), axis=0, tiled=True),
        lax.all_gather(key_weight.astype(jnp.bfloat16), ("dp", "ctx"), axis=0, tiled=True),
        lax.all_gather(value_weight.astype(jnp.bfloat16), ("dp", "ctx"), axis=0, tiled=True),
        lax.all_gather(w_output.astype(jnp.bfloat16), ("dp", "ctx"), axis=0, tiled=True),
        lax.all_gather(w_gate.astype(jnp.bfloat16), ("dp", "ctx"), axis=0, tiled=True),
        lax.all_gather(w_up.astype(jnp.bfloat16), ("dp", "ctx"), axis=0, tiled=True),
        lax.all_gather(w_down.astype(jnp.bfloat16), ("dp", "ctx"), axis=0, tiled=True),
        lax.all_gather(gain_attn.astype(jnp.bfloat16), ("dp", "ctx"), axis=0, tiled=True),
        lax.all_gather(gain_post_attn.astype(jnp.bfloat16), ("dp", "ctx"), axis=0, tiled=True),
        lax.all_gather(gain_ffn.astype(jnp.bfloat16), ("dp", "ctx"), axis=0, tiled=True),
        lax.all_gather(gain_post_ffn.astype(jnp.bfloat16), ("dp", "ctx"), axis=0, tiled=True),
    )
    outputs_list = []
    input_grads_list = []
    summed = None
    for micro_batch in range(inputs.shape[0]):
        final, input_grad, grads = run_batch(micro_batch, shared)
        outputs_list.append(final)
        input_grads_list.append(input_grad)
        summed = (
            grads
            if summed is None
            else tuple((earlier + later for earlier, later in zip(summed, grads)))
        )
    summed = (
        lax.psum_scatter(
            summed[0].astype(jnp.bfloat16), ("dp", "ctx"), scatter_dimension=0, tiled=True
        ).astype(jnp.float32),
        lax.psum_scatter(
            summed[1].astype(jnp.bfloat16), ("dp", "ctx"), scatter_dimension=0, tiled=True
        ).astype(jnp.float32),
        lax.psum_scatter(
            summed[2].astype(jnp.bfloat16), ("dp", "ctx"), scatter_dimension=0, tiled=True
        ).astype(jnp.float32),
        lax.psum_scatter(
            summed[3].astype(jnp.bfloat16), ("dp", "ctx"), scatter_dimension=0, tiled=True
        ).astype(jnp.float32),
        lax.psum_scatter(
            summed[4].astype(jnp.bfloat16), ("dp", "ctx"), scatter_dimension=0, tiled=True
        ).astype(jnp.float32),
        lax.psum_scatter(
            summed[5].astype(jnp.bfloat16), ("dp", "ctx"), scatter_dimension=0, tiled=True
        ).astype(jnp.float32),
        lax.psum_scatter(
            summed[6].astype(jnp.bfloat16), ("dp", "ctx"), scatter_dimension=0, tiled=True
        ).astype(jnp.float32),
        lax.psum_scatter(
            summed[7].astype(jnp.bfloat16), ("dp", "ctx"), scatter_dimension=0, tiled=True
        ).astype(jnp.float32),
        lax.psum_scatter(
            summed[8].astype(jnp.bfloat16), ("dp", "ctx"), scatter_dimension=0, tiled=True
        ).astype(jnp.float32),
        lax.psum_scatter(
            summed[9].astype(jnp.bfloat16), ("dp", "ctx"), scatter_dimension=0, tiled=True
        ).astype(jnp.float32),
        lax.psum_scatter(
            summed[10].astype(jnp.bfloat16), ("dp", "ctx"), scatter_dimension=0, tiled=True
        ).astype(jnp.float32),
    )
    weight_sq = sum((jnp.sum(grad_part * grad_part) for grad_part in summed[:7]))
    gain_sq = sum((jnp.sum(grad_part * grad_part) for grad_part in summed[7:]))
    first_core = (lax.axis_index("mp") == 0).astype(jnp.float32)
    global_sq = lax.psum(weight_sq + first_core * gain_sq, ("dp", "ctx", "mp"))
    norm_value = jnp.sqrt(global_sq)
    factor = 1.0 / jnp.maximum(norm_value, 1.0)
    rate_now = base_rate / math.sqrt(1.0 + STEP / decay_steps)
    new_moments = tuple(
        (0.5 * moment + 0.5 * factor * grad_part for moment, grad_part in zip(moments, summed))
    )
    changes = tuple(
        (
            -rate_now * (new_moment + 0.01 * weight_arr)
            for weight_arr, new_moment in zip(masters[:7], new_moments[:7])
        )
    )
    output = jnp.stack(outputs_list, axis=0)
    input_grads = jnp.stack(input_grads_list, axis=0)
    return (
        output,
        input_grads,
        norm_value.reshape(1),
        changes[0],
        changes[1],
        changes[2],
        changes[3],
        changes[4],
        changes[5],
        changes[6],
        new_moments[0],
        new_moments[1],
        new_moments[2],
        new_moments[3],
        new_moments[4],
        new_moments[5],
        new_moments[6],
        new_moments[7],
        new_moments[8],
        new_moments[9],
        new_moments[10],
    )


def solution(mesh):
    return jax.shard_map(
        per_device,
        mesh=mesh,
        in_specs=(
            P(None, "dp", "ctx", None),
            P(None, "dp", None),
            P(None, "dp", "ctx"),
            P(None, "dp", "ctx", None),
            P(("dp", "ctx"), "mp"),
            P(("dp", "ctx"), "mp"),
            P(("dp", "ctx"), "mp"),
            P(("dp", "ctx"), "mp"),
            P(("dp", "ctx"), "mp"),
            P(("dp", "ctx"), "mp"),
            P(("dp", "ctx"), "mp"),
            P(("dp", "ctx")),
            P(("dp", "ctx")),
            P(("dp", "ctx")),
            P(("dp", "ctx")),
            P(("dp", "ctx"), "mp"),
            P(("dp", "ctx"), "mp"),
            P(("dp", "ctx"), "mp"),
            P(("dp", "ctx"), "mp"),
            P(("dp", "ctx"), "mp"),
            P(("dp", "ctx"), "mp"),
            P(("dp", "ctx"), "mp"),
            P(("dp", "ctx")),
            P(("dp", "ctx")),
            P(("dp", "ctx")),
            P(("dp", "ctx")),
        ),
        out_specs=(
            P(None, "dp", "ctx", None),
            P(None, "dp", "ctx", None),
            P(),
            P(("dp", "ctx"), "mp"),
            P(("dp", "ctx"), "mp"),
            P(("dp", "ctx"), "mp"),
            P(("dp", "ctx"), "mp"),
            P(("dp", "ctx"), "mp"),
            P(("dp", "ctx"), "mp"),
            P(("dp", "ctx"), "mp"),
            P(("dp", "ctx"), "mp"),
            P(("dp", "ctx"), "mp"),
            P(("dp", "ctx"), "mp"),
            P(("dp", "ctx"), "mp"),
            P(("dp", "ctx"), "mp"),
            P(("dp", "ctx"), "mp"),
            P(("dp", "ctx"), "mp"),
            P(("dp", "ctx")),
            P(("dp", "ctx")),
            P(("dp", "ctx")),
            P(("dp", "ctx")),
        ),
        check_vma=False,
    )
```

profile of v0, /device:TPU:0, one launch (start us, length us, event | category | flops | bytes accessed | tf_op | source)
XLA Modules:
  0.0 2207.2 jit_solution(16579028572243263208)
XLA Ops:
  23.7 26.2 %all-reduce.20 = (bf16[2304]{0:T(1024)(128)(2,1)S(1)}, bf16[2304]{0:T(1024)(128)(2,1)S(1)}, bf16[2304]{0:T(1024)(128)(2,1)S(1)}, bf16[2304]{0:T(1024)(128)(2,1)}) all-reduce(bf16[2304]{0:T(1024)(128)(2,1)S(1)} %dynamic-update-slice, bf16[2304]{0:T(1024)(128)(2,1)S(1)} %dynamic-update-slice.1, ...), channel_id=1, replica_groups=mesh['dp'=4,'ctx'=2,'mp'=4] {'dp','ctx'}, use_global_device_ids=true, to_apply=%add.8 | all-reduce | flops 9216 | bytes 36864
  76.7 18.8 all-gather.14.cloned.1.call-done
  95.5 4.6 copy.64
  115.2 11.6 all-gather.16.cloned.1.call-done
  126.9 16.4 convolution_bitcast_fusion.1
  155.2 317.2 %all-reduce.31.cloned.1.call-done = (f32[1,512,2304]{2,1,0:T(8,128)}, f32[1,512,2304]{2,1,0:T(8,128)}) async-done(((f32[1,512,2304]{2,1,0:T(8,128)}, f32[1,512,2304]{2,1,0:T(8,128)}), (f32[1,512,2304]{2,1,0:T(8,128)}, f32[1,512,2304]{2,1,0:T(8,128)})) %all-reduce.31.cloned.1.call-update) | async-done | bytes 9437200 | tf_op jit(solution)/shard_map/psum | solution.py:171
  489.5 48.1 %all-gather.18.cloned.1.call-done = bf16[2304,2304]{1,0:T(8,128)(2,1)} async-done(((bf16[288,2304]{1,0:T(8,128)(2,1)}), bf16[2304,2304]{1,0:T(8,128)(2,1)}) %all-gather.18.cloned.1.call-update) | async-done | bytes 10616848 | tf_op jit(solution)/shard_map/all_gather | solution.py:277
  537.6 11.8 fusion.312
  549.4 7.3 fusion.313
  556.6 47.3 %all-gather.20.cloned.1.call-done = bf16[2304,2304]{1,0:T(8,128)(2,1)} async-done(((bf16[288,2304]{1,0:T(8,128)(2,1)}), bf16[2304,2304]{1,0:T(8,128)(2,1)}) %all-gather.20.cloned.1.call-update) | async-done | bytes 10616848 | tf_op jit(solution)/shard_map/all_gather | solution.py:278
  603.9 12.6 multiply_convert_fusion.2
  617.1 7.7 multiply_convert_fusion.4
  624.8 45.4 %all-gather.22.cloned.1.call-done = bf16[2304,2304]{1,0:T(8,128)(2,1)} async-done(((bf16[288,2304]{1,0:T(8,128)(2,1)}), bf16[2304,2304]{1,0:T(8,128)(2,1)}) %all-gather.22.cloned.1.call-update) | async-done | bytes 10616848 | tf_op jit(solution)/shard_map/all_gather | solution.py:279
  670.2 11.9 convolution_bitcast_fusion
  682.1 7.6 convolution_bitcast_fusion.2
  690.3 324.9 %all-reduce.29.cloned.1.call-done = (f32[1,512,2304]{2,1,0:T(8,128)}, f32[1,512,2304]{2,1,0:T(8,128)}) async-done(((f32[1,512,2304]{2,1,0:T(8,128)}, f32[1,512,2304]{2,1,0:T(8,128)}), (f32[1,512,2304]{2,1,0:T(8,128)}, f32[1,512,2304]{2,1,0:T(8,128)})) %all-reduce.29.cloned.1.call-update) | async-done | bytes 9437200 | tf_op jit(solution)/shard_map/psum | solution.py:180
  1020.4 6.5 fusion.58
  1026.9 8.2 fusion.101
  1035.2 14.2 multiply_convert_fusion.1
  1049.5 13.1 fusion.314
  1062.6 15.0 multiply_convert_fusion
  1077.6 9.5 fusion.315
  1087.1 12.2 fusion.16
  1099.3 12.2 fusion.17
  1112.2 323.9 %all-reduce.27.cloned.1.call-done = (f32[1,512,2304]{2,1,0:T(8,128)}, f32[1,512,2304]{2,1,0:T(8,128)}) async-done(((f32[1,512,2304]{2,1,0:T(8,128)}, f32[1,512,2304]{2,1,0:T(8,128)}), (f32[1,512,2304]{2,1,0:T(8,128)}, f32[1,512,2304]{2,1,0:T(8,128)})) %all-reduce.27.cloned.1.call-update) | async-done | bytes 9437200 | tf_op jit(solution)/shard_map/psum | solution.py:191
  1436.1 8.7 multiply_reduce_fusion.1
  1445.0 16.0 multiply_reduce_fusion.3
  1461.0 6.2 fusion.100
  1473.8 6.3 fusion.79
  1489.2 4.8 fusion.65
  1497.1 4.8 fusion.67
  1509.3 4.7 fusion.83
  1556.8 12.3 fusion.317
  1569.2 13.0 add_convert_fusion.2
  1582.2 12.3 fusion.318
  1594.5 12.5 add_convert_fusion.1
  1607.3 12.6 fusion.319
  1619.9 12.8 add_convert_fusion
  1642.1 5.1 reduce-scatter.20.cloned.1.call-done
  1650.9 42.4 %reduce-scatter.26.cloned.1.call-done = bf16[288,512]{1,0:T(8,128)(2,1)} async-done(((bf16[2304,512]{1,0:T(8,128)(2,1)}), bf16[288,512]{1,0:T(8,128)(2,1)}) %reduce-scatter.26.cloned.1.call-update) | async-done | bytes 294928 | tf_op jit(solution)/shard_map/reduce_scatter | solution.py:307
  1695.7 172.4 %all-reduce.33.cloned.1.call-done = (bf16[1,512,2304]{2,1,0:T(8,128)(2,1)}, bf16[1,512,2304]{2,1,0:T(8,128)(2,1)}) async-done(((bf16[1,512,2304]{2,1,0:T(8,128)(2,1)}, bf16[1,512,2304]{2,1,0:T(8,128)(2,1)}), (bf16[1,512,2304]{2,1,0:T(8,128)(2,1)}, bf16[1,512,2304]{2,1,0:T(8,128)(2,1)})) %all-reduce.33.cloned.1.call-update) | async-done | bytes 4718608 | tf_op jit(solution)/shard_map/psum | solution.py:243
  1868.0 7.6 fusion.20
  1875.6 24.5 %all-reduce.19 = (bf16[2304]{0:T(1024)(128)(2,1)S(1)}, bf16[2304]{0:T(1024)(128)(2,1)S(1)}, bf16[2304]{0:T(1024)(128)(2,1)S(1)}, bf16[2304]{0:T(1024)(128)(2,1)S(1)}) all-reduce(bf16[2304]{0:T(1024)(128)(2,1)S(1)} %add_convert_fusion.14, ...), channel_id=15, replica_groups=mesh['dp'=4,'ctx'=2,'mp'=4] {'dp','ctx'}, use_global_device_ids=true, to_apply=%region_50.51.clone | all-reduce | flops 9216 | bytes 36864
  1904.2 9.8 fusion.99
  1914.1 38.5 %reduce-scatter.28.cloned.1.call-done = bf16[288,2304]{1,0:T(8,128)(2,1)} async-done(((bf16[2304,2304]{1,0:T(8,128)(2,1)}), bf16[288,2304]{1,0:T(8,128)(2,1)}) %reduce-scatter.28.cloned.1.call-update) | async-done | bytes 1327120 | tf_op jit(solution)/shard_map/reduce_scatter | solution.py:310
  1955.9 82.5 %reduce-scatter.30.cloned.1.call-done = bf16[288,2304]{1,0:T(8,128)(2,1)} async-done(((bf16[2304,2304]{1,0:T(8,128)(2,1)}), bf16[288,2304]{1,0:T(8,128)(2,1)}) %reduce-scatter.30.cloned.1.call-update) | async-done | bytes 1327120 | tf_op jit(solution)/shard_map/reduce_scatter | solution.py:313
  2041.6 82.5 %reduce-scatter.32.cloned.1.call-done = bf16[288,2304]{1,0:T(8,128)(2,1)} async-done(((bf16[2304,2304]{1,0:T(8,128)(2,1)}), bf16[288,2304]{1,0:T(8,128)(2,1)}) %reduce-scatter.32.cloned.1.call-update) | async-done | bytes 1327120 | tf_op jit(solution)/shard_map/reduce_scatter | solution.py:316
  2131.8 39.3 %psum.71 = f32[]{:T(128)} all-reduce(f32[]{:T(128)S(6)} %add.462), channel_id=1, replica_groups=mesh['dp'=4,'ctx'=2,'mp'=4] {'dp','ctx','mp'}, use_global_device_ids=true, to_apply=%region_64.65 | all-reduce | flops 1 | bytes 8 | tf_op jit(solution)/shard_map/psum | solution.py:335
  (542 shorter events, 214.2 us)
Async XLA Ops:
  7.2 45.8 %all-gather.10.cloned.1.call-start = ((), (), s32[]{:S(2)}) async-start(), calls=%async_computation.11 | async-start | bytes 1327104 | tf_op jit(solution)/shard_map/all_gather | solution.py:275
  8.9 55.1 %all-gather.12.cloned.1.call-start = ((), (), s32[]{:S(2)}) async-start(), calls=%async_computation.12 | async-start | bytes 1327104 | tf_op jit(solution)/shard_map/all_gather | solution.py:274
  10.6 84.9 %all-gather.14.cloned.1.call-start = ((), (), s32[]{:S(2)}) async-start(), calls=%async_computation.13 | async-start | bytes 2654208 | tf_op jit(solution)/shard_map/all_gather | solution.py:273
  12.5 114.4 %all-gather.16.cloned.1.call-start = ((), (), s32[]{:S(2)}) async-start(), calls=%async_computation.14 | async-start | bytes 2654208 | tf_op jit(solution)/shard_map/all_gather | solution.py:276
  14.4 458.0 %all-reduce.31.cloned.1.call-start = ((), (), s32[]{:S(2)}) async-start(), calls=%async_computation.31 | async-start | bytes 18874368 | tf_op jit(solution)/shard_map/psum | solution.py:171
  14.5 55.3 %copy-start.131 = (f32[128]{0:T(128)}, f32[128]{0:T(128)S(1)}, u32[]{:S(2)}) copy-start(f32[128]{0:T(128)S(1)} %multiply_exponential_fusion) | copy-start | bytes 1540
  18.0 51.9 %copy-start.97 = (f32[1,1,512]{2,1,0:T(1,128)}, f32[1,1,512]{2,1,0:T(1,128)S(1)}, u32[]{:S(2)}) copy-start(f32[1,1,512]{2,1,0:T(1,128)S(1)} %get-tuple-element.120) | copy-start | bytes 6148
  18.0 51.9 %copy-start.99 = (f32[1,1,512]{2,1,0:T(1,128)}, f32[1,1,512]{2,1,0:T(1,128)S(1)}, u32[]{:S(2)}) copy-start(f32[1,1,512]{2,1,0:T(1,128)S(1)} %get-tuple-element.121) | copy-start | bytes 6148
  21.4 78.7 %copy-start.109 = (f32[512]{0:T(512)}, f32[512]{0:T(512)S(1)}, u32[]{:S(2)}) copy-start(f32[512]{0:T(512)S(1)} %fusion.277) | copy-start | bytes 6148
  21.4 82.9 %copy-start.111 = (f32[512]{0:T(512)}, f32[512]{0:T(512)S(1)}, u32[]{:S(2)}) copy-start(f32[512]{0:T(512)S(1)} %fusion.281) | copy-start | bytes 6148
  49.9 54.5 %copy-start.85 = (f32[2304]{0:T(1024)}, f32[2304]{0:T(1024)S(1)}, u32[]{:S(2)}) copy-start(f32[2304]{0:T(1024)S(1)} %convert_add_fusion.5) | copy-start | bytes 27652
  51.9 52.3 %copy-start.44 = (f32[512,128]{0,1:T(8,128)}, f32[512,128]{0,1:T(8,128)S(1)}, u32[]{:S(2)}) copy-start(f32[512,128]{0,1:T(8,128)S(1)} %get-tuple-element.122) | copy-start | bytes 786436
  51.9 52.3 %copy-start.46 = (f32[512,128]{0,1:T(8,128)}, f32[512,128]{0,1:T(8,128)S(1)}, u32[]{:S(2)}) copy-start(f32[512,128]{0,1:T(8,128)S(1)} %get-tuple-element.123) | copy-start | bytes 786436
  51.9 54.2 %copy-start.48 = (f32[512,128]{0,1:T(8,128)}, f32[512,128]{0,1:T(8,128)S(1)}, u32[]{:S(2)}) copy-start(f32[512,128]{0,1:T(8,128)S(1)} %get-tuple-element.132) | copy-start | bytes 786436
  51.9 54.2 %copy-start.50 = (f32[512,128]{0,1:T(8,128)}, f32[512,128]{0,1:T(8,128)S(1)}, u32[]{:S(2)}) copy-start(f32[512,128]{0,1:T(8,128)S(1)} %get-tuple-element.133) | copy-start | bytes 786436
  52.9 58.5 %copy-start.28 = (pred[512,1024]{0,1:T(8,128)(4,1)}, pred[512,1024]{0,1:T(8,128)(4,1)S(1)}, u32[]{:S(2)}) copy-start(pred[512,1024]{0,1:T(8,128)(4,1)S(1)} %get-tuple-element.126) | copy-start | bytes 1572868
  52.9 60.4 %copy-start.30 = (pred[512,1024]{0,1:T(8,128)(4,1)}, pred[512,1024]{0,1:T(8,128)(4,1)S(1)}, u32[]{:S(2)}) copy-start(pred[512,1024]{0,1:T(8,128)(4,1)S(1)} %get-tuple-element.127) | copy-start | bytes 1572868
  146.9 390.7 %all-gather.18.cloned.1.call-start = ((), (), s32[]{:S(2)}) async-start(), calls=%async_computation.15 | async-start | bytes 11943936 | tf_op jit(solution)/shard_map/all_gather | solution.py:277
  150.1 453.8 %all-gather.20.cloned.1.call-start = ((), (), s32[]{:S(2)}) async-start(), calls=%async_computation.16 | async-start | bytes 11943936 | tf_op jit(solution)/shard_map/all_gather | solution.py:278
  151.4 518.8 %all-gather.22.cloned.1.call-start = ((), (), s32[]{:S(2)}) async-start(), calls=%async_computation.17 | async-start | bytes 11943936 | tf_op jit(solution)/shard_map/all_gather | solution.py:279
  155.1 860.1 %all-reduce.29.cloned.1.call-start = ((), (), s32[]{:S(2)}) async-start(), calls=%async_computation.30 | async-start | bytes 18874368 | tf_op jit(solution)/shard_map/psum | solution.py:180
  155.2 324.0 %copy-start.81 = (f32[2304]{0:T(1024)}, f32[2304]{0:T(1024)S(1)}, u32[]{:S(2)}) copy-start(f32[2304]{0:T(1024)S(1)} %convert_add_fusion.4) | copy-start | bytes 27652
  155.2 324.0 %slice-start.8 = ((s8[4718592]{0:T(1024)(128)(4,1)}), s8[524288]{0:T(1024)(128)(4,1)S(1)}, s32[]{:S(2)}) async-start(s8[4718592]{0:T(1024)(128)(4,1)} %bitcast.527), calls=%async_computation.41 | async-start | bytes 1048576
  155.2 328.9 %copy-start.83 = (f32[2304]{0:T(1024)}, f32[2304]{0:T(1024)S(1)}, u32[]{:S(2)}) copy-start(f32[2304]{0:T(1024)S(1)} %convert_add_fusion.3) | copy-start | bytes 27652
  489.5 114.4 %copy-start.41 = (bf16[512,2304]{1,0:T(8,128)(2,1)}, bf16[512,2304]{1,0:T(8,128)(2,1)S(1)}, u32[]{:S(2)}) copy-start(bf16[512,2304]{1,0:T(8,128)(2,1)S(1)} %get-tuple-element.117) | copy-start | bytes 7077892
  624.8 57.3 %copy-start.146 = (bf16[512,2304]{1,0:T(8,128)(2,1)}, bf16[512,2304]{1,0:T(8,128)(2,1)S(1)}, u32[]{:S(2)}) copy-start(bf16[512,2304]{1,0:T(8,128)(2,1)S(1)} %get-tuple-element.142) | copy-start | bytes 7077892
  689.7 746.4 %all-reduce.27.cloned.1.call-start = ((), (), s32[]{:S(2)}) async-start(), calls=%async_computation.29 | async-start | bytes 18874368 | tf_op jit(solution)/shard_map/psum | solution.py:191
  1049.4 49.9 %copy-start.147 = (bf16[512,2304]{1,0:T(8,128)(2,1)}, bf16[512,2304]{1,0:T(8,128)(2,1)S(1)}, u32[]{:S(2)}) copy-start(bf16[512,2304]{1,0:T(8,128)(2,1)S(1)} %get-tuple-element.79) | copy-start | bytes 7077892
  1111.5 324.6 %copy-start.84 = (f32[2304]{0:T(1024)S(1)}, f32[2304]{0:T(1024)}, u32[]{:S(2)}) copy-start(f32[2304]{0:T(1024)} %copy-done.83) | copy-start | bytes 27652
  1111.5 324.6 %copy-start.106 = (f32[512]{0:T(512)S(1)}, f32[512]{0:T(512)}, u32[]{:S(2)}) copy-start(f32[512]{0:T(512)} %copy-done.105) | copy-start | bytes 6148
  1111.5 324.6 %copy-start.108 = (f32[512]{0:T(512)S(1)}, f32[512]{0:T(512)}, u32[]{:S(2)}) copy-start(f32[512]{0:T(512)} %copy-done.107) | copy-start | bytes 6148
  1111.5 333.4 %slice-start.2 = ((s8[4718592]{0:T(1024)(128)(4,1)}), s8[524288]{0:T(1024)(128)(4,1)S(1)}, s32[]{:S(2)}) async-start(s8[4718592]{0:T(1024)(128)(4,1)} %bitcast.521), calls=%async_computation.35 | async-start | bytes 1048576
  1111.5 393.5 %reduce-scatter.14.cloned.1.call-start = ((), (), s32[]{:S(2)}) async-start(), calls=%async_computation.19 | async-start | bytes 786432 | tf_op jit(solution)/shard_map/reduce_scatter | solution.py:224
  1473.3 36.0 %reduce-scatter.18.cloned.1.call-start = ((), (), s32[]{:S(2)}) async-start(), calls=%async_computation.21 | async-start | bytes 786432 | tf_op jit(solution)/shard_map/reduce_scatter | solution.py:224
  1489.1 28.5 %reduce-scatter.16.cloned.1.call-start = ((), (), s32[]{:S(2)}) async-start(), calls=%async_computation.20 | async-start | bytes 786432 | tf_op jit(solution)/shard_map/reduce_scatter | solution.py:221
  1497.0 23.2 %reduce-scatter.12.cloned.1.call-start = ((), (), s32[]{:S(2)}) async-start(), calls=%async_computation.18 | async-start | bytes 786432 | tf_op jit(solution)/shard_map/reduce_scatter | solution.py:221
  1504.8 134.1 %reduce-scatter.24.cloned.1.call-start = ((), (), s32[]{:S(2)}) async-start(), calls=%async_computation.24 | async-start | bytes 1327104 | tf_op jit(solution)/shard_map/reduce_scatter | solution.py:304
  1514.0 126.5 %reduce-scatter.22.cloned.1.call-start = ((), (), s32[]{:S(2)}) async-start(), calls=%async_computation.23 | async-start | bytes 1327104 | tf_op jit(solution)/shard_map/reduce_scatter | solution.py:301
  1528.9 118.3 %reduce-scatter.20.cloned.1.call-start = ((), (), s32[]{:S(2)}) async-start(), calls=%async_computation.22 | async-start | bytes 2654208 | tf_op jit(solution)/shard_map/reduce_scatter | solution.py:298
  1538.3 155.0 %reduce-scatter.26.cloned.1.call-start = ((), (), s32[]{:S(2)}) async-start(), calls=%async_computation.25 | async-start | bytes 2654208 | tf_op jit(solution)/shard_map/reduce_scatter | solution.py:307
  1544.8 323.3 %all-reduce.33.cloned.1.call-start = ((), (), s32[]{:S(2)}) async-start(), calls=%async_computation.32 | async-start | bytes 9437184 | tf_op jit(solution)/shard_map/psum | solution.py:243
  1556.3 396.3 %reduce-scatter.28.cloned.1.call-start = ((), (), s32[]{:S(2)}) async-start(), calls=%async_computation.26 | async-start | bytes 11943936 | tf_op jit(solution)/shard_map/reduce_scatter | solution.py:310
  1582.1 456.2 %reduce-scatter.30.cloned.1.call-start = ((), (), s32[]{:S(2)}) async-start(), calls=%async_computation.27 | async-start | bytes 11943936 | tf_op jit(solution)/shard_map/reduce_scatter | solution.py:313
  1607.1 517.0 %reduce-scatter.32.cloned.1.call-start = ((), (), s32[]{:S(2)}) async-start(), calls=%async_computation.28 | async-start | bytes 11943936 | tf_op jit(solution)/shard_map/reduce_scatter | solution.py:316
  1914.0 213.3 %copy-start.19 = (bf16[1,1,512,2304]{3,2,1,0:T(8,128)(2,1)S(1)}, bf16[1,1,512,2304]{3,2,1,0:T(8,128)(2,1)}, u32[]{:S(2)}) copy-start(bf16[1,1,512,2304]{3,2,1,0:T(8,128)(2,1)} %get-tuple-element.90) | copy-start | bytes 7077892
  2127.4 50.0 %copy-start.60 = (f32[288,256]{1,0:T(8,128)S(1)}, f32[288,256]{1,0:T(8,128)}, u32[]{:S(2)}) copy-start(f32[288,256]{1,0:T(8,128)} %param.32) | copy-start | bytes 884740
  2127.5 53.9 %copy-start.40 = (f32[288,512]{1,0:T(8,128)S(1)}, f32[288,512]{1,0:T(8,128)}, u32[]{:S(2)}) copy-start(f32[288,512]{1,0:T(8,128)} %param.33) | copy-start | bytes 1769476
  2131.8 54.5 %copy-start.12 = (f32[288,2304]{1,0:T(8,128)S(1)}, f32[288,2304]{1,0:T(8,128)}, u32[]{:S(2)}) copy-start(f32[288,2304]{1,0:T(8,128)} %param.35) | copy-start | bytes 7962628
  (147 other events, 1262.0 us)
Sparse Core Ops, SparseCore 0:
  10.5 26.8 all-gather.9
  39.9 24.0 all-gather.11
  66.5 29.0 all-gather.13
  97.8 29.0 all-gather.15
  147.0 325.3 all-reduce.30
  474.8 62.8 all-gather.17
  540.1 63.8 all-gather.19
  606.4 63.8 all-gather.21
  689.8 325.3 all-reduce.28
  1111.7 324.3 all-reduce.26
  1473.5 6.9 reduce-scatter.13
  1489.3 7.0 reduce-scatter.17
  1499.2 9.1 reduce-scatter.15
  1511.1 9.0 reduce-scatter.11
  1523.3 37.9 reduce-scatter.23
  1564.7 36.7 reduce-scatter.21
  1604.7 42.4 reduce-scatter.19
  1650.8 42.4 reduce-scatter.25
  1695.7 172.2 all-reduce.32
  1871.4 81.1 reduce-scatter.27
  1956.1 82.2 reduce-scatter.29
  2041.9 82.2 reduce-scatter.31
where the time goes:
time: 2210 us
  waiting for transfers between devices  1560 us (71%)
  matrix products  316 us (14%)
  other arithmetic  174 us (8%)
  blocking collectives  99.2 us (4%)
  between operations  27.4 us (1%)
  local copies, waits for them, and re-layouts  25 us (1%)
    psum x1, waiting for transfers between devices, run_batch(): ffn_sum = lax.psum(project_back(hidden, down_full), 'mp')  325 us
    psum x1, waiting for transfers between devices, run_batch(): lax.psum(project_back(grad_gate_low, gate_full) + project_back(grad_up_lo...  324 us
    psum x1, waiting for transfers between devices, run_batch(): attn_sum = lax.psum(project_back(heads_out, output_full), 'mp')  317 us
    psum x1, waiting for transfers between devices, run_batch(): lax.psum((project_back(grad_query_proj, query_full) + project_back(grad_k...  172 us
    dot_general x14, matrix products, weight_grad(): jnp.einsum('rxo,rxm->om', left_row_block, right_row_block, preferred_elem...  100 us
    dot_general x14, matrix products, project_back(): jnp.einsum('fam,xm->fax', incoming_gradient, weight_matrix, preferred_ele...  96.9 us
    dot_general x14, matrix products, project(): jnp.einsum('qbf,fx->qbx', input_activity, weight_matrix, preferred_elemen...  88.5 us
    reduce_scatter x1, waiting for transfers between devices, per_device(): lax.psum_scatter(summed[5].astype(jnp.bfloat16), ('dp', 'ctx'), scatter_d...  82.5 us
  transfers between devices with their start and end apart: 22, of which 16 were waited for; matrix products, arithmetic and copies ran while one was open for 13% of the time, Pallas kernels for 0%

commit v1 on v0

v1 whole, which is shorter than its diff:
```python
import math

import jax
import jax.numpy as jnp
from jax import lax
from jax.sharding import PartitionSpec as P

HEAD = 256
STEP = 10
EPS = 1e-06
CAP = 50.0
RATE = 1.0 / math.sqrt(1.0 + STEP / 1000.0)
SCALE = HEAD ** (-0.5)
BF = jnp.bfloat16
F32 = jnp.float32


def flip(axis, size, mask):
    return dict(axis_name=axis, perm=[(i, i ^ mask) for i in range(size)])


def after(value, other):
    return lax.optimization_barrier((value, other))[0]


def gather_rows(own, sizes, wait):
    dp, ctx = sizes["dp"], sizes["ctx"]
    rows, cols = own.shape
    if wait is not None:
        own = after(own, wait)
    if dp != 4:
        out = lax.all_gather(own, ("dp", "ctx"), axis=0, tiled=True)
        return out, own
    me = lax.axis_index("dp")
    half = rows // 2 // 16 * 16
    from_x = lax.ppermute(own, **flip("dp", dp, 1))
    from_y = lax.ppermute(own, **flip("dp", dp, 2))
    far_top = lax.ppermute(from_y[:half], **flip("dp", dp, 1))
    far_low = lax.ppermute(from_x[half:], **flip("dp", dp, 2))
    mine = jnp.zeros((dp, rows, cols), own.dtype)
    mine = lax.dynamic_update_slice(mine, own[None], (me, 0, 0))
    mine = lax.dynamic_update_slice(mine, from_x[None], (me ^ 1, 0, 0))
    mine = lax.dynamic_update_slice(mine, from_y[None], (me ^ 2, 0, 0))
    mine = lax.dynamic_update_slice(mine, far_top[None], (me ^ 3, 0, 0))
    mine = lax.dynamic_update_slice(mine, far_low[None], (me ^ 3, half, 0))
    if ctx == 2:
        other = lax.ppermute(mine, **flip("ctx", ctx, 1))
        core = lax.axis_index("ctx")
        out = jnp.zeros((dp, ctx, rows, cols), own.dtype)
        out = lax.dynamic_update_slice(out, mine[:, None], (0, core, 0, 0))
        out = lax.dynamic_update_slice(out, other[:, None], (0, 1 - core, 0, 0))
    else:
        out = lax.all_gather(mine, "ctx", axis=1)
    return out.reshape(dp * ctx * rows, cols), from_x


def scatter_rows(full, sizes, wait):
    dp, ctx = sizes["dp"], sizes["ctx"]
    full = full.astype(BF)
    if wait is not None:
        full = after(full, wait)
    rows = full.shape[0] // (dp * ctx)
    cols = full.shape[1]
    if dp != 4:
        out = lax.psum_scatter(full, ("dp", "ctx"), scatter_dimension=0, tiled=True)
        return out.astype(F32), out
    blocks = full.reshape(dp, ctx, rows, cols)
    if ctx == 2:
        core = lax.axis_index("ctx")
        send = lax.dynamic_index_in_dim(blocks, 1 - core, 1, keepdims=False)
        keep = lax.dynamic_index_in_dim(blocks, core, 1, keepdims=False)
        got = lax.ppermute(send, **flip("ctx", ctx, 1))
    else:
        keep = lax.psum_scatter(blocks, "ctx", scatter_dimension=1, tiled=False)
        got = None
    me = lax.axis_index("dp")
    half = rows // 2 // 16 * 16

    def part(mask, low, high):
        size = (1, high - low, cols)
        piece = lax.dynamic_slice(keep, (me ^ mask, low, 0), size)[0].astype(F32)
        if got is not None:
            piece = piece + lax.dynamic_slice(got, (me ^ mask, low, 0), size)[0].astype(F32)
        return piece

    far_top = lax.ppermute(part(3, 0, half).astype(BF), **flip("dp", dp, 1))
    far_low = lax.ppermute(part(3, half, rows).astype(BF), **flip("dp", dp, 2))
    to_y = jnp.concatenate([part(2, 0, half) + far_top.astype(F32), part(2, half, rows)])
    to_x = jnp.concatenate([part(1, 0, half), part(1, half, rows) + far_low.astype(F32)])
    by_y = lax.ppermute(to_y.astype(BF), **flip("dp", dp, 2))
    by_x = lax.ppermute(to_x.astype(BF), **flip("dp", dp, 1))
    total = part(0, 0, rows) + by_x.astype(F32) + by_y.astype(F32)
    return total, far_top


def sum_mp(part, sizes):
    if sizes["mp"] != 4:
        return lax.psum(part, "mp")
    place = lax.axis_index("mp")
    inner = (place == 1) | (place == 2)
    near = lax.ppermute(part, "mp", [(0, 1), (3, 2)])
    pair = (part.astype(F32) + near.astype(F32)).astype(BF)
    across = lax.ppermute(pair, "mp", [(1, 2), (2, 1)])
    total = (pair.astype(F32) + across.astype(F32)).astype(BF)
    back = lax.ppermute(total, "mp", [(1, 0), (2, 3)])
    return jnp.where(inner, total, back)


def sum_small(value, axes, sizes):
    for axis in axes:
        size = sizes[axis]
        step = 1
        while step < size:
            value = value + lax.ppermute(value, **flip(axis, size, step))
            step *= 2
    return value


def swap_ctx(local, sizes):
    if sizes["ctx"] != 2:
        return lax.all_gather(local, "ctx", axis=0, tiled=True)
    other = lax.ppermute(local, **flip("ctx", 2, 1))
    first = lax.axis_index("ctx") == 0
    return jnp.concatenate([jnp.where(first, local, other), jnp.where(first, other, local)])


def scatter_ctx(full, sizes):
    if sizes["ctx"] != 2:
        return lax.psum_scatter(full.astype(BF), "ctx", scatter_dimension=0, tiled=True).astype(F32)
    core = lax.axis_index("ctx")
    rows = full.shape[0] // 2
    send = lax.dynamic_slice_in_dim(full, (1 - core) * rows, rows).astype(BF)
    keep = lax.dynamic_slice_in_dim(full, core * rows, rows)
    return keep.astype(BF).astype(F32) + lax.ppermute(send, **flip("ctx", 2, 1)).astype(F32)


def dot(a, b):
    return lax.dot_general(a, b, (((1,), (0,)), ((), ())), preferred_element_type=F32)


def dot_t(a, b):
    return lax.dot_general(a, b, (((1,), (1,)), ((), ())), preferred_element_type=F32)


def t_dot(a, b):
    return lax.dot_general(a, b, (((0,), (0,)), ((), ())), preferred_element_type=F32)


def inverse_rms(v):
    return lax.rsqrt(jnp.mean(v * v, axis=-1, keepdims=True) + EPS)


def norm_back(v, r, gain, dy):
    scaled = (1.0 + gain) * dy
    mean = jnp.mean(scaled * v, axis=-1, keepdims=True)
    return r * scaled - v * (r * r * r) * mean, jnp.sum(v * r * dy, axis=0)


def rotate(v, cosine, sine):
    a, b = v[:, : HEAD // 2], v[:, HEAD // 2 :]
    return jnp.concatenate([a * cosine - b * sine, b * cosine + a * sine], axis=1)


GELU_C = math.sqrt(2.0 / math.pi)


def gelu_parts(u):
    tanh = jnp.tanh(GELU_C * (u + 0.044715 * u * u * u))
    value = 0.5 * u * (1.0 + tanh)
    slope = 0.5 * (1.0 + tanh) + 0.5 * u * (1.0 - tanh * tanh) * GELU_C * (
        1.0 + 3.0 * 0.044715 * u * u
    )
    return value, slope


def attend(queries, keys, values, allowed):
    raw = dot_t(queries, keys) * SCALE
    tanh = jnp.tanh(raw / CAP)
    heads = queries.shape[0] // allowed.shape[0]
    mask = jnp.concatenate([allowed] * heads, axis=0)
    weight = jnp.where(mask, jnp.exp(CAP * tanh), 0.0)
    probs = weight / jnp.sum(weight, axis=1, keepdims=True)
    out = dot(probs.astype(BF), values).astype(BF)
    return out, (probs, tanh)


def attend_back(saved, queries, keys, values, d_out):
    probs, tanh = saved
    d_probs = dot_t(d_out, values)
    inner = jnp.sum(probs * d_probs, axis=1, keepdims=True)
    d_raw = (probs * (d_probs - inner) * (1.0 - tanh * tanh)).astype(BF)
    d_queries = dot(d_raw, keys) * SCALE
    d_keys = t_dot(d_raw, queries) * SCALE
    d_values = t_dot(probs.astype(BF), d_out)
    return d_queries, d_keys, d_values


def per_device(
    sizes,
    inputs,
    segment_ids,
    positions,
    cotangent,
    *params,
):
    masters, moments = params[:11], params[11:]
    batches, seqs, tokens, width = inputs.shape
    assert seqs == 1
    full_len = segment_ids.shape[2]
    q_cols, k_cols = masters[0].shape[1], masters[1].shape[1]
    heads = q_cols // HEAD
    assert k_cols == HEAD
    cuts = 2 if tokens >= 512 else 1
    unit = tokens // cuts

    low = [w.astype(BF) for w in masters[:7]]
    qkv_own = jnp.concatenate(low[:3], axis=1)
    gains_own = jnp.stack([g.astype(BF) for g in masters[7:]], axis=1)
    gains = lax.all_gather(gains_own, ("dp", "ctx"), axis=0, tiled=True).astype(F32)
    gain_one, gain_two, gain_three, gain_four = [gains[:, i] for i in range(4)]
    w_qkv, mark = gather_rows(qkv_own, sizes, None)
    w_out, mark = gather_rows(low[3], sizes, mark)
    w_gate, mark = gather_rows(low[4], sizes, mark)
    w_up, mark = gather_rows(low[5], sizes, mark)
    w_down, mark = gather_rows(low[6], sizes, mark)

    start = lax.axis_index("ctx") * tokens
    causal = (start + jnp.arange(tokens))[:, None] >= jnp.arange(full_len)[None, :]
    frequency = jnp.exp(
        jnp.arange(HEAD // 2, dtype=F32) * (-2.0 * math.log(10000.0) / HEAD)
    )

    state = []
    for mb in range(batches):
        x = inputs[mb, 0].astype(F32)
        r_one = inverse_rms(x)
        attn_in = (x * r_one * (1.0 + gain_one)).astype(BF)
        angles = positions[mb, 0].astype(F32)[:, None] * frequency
        cosine, sine = jnp.cos(angles), jnp.sin(angles)
        seg = segment_ids[mb, 0]
        seg_local = lax.dynamic_slice_in_dim(seg, start, tokens)
        allowed = causal & (seg_local[:, None] == seg[None, :])
        proj = dot(attn_in, w_qkv)
        queries = jnp.concatenate(
            [rotate(proj[:, h * HEAD : (h + 1) * HEAD], cosine, sine) for h in range(heads)]
        ).astype(BF)
        keys = rotate(proj[:, q_cols : q_cols + HEAD], cosine, sine).astype(BF)
        values = proj[:, q_cols + HEAD :].astype(BF)
        both = swap_ctx(jnp.concatenate([keys, values], axis=1), sizes)
        keys_all, values_all = both[:, :HEAD], both[:, HEAD:]
        out, saved = attend(queries, keys_all, values_all, allowed)
        heads_out = jnp.concatenate(jnp.split(out, heads, axis=0), axis=1)
        state.append(
            dict(
                x=x, r_one=r_one, attn_in=attn_in, cosine=cosine, sine=sine, queries=queries,
                keys=keys_all, values=values_all, saved=saved, heads_out=heads_out,
            )
        )

    units = [(mb, cut) for mb in range(batches) for cut in range(cuts)]
    work = []
    for mb, cut in units:
        rows = slice(cut * unit, (cut + 1) * unit)
        part = dot_t(state[mb]["heads_out"][rows], w_out).astype(BF)
        work.append(dict(rows=rows, mb=mb, attn_low=sum_mp(part, sizes)))
    for w in work:
        attn = w["attn_low"].astype(F32)
        r_two = inverse_rms(attn)
        mid = state[w["mb"]]["x"][w["rows"]] + attn * r_two * (1.0 + gain_two)
        r_three = inverse_rms(mid)
        ffn_in = (mid * r_three * (1.0 + gain_three)).astype(BF)
        gate, up = dot(ffn_in, w_gate), dot(ffn_in, w_up)
        value, slope = gelu_parts(gate)
        hidden = (value * up).astype(BF)
        part = dot_t(hidden, w_down).astype(BF)
        w.update(
            mid=mid, r_two=r_two, r_three=r_three, ffn_in=ffn_in, gate=gate, up=up, hidden=hidden,
            ffn_low=sum_mp(part, sizes),
        )
    for w in work:
        ffn = w["ffn_low"].astype(F32)
        r_four = inverse_rms(ffn)
        grad = cotangent[w["mb"], 0][w["rows"]].astype(F32)
        w["output"] = (w["mid"] + ffn * r_four * (1.0 + gain_four)).astype(BF)
        d_ffn, w["g_four"] = norm_back(ffn, r_four, gain_four, grad)
        d_ffn = d_ffn.astype(BF)
        d_hidden = dot(d_ffn, w_down)
        value, slope = gelu_parts(w["gate"])
        d_gate = (d_hidden * w["up"] * slope).astype(BF)
        d_up = (d_hidden * value).astype(BF)
        part = (dot_t(d_gate, w_gate) + dot_t(d_up, w_up)).astype(BF)
        w.update(grad=grad, d_ffn=d_ffn, d_gate=d_gate, d_up=d_up, d_in_low=sum_mp(part, sizes))
    for w in work:
        d_in = w["d_in_low"].astype(F32)
        back, w["g_three"] = norm_back(w["mid"], w["r_three"], gain_three, d_in)
        d_mid = w["grad"] + back
        attn = w["attn_low"].astype(F32)
        d_attn, w["g_two"] = norm_back(attn, w["r_two"], gain_two, d_mid)
        d_attn = d_attn.astype(BF)
        w.update(d_mid=d_mid, d_attn=d_attn, d_heads=dot(d_attn, w_out).astype(BF))

    def rows_of(key):
        return jnp.concatenate([w[key] for w in work])

    ffn_in = rows_of("ffn_in")
    g_down = t_dot(rows_of("d_ffn"), rows_of("hidden"))
    g_gate = t_dot(ffn_in, rows_of("d_gate"))
    g_up = t_dot(ffn_in, rows_of("d_up"))
    s_down, mark = scatter_rows(g_down, sizes, None)
    s_gate, mark = scatter_rows(g_gate, sizes, mark)
    s_up, mark = scatter_rows(g_up, sizes, mark)

    for mb in range(batches):
        s = state[mb]
        d_heads = jnp.concatenate([w["d_heads"] for w in work if w["mb"] == mb])
        d_out = jnp.concatenate(jnp.split(d_heads, heads, axis=1))
        d_queries, d_keys, d_values = attend_back(
            s["saved"], s["queries"], s["keys"], s["values"], d_out
        )
        d_kv = scatter_ctx(jnp.concatenate([d_keys, d_values], axis=1), sizes)
        pieces = [rotate(q, s["cosine"], -s["sine"]) for q in jnp.split(d_queries, heads)]
        pieces += [rotate(d_kv[:, :HEAD], s["cosine"], -s["sine"]), d_kv[:, HEAD:]]
        s["d_proj"] = jnp.concatenate(pieces, axis=1).astype(BF)
    for w in work:
        part = dot_t(state[w["mb"]]["d_proj"][w["rows"]], w_qkv).astype(BF)
        w["d_attn_in"] = sum_mp(part, sizes)

    g_out = t_dot(rows_of("d_attn"), jnp.concatenate([s["heads_out"] for s in state]))
    g_qkv = t_dot(
        jnp.concatenate([s["attn_in"] for s in state]),
        jnp.concatenate([s["d_proj"] for s in state]),
    )
    s_out, mark = scatter_rows(g_out, sizes, mark)
    s_qkv, mark = scatter_rows(g_qkv, sizes, mark)

    for w in work:
        s = state[w["mb"]]
        back, w["g_one"] = norm_back(
            s["x"][w["rows"]], s["r_one"][w["rows"]], gain_one, w["d_attn_in"].astype(F32)
        )
        w["input_grad"] = (w["d_mid"] + back).astype(BF)

    gain_grads = jnp.stack(
        [sum(w[key] for w in work) for key in ("g_one", "g_two", "g_three", "g_four")]
    )
    gain_grads = sum_small(gain_grads, ("ctx", "dp"), sizes)
    summed = (
        s_qkv[:, :q_cols], s_qkv[:, q_cols : q_cols + k_cols], s_qkv[:, q_cols + k_cols :],
        s_out, s_gate, s_up, s_down,
    )
    weight_sq = sum(jnp.sum(g * g) for g in (s_qkv, s_out, s_gate, s_up, s_down))
    weight_sq = sum_small(weight_sq.reshape(1, 1), ("ctx", "dp", "mp"), sizes)[0, 0]
    norm_value = jnp.sqrt(weight_sq + jnp.sum(gain_grads * gain_grads))
    factor = 1.0 / jnp.maximum(norm_value, 1.0)
    own = masters[7].shape[0]
    place = (lax.axis_index("dp") * sizes["ctx"] + lax.axis_index("ctx")) * own
    own_gains = lax.dynamic_slice_in_dim(gain_grads, place, own, 1)
    summed += tuple(own_gains[i] for i in range(4))
    new_moments = tuple(0.5 * m + 0.5 * factor * g for m, g in zip(moments, summed))
    changes = tuple(-RATE * (m + 0.01 * w) for w, m in zip(masters[:7], new_moments[:7]))

    def whole(key):
        return rows_of(key).reshape(inputs.shape)

    return (
        whole("output"), whole("input_grad"), norm_value.reshape(1), *changes, *new_moments
    )


def solution(mesh):
    sizes = dict(mesh.shape)
    weight, vector = P(("dp", "ctx"), "mp"), P(("dp", "ctx"))
    params = (weight,) * 7 + (vector,) * 4
    data = P(None, "dp", "ctx", None)

    def run(*args):
        return per_device(sizes, *args)

    return jax.shard_map(
        run,
        mesh=mesh,
        in_specs=(data, P(None, "dp", None), P(None, "dp", "ctx"), data) + params + params,
        out_specs=(data, data, P()) + (weight,) * 7 + params,
        check_vma=False,
    )
```

time: 2210 us -> 1600 us (0.72)
  waiting for transfers between devices: 1560 us -> 841 us
  starting transfers between devices: 2.28 us -> 131 us
  blocking collectives: 99.2 us -> 8.22 us
  local copies, waits for them, and re-layouts: 25 us -> 112 us
  matrix products: 316 us -> 277 us
  other arithmetic: 174 us -> 207 us
    psum x4 -> x0, waiting for transfers between devices: 1140 us -> none  [the longest x1 325 us: run_batch(): ffn_sum = lax.psum(project_back(hidden, down_full), 'mp')]
    ppermute x0 -> x110, waiting for transfers between devices: none -> 841 us  [the longest x16 395 us: sum_mp(): back = lax.ppermute(total, 'mp', [(1, 0), (2, 3)])]
    reduce_scatter x11 -> x0, waiting for transfers between devices: 253 us -> none  [the longest x1 82.5 us: per_device(): lax.psum_scatter(summed[5].astype(jnp.bfloat16), ('dp', 'ctx'), scatter_d...]
    all_gather x7 -> x0, waiting for transfers between devices: 172 us -> none  [the longest x1 48.1 us: per_device(): lax.all_gather(w_gate.astype(jnp.bfloat16), ('dp', 'ctx'), axis=0, tiled=...]
    ppermute x0 -> x110, starting transfers between devices: none -> 131 us  [the longest x16 34.2 us: sum_mp(): near = lax.ppermute(part, 'mp', [(0, 1), (3, 2)])]
    unnamed x2 -> x0, blocking collectives: 50.7 us -> none
    dynamic_update_slice x0 -> x33, local copies, waits for them, and re-layouts: none -> 50.4 us  [the longest x4 18.2 us: gather_rows(): out = lax.dynamic_update_slice(out, other[:, None], (0, 1 - core, 0, 0))]
    convert_element_type x22 -> x62, other arithmetic: 31.5 us -> 74.3 us  [the longest x16 19.1 us: sum_mp(): pair = (part.astype(F32) + near.astype(F32)).astype(BF)]
  transfers between devices with their start and end apart: 22 -> 110, of which waited for: 16 -> 50; matrix products, arithmetic and copies ran while one was open for 13% -> 26% of each run, Pallas kernels for 0% -> 0%
where the time goes in v1:
time: 1600 us; the launch traced here: 1590 us
  waiting for transfers between devices  841 us (53%)
  matrix products  277 us (17%)
  other arithmetic  207 us (13%)
  starting transfers between devices  131 us (8%)
  local copies, waits for them, and re-layouts  112 us (7%)
    ppermute x16, waiting for transfers between devices, sum_mp(): back = lax.ppermute(total, 'mp', [(1, 0), (2, 3)])  395 us
    ppermute x16, waiting for transfers between devices, sum_mp(): near = lax.ppermute(part, 'mp', [(0, 1), (3, 2)])  211 us
    dot_general x24, matrix products, dot_t(): lax.dot_general(a, b, (((1,), (1,)), ((), ())), preferred_element_type=F32)  108 us
    dot_general x22, matrix products, dot(): lax.dot_general(a, b, (((1,), (0,)), ((), ())), preferred_element_type=F32)  96.9 us
    ppermute x5, waiting for transfers between devices, gather_rows(): far_top = lax.ppermute(from_y[:half], **flip('dp', dp, 1))  80.4 us
    ppermute x5, waiting for transfers between devices, scatter_rows(): far_low = lax.ppermute(part(3, half, rows).astype(BF), **flip('dp', dp, 2))  78.3 us
    dot_general x9, matrix products, t_dot(): lax.dot_general(a, b, (((0,), (0,)), ((), ())), preferred_element_type=F32)  72.2 us
    ppermute x5, waiting for transfers between devices, scatter_rows(): far_top = lax.ppermute(part(3, 0, half).astype(BF), **flip('dp', dp, 1))  53.7 us
  transfers between devices with their start and end apart: 110, of which 50 were waited for; matrix products, arithmetic and copies ran while one was open for 26% of the time, Pallas kernels for 0%

profile of v1, /device:TPU:0, one launch (start us, length us, event | category | flops | bytes accessed | tf_op | source)
XLA Modules:
  0.0 1590.4 jit_solution(6366225284274965080)
XLA Ops:
  69.4 24.7 %collective-permute-done.8 = bf16[144,512]{1,0:T(8,128)(2,1)S(1)} collective-permute-done((bf16[144,512]{1,0:T(8,128)(2,1)S(1)}, bf16[144,512]{1,0:T(8,128)(2,1)S(1)}, u32[]{:S(2)}, u32[]{:S(2)}) %collective-permute-start.8) | collective-permute-done | bytes 147488 | tf_op jit(solution)/shard_map/ppermute | solution.py:38
  106.0 36.0 %collective-permute-done.16 = bf16[144,2304]{1,0:T(8,128)(2,1)S(1)} collective-permute-done((bf16[144,2304]{1,0:T(8,128)(2,1)S(1)}, bf16[144,2304]{1,0:T(8,128)(2,1)S(1)}, u32[]{:S(2)}, u32[]{:S(2)}) %collective-permute-start.16) | collective-permute-done | bytes 663584 | tf_op jit(solution)/shard_map/ppermute | solution.py:38
  192.6 17.6 %collective-permute-done.21 = bf16[144,2304]{1,0:T(8,128)(2,1)S(1)} collective-permute-done((bf16[144,2304]{1,0:T(8,128)(2,1)S(1)}, bf16[144,2304]{1,0:T(8,128)(2,1)S(1)}, u32[]{:S(2)}, u32[]{:S(2)}) %collective-permute-start.21) | collective-permute-done | bytes 663584 | tf_op jit(solution)/shard_map/ppermute | solution.py:38
  243.4 22.4 %collective-permute-done.32 = bf16[256,2304]{1,0:T(8,128)(2,1)} collective-permute-done((bf16[256,2304]{1,0:T(8,128)(2,1)}, bf16[256,2304]{1,0:T(8,128)(2,1)}, u32[]{:S(2)}, u32[]{:S(2)}) %collective-permute-start.32) | collective-permute-done | bytes 1179680 | tf_op jit(solution)/shard_map/ppermute | solution.py:101
  269.2 21.8 %collective-permute-done.45 = bf16[256,2304]{1,0:T(8,128)(2,1)S(1)} collective-permute-done((bf16[256,2304]{1,0:T(8,128)(2,1)S(1)}, bf16[256,2304]{1,0:T(8,128)(2,1)S(1)}, u32[]{:S(2)}, u32[]{:S(2)}) %collective-permute-start.45) | collective-permute-done | bytes 1179680 | tf_op jit(solution)/shard_map/ppermute | solution.py:101
  293.8 21.1 %collective-permute-done.39 = bf16[256,2304]{1,0:T(8,128)(2,1)S(1)} collective-permute-done((bf16[256,2304]{1,0:T(8,128)(2,1)S(1)}, bf16[256,2304]{1,0:T(8,128)(2,1)S(1)}, u32[]{:S(2)}, u32[]{:S(2)}) %collective-permute-start.39) | collective-permute-done | bytes 1179680 | tf_op jit(solution)/shard_map/ppermute | solution.py:101
  338.7 57.8 %collective-permute-done.13 = bf16[256,2304]{1,0:T(8,128)(2,1)S(1)} collective-permute-done((bf16[256,2304]{1,0:T(8,128)(2,1)S(1)}, bf16[256,2304]{1,0:T(8,128)(2,1)S(1)}, u32[]{:S(2)}, u32[]{:S(2)}) %collective-permute-start.13) | collective-permute-done | bytes 1179680 | tf_op jit(solution)/shard_map/ppermute | solution.py:105
  398.9 22.9 %collective-permute-done.34 = bf16[256,2304]{1,0:T(8,128)(2,1)S(1)} collective-permute-done((bf16[256,2304]{1,0:T(8,128)(2,1)S(1)}, bf16[256,2304]{1,0:T(8,128)(2,1)S(1)}, u32[]{:S(2)}, u32[]{:S(2)}) %collective-permute-start.34) | collective-permute-done | bytes 1179680 | tf_op jit(solution)/shard_map/ppermute | solution.py:105
  423.9 26.0 %collective-permute-done.47 = bf16[256,2304]{1,0:T(8,128)(2,1)S(1)} collective-permute-done((bf16[256,2304]{1,0:T(8,128)(2,1)S(1)}, bf16[256,2304]{1,0:T(8,128)(2,1)S(1)}, u32[]{:S(2)}, u32[]{:S(2)}) %collective-permute-start.47) | collective-permute-done | bytes 1179680 | tf_op jit(solution)/shard_map/ppermute | solution.py:105
  451.9 20.4 %collective-permute-done.41 = bf16[256,2304]{1,0:T(8,128)(2,1)S(1)} collective-permute-done((bf16[256,2304]{1,0:T(8,128)(2,1)S(1)}, bf16[256,2304]{1,0:T(8,128)(2,1)S(1)}, u32[]{:S(2)}, u32[]{:S(2)}) %collective-permute-start.41) | collective-permute-done | bytes 1179680 | tf_op jit(solution)/shard_map/ppermute | solution.py:105
  490.5 8.5 fusion.482
  512.0 8.7 bitcast_dynamic-update-slice_fusion
  520.7 9.2 multiply_convert_fusion.8
  535.3 8.8 multiply_convert_fusion.12
  550.2 8.8 multiply_convert_fusion.14
  564.7 9.3 multiply_convert_fusion.10
  587.0 24.3 %collective-permute-done.29 = bf16[256,2304]{1,0:T(8,128)(2,1)S(1)} collective-permute-done((bf16[256,2304]{1,0:T(8,128)(2,1)S(1)}, bf16[256,2304]{1,0:T(8,128)(2,1)S(1)}, u32[]{:S(2)}, u32[]{:S(2)}) %collective-permute-start.29) | collective-permute-done | bytes 1179680 | tf_op jit(solution)/shard_map/ppermute | solution.py:101
  612.3 20.7 %collective-permute-done.42 = bf16[256,2304]{1,0:T(8,128)(2,1)S(1)} collective-permute-done((bf16[256,2304]{1,0:T(8,128)(2,1)S(1)}, bf16[256,2304]{1,0:T(8,128)(2,1)S(1)}, u32[]{:S(2)}, u32[]{:S(2)}) %collective-permute-start.42) | collective-permute-done | bytes 1179680 | tf_op jit(solution)/shard_map/ppermute | solution.py:101
  641.2 26.5 %collective-permute-done.50 = bf16[256,2304]{1,0:T(8,128)(2,1)S(1)} collective-permute-done((bf16[256,2304]{1,0:T(8,128)(2,1)S(1)}, bf16[256,2304]{1,0:T(8,128)(2,1)S(1)}, u32[]{:S(2)}, u32[]{:S(2)}) %collective-permute-start.50) | collective-permute-done | bytes 1179680 | tf_op jit(solution)/shard_map/ppermute | solution.py:105
  668.2 24.7 %collective-permute-done.37 = bf16[256,2304]{1,0:T(8,128)(2,1)S(1)} collective-permute-done((bf16[256,2304]{1,0:T(8,128)(2,1)S(1)}, bf16[256,2304]{1,0:T(8,128)(2,1)S(1)}, u32[]{:S(2)}, u32[]{:S(2)}) %collective-permute-start.37) | collective-permute-done | bytes 1179680 | tf_op jit(solution)/shard_map/ppermute | solution.py:105
  693.5 24.7 %collective-permute-done.31 = bf16[256,2304]{1,0:T(8,128)(2,1)S(1)} collective-permute-done((bf16[256,2304]{1,0:T(8,128)(2,1)S(1)}, bf16[256,2304]{1,0:T(8,128)(2,1)S(1)}, u32[]{:S(2)}, u32[]{:S(2)}) %collective-permute-start.31) | collective-permute-done | bytes 1179680 | tf_op jit(solution)/shard_map/ppermute | solution.py:105
  718.8 20.2 %collective-permute-done.44 = bf16[256,2304]{1,0:T(8,128)(2,1)S(1)} collective-permute-done((bf16[256,2304]{1,0:T(8,128)(2,1)S(1)}, bf16[256,2304]{1,0:T(8,128)(2,1)S(1)}, u32[]{:S(2)}, u32[]{:S(2)}) %collective-permute-start.44) | collective-permute-done | bytes 1179680 | tf_op jit(solution)/shard_map/ppermute | solution.py:105
  750.1 8.8 fusion.486
  767.7 8.9 fusion.483
  783.2 8.8 fusion.485
  808.1 18.4 %convolution_convert_fusion.2 = bf16[2304,2304]{1,0:T(8,128)(2,1)} fusion(bf16[256,2304]{1,0:T(8,128)(2,1)} %copy-done.220, bf16[256,2304]{1,0:T(8,128)(2,1)} %copy-done.221, bf16[256,2304]{1,0:T(8,128)(2,1)} %copy-done.222, bf16[256,2304]{1,0:T(8,128)(2,1)} %get-tuple-element.307, bf16[256,2304]{1,0:T(8,128)(2,1)} %get-tuple-element.366, ...), kind=kOutput, calls=%fused_computation.2 | convolution fusion | flops 10914693120 | bytes 20054016 | tf_op jit(solution)/shard_map/dot_general | solution.py:146
  826.5 18.6 %convolution_convert_fusion = bf16[2304,2304]{1,0:T(8,128)(2,1)} fusion(bf16[256,2304]{1,0:T(8,128)(2,1)} %copy-done.101, bf16[256,2304]{1,0:T(8,128)(2,1)} %get-tuple-element.299, bf16[256,2304]{1,0:T(8,128)(2,1)} %get-tuple-element.298, bf16[256,2304]{1,0:T(8,128)(2,1)} %copy-done.84, bf16[256,2304]{1,0:T(8,128)(2,1)} %copy-done.218, ...), kind=kOutput, calls=%fused_computation | convolution fusion | flops 10914693120 | bytes 20054016 | tf_op jit(solution)/shard_map/dot_general | solution.py:146
  845.2 9.1 fusion.51
  856.7 12.4 fusion.48
  880.1 18.2 %convolution_convert_fusion.1 = bf16[2304,2304]{1,0:T(8,128)(2,1)} fusion(bf16[256,2304]{1,0:T(8,128)(2,1)} %get-tuple-element.312, bf16[256,2304]{1,0:T(8,128)(2,1)} %get-tuple-element.310, bf16[256,2304]{1,0:T(8,128)(2,1)} %get-tuple-element.308, bf16[256,2304]{1,0:T(8,128)(2,1)} %get-tuple-element.306, bf16[256,2304]{1,0:T(8,128)(2,1)} %get-tuple-element.366, ...), kind=kOutput, calls=%fused_computation.1 | convolution fusion | flops 10914693120 | bytes 20054016 | tf_op jit(solution)/shard_map/dot_general | solution.py:146
  916.4 16.7 %collective-permute-done.64 = bf16[256,2304]{1,0:T(8,128)(2,1)} collective-permute-done((bf16[256,2304]{1,0:T(8,128)(2,1)}, bf16[256,2304]{1,0:T(8,128)(2,1)}, u32[]{:S(2)}, u32[]{:S(2)}) %collective-permute-start.64) | collective-permute-done | bytes 1179680 | tf_op jit(solution)/shard_map/ppermute | solution.py:101
  935.6 17.2 %collective-permute-done.54 = bf16[256,2304]{1,0:T(8,128)(2,1)S(1)} collective-permute-done((bf16[256,2304]{1,0:T(8,128)(2,1)S(1)}, bf16[256,2304]{1,0:T(8,128)(2,1)S(1)}, u32[]{:S(2)}, u32[]{:S(2)}) %collective-permute-start.54) | collective-permute-done | bytes 1179680 | tf_op jit(solution)/shard_map/ppermute | solution.py:101
  963.6 30.5 %collective-permute-done.66 = bf16[256,2304]{1,0:T(8,128)(2,1)S(1)} collective-permute-done((bf16[256,2304]{1,0:T(8,128)(2,1)S(1)}, bf16[256,2304]{1,0:T(8,128)(2,1)S(1)}, u32[]{:S(2)}, u32[]{:S(2)}) %collective-permute-start.66) | collective-permute-done | bytes 1179680 | tf_op jit(solution)/shard_map/ppermute | solution.py:105
  994.1 27.8 %collective-permute-done.56 = bf16[256,2304]{1,0:T(8,128)(2,1)S(1)} collective-permute-done((bf16[256,2304]{1,0:T(8,128)(2,1)S(1)}, bf16[256,2304]{1,0:T(8,128)(2,1)S(1)}, u32[]{:S(2)}, u32[]{:S(2)}) %collective-permute-start.56) | collective-permute-done | bytes 1179680 | tf_op jit(solution)/shard_map/ppermute | solution.py:105
  1025.7 21.5 %collective-permute-done.69 = bf16[256,2304]{1,0:T(8,128)(2,1)S(1)} collective-permute-done((bf16[256,2304]{1,0:T(8,128)(2,1)S(1)}, bf16[256,2304]{1,0:T(8,128)(2,1)S(1)}, u32[]{:S(2)}, u32[]{:S(2)}) %collective-permute-start.69) | collective-permute-done | bytes 1179680 | tf_op jit(solution)/shard_map/ppermute | solution.py:105
  1047.2 22.7 %collective-permute-done.53 = bf16[256,2304]{1,0:T(8,128)(2,1)S(1)} collective-permute-done((bf16[256,2304]{1,0:T(8,128)(2,1)S(1)}, bf16[256,2304]{1,0:T(8,128)(2,1)S(1)}, u32[]{:S(2)}, u32[]{:S(2)}) %collective-permute-start.53) | collective-permute-done | bytes 1179680 | tf_op jit(solution)/shard_map/ppermute | solution.py:105
  1164.7 20.0 %collective-permute-done.61 = bf16[256,2304]{1,0:T(8,128)(2,1)S(1)} collective-permute-done((bf16[256,2304]{1,0:T(8,128)(2,1)S(1)}, bf16[256,2304]{1,0:T(8,128)(2,1)S(1)}, u32[]{:S(2)}, u32[]{:S(2)}) %collective-permute-start.61) | collective-permute-done | bytes 1179680 | tf_op jit(solution)/shard_map/ppermute | solution.py:101
  1192.3 17.8 %collective-permute-done.71 = bf16[256,2304]{1,0:T(8,128)(2,1)} collective-permute-done((bf16[256,2304]{1,0:T(8,128)(2,1)}, bf16[256,2304]{1,0:T(8,128)(2,1)}, u32[]{:S(2)}, u32[]{:S(2)}) %collective-permute-start.71) | collective-permute-done | bytes 1179680 | tf_op jit(solution)/shard_map/ppermute | solution.py:101
  1212.7 21.8 %collective-permute-done.74 = bf16[256,2304]{1,0:T(8,128)(2,1)} collective-permute-done((bf16[256,2304]{1,0:T(8,128)(2,1)}, bf16[256,2304]{1,0:T(8,128)(2,1)}, u32[]{:S(2)}, u32[]{:S(2)}) %collective-permute-start.74) | collective-permute-done | bytes 1179680 | tf_op jit(solution)/shard_map/ppermute | solution.py:101
  1261.5 11.7 collective-permute-done.80
  1281.7 21.1 %collective-permute-done.63 = bf16[256,2304]{1,0:T(8,128)(2,1)} collective-permute-done((bf16[256,2304]{1,0:T(8,128)(2,1)}, bf16[256,2304]{1,0:T(8,128)(2,1)}, u32[]{:S(2)}, u32[]{:S(2)}) %collective-permute-start.63) | collective-permute-done | bytes 1179680 | tf_op jit(solution)/shard_map/ppermute | solution.py:105
  1302.8 25.3 %collective-permute-done.73 = bf16[256,2304]{1,0:T(8,128)(2,1)} collective-permute-done((bf16[256,2304]{1,0:T(8,128)(2,1)}, bf16[256,2304]{1,0:T(8,128)(2,1)}, u32[]{:S(2)}, u32[]{:S(2)}) %collective-permute-start.73) | collective-permute-done | bytes 1179680 | tf_op jit(solution)/shard_map/ppermute | solution.py:105
  1328.1 23.3 %collective-permute-done.76 = bf16[256,2304]{1,0:T(8,128)(2,1)} collective-permute-done((bf16[256,2304]{1,0:T(8,128)(2,1)}, bf16[256,2304]{1,0:T(8,128)(2,1)}, u32[]{:S(2)}, u32[]{:S(2)}) %collective-permute-start.76) | collective-permute-done | bytes 1179680 | tf_op jit(solution)/shard_map/ppermute | solution.py:105
  1372.7 11.9 collective-permute-done.82
  1395.0 10.8 collective-permute-done.93
  1413.8 34.8 %collective-permute-done.96 = bf16[144,2304]{1,0:T(8,128)(2,1)S(1)} collective-permute-done((bf16[144,2304]{1,0:T(8,128)(2,1)S(1)}, bf16[144,2304]{1,0:T(8,128)(2,1)S(1)}, u32[]{:S(2)}, u32[]{:S(2)}) %collective-permute-start.96) | collective-permute-done | bytes 663584 | tf_op jit(solution)/shard_map/ppermute | solution.py:87
  1452.8 27.3 %collective-permute-done.90 = bf16[144,512]{1,0:T(8,128)(2,1)S(1)} collective-permute-done((bf16[144,512]{1,0:T(8,128)(2,1)S(1)}, bf16[144,512]{1,0:T(8,128)(2,1)S(1)}, u32[]{:S(2)}, u32[]{:S(2)}) %collective-permute-start.90) | collective-permute-done | bytes 147488 | tf_op jit(solution)/shard_map/ppermute | solution.py:87
  1486.7 30.1 %collective-permute-done.88 = bf16[144,1024]{1,0:T(8,128)(2,1)S(1)} collective-permute-done((bf16[144,1024]{1,0:T(8,128)(2,1)S(1)}, bf16[144,1024]{1,0:T(8,128)(2,1)S(1)}, u32[]{:S(2)}, u32[]{:S(2)}) %collective-permute-start.88) | collective-permute-done | bytes 294944 | tf_op jit(solution)/shard_map/ppermute | solution.py:86
  (999 shorter events, 616.5 us)
Async XLA Ops:
  66.3 83.5 %collective-permute-start.4 = (bf16[4,288,1024]{2,1,0:T(8,128)(2,1)}, bf16[4,288,1024]{2,1,0:T(8,128)(2,1)}, u32[]{:S(2)}, u32[]{:S(2)}) collective-permute-start(bf16[4,288,1024]{2,1,0:T(8,128)(2,1)} %bitcast_dynamic-update-slice_fusion.31), channel_id=1, source_target_pairs={{0,4},{4,0},{1,5},{5,1},{2,6},{6,2},{3,7},{7,3},{8,12},{12,8},{9,1... | collective-permute-start | bytes 7077896 | tf_op jit(solution)/shard_map/ppermute | solution.py:47
  96.0 68.5 %collective-permute-start.19 = (bf16[288,2304]{1,0:T(8,128)(2,1)}, bf16[288,2304]{1,0:T(8,128)(2,1)}, u32[]{:S(2)}, u32[]{:S(2)}) collective-permute-start(bf16[288,2304]{1,0:T(8,128)(2,1)} %convert_element_type.1220), channel_id=1, source_target_pairs={{0,8},{8,0},{16,24},{24,16},{1,9},{9,1},{17,25},{25,17},{2,10},{10... | collective-permute-start | bytes 3981320 | tf_op jit(solution)/shard_map/ppermute | solution.py:36
  96.4 74.9 %collective-permute-start.20 = (bf16[288,2304]{1,0:T(8,128)(2,1)}, bf16[288,2304]{1,0:T(8,128)(2,1)}, u32[]{:S(2)}, u32[]{:S(2)}) collective-permute-start(bf16[288,2304]{1,0:T(8,128)(2,1)} %convert_element_type.1220), channel_id=1, source_target_pairs={{0,16},{8,24},{16,0},{24,8},{1,17},{9,25},{17,1},{25,9},{2,18},{10... | collective-permute-start | bytes 3981320 | tf_op jit(solution)/shard_map/ppermute | solution.py:37
  142.1 342.3 %collective-permute-start.18 = (bf16[4,288,2304]{2,1,0:T(8,128)(2,1)S(1)}, bf16[4,288,2304]{2,1,0:T(8,128)(2,1)}, u32[]{:S(2)}, u32[]{:S(2)}) collective-permute-start(bf16[4,288,2304]{2,1,0:T(8,128)(2,1)S(1)} %bitcast_dynamic-update-slice_fusion.23), channel_id=1, source_target_pairs={{0,4},{4,0},{1,5},{5,1},{2,6},{6,2},{3,7},{7,3},{8,12},{12,8},{9,1... | collective-permute-start | bytes 15925256 | tf_op jit(solution)/shard_map/ppermute | solution.py:47
  164.4 70.4 %collective-permute-start.24 = (bf16[288,2304]{1,0:T(8,128)(2,1)S(1)}, bf16[288,2304]{1,0:T(8,128)(2,1)}, u32[]{:S(2)}, u32[]{:S(2)}) collective-permute-start(bf16[288,2304]{1,0:T(8,128)(2,1)S(1)} %convert_element_type.1222), channel_id=1, source_target_pairs={{0,8},{8,0},{16,24},{24,16},{1,9},{9,1},{17,25},{25,17},{2,10},{10... | collective-permute-start | bytes 3981320 | tf_op jit(solution)/shard_map/ppermute | solution.py:36
  171.2 61.1 %collective-permute-start.25 = (bf16[288,2304]{1,0:T(8,128)(2,1)S(1)}, bf16[288,2304]{1,0:T(8,128)(2,1)}, u32[]{:S(2)}, u32[]{:S(2)}) collective-permute-start(bf16[288,2304]{1,0:T(8,128)(2,1)S(1)} %convert_element_type.1222), channel_id=1, source_target_pairs={{0,16},{8,24},{16,0},{24,8},{1,17},{9,25},{17,1},{25,9},{2,18},{10... | collective-permute-start | bytes 3981320 | tf_op jit(solution)/shard_map/ppermute | solution.py:37
  216.7 49.1 %collective-permute-start.32 = (bf16[256,2304]{1,0:T(8,128)(2,1)}, bf16[256,2304]{1,0:T(8,128)(2,1)}, u32[]{:S(2)}, u32[]{:S(2)}) collective-permute-start(bf16[256,2304]{1,0:T(8,128)(2,1)} %convolution_convert_fusion.14), channel_id=1, source_target_pairs={{0,1},{3,2},{4,5},{7,6},{8,9},{11,10},{12,13},{15,14},{16,17},{19,... | collective-permute-start | bytes 3538952 | tf_op jit(solution)/shard_map/ppermute | solution.py:101
  232.3 58.6 %collective-permute-start.45 = (bf16[256,2304]{1,0:T(8,128)(2,1)S(1)}, bf16[256,2304]{1,0:T(8,128)(2,1)S(1)}, u32[]{:S(2)}, u32[]{:S(2)}) collective-permute-start(bf16[256,2304]{1,0:T(8,128)(2,1)S(1)} %copy-done.53), channel_id=1, source_target_pairs={{0,1},{3,2},{4,5},{7,6},{8,9},{11,10},{12,13},{15,14},{16,17},{19,... | collective-permute-start | bytes 3538952 | tf_op jit(solution)/shard_map/ppermute | solution.py:101
  234.8 80.0 %collective-permute-start.39 = (bf16[256,2304]{1,0:T(8,128)(2,1)S(1)}, bf16[256,2304]{1,0:T(8,128)(2,1)S(1)}, u32[]{:S(2)}, u32[]{:S(2)}) collective-permute-start(bf16[256,2304]{1,0:T(8,128)(2,1)S(1)} %copy-done.52), channel_id=1, source_target_pairs={{0,1},{3,2},{4,5},{7,6},{8,9},{11,10},{12,13},{15,14},{16,17},{19,... | collective-permute-start | bytes 3538952 | tf_op jit(solution)/shard_map/ppermute | solution.py:101
  241.5 270.4 %collective-permute-start.23 = (bf16[4,288,2304]{2,1,0:T(8,128)(2,1)}, bf16[4,288,2304]{2,1,0:T(8,128)(2,1)}, u32[]{:S(2)}, u32[]{:S(2)}) collective-permute-start(bf16[4,288,2304]{2,1,0:T(8,128)(2,1)} %bitcast_dynamic-update-slice_fusion.21), channel_id=1, source_target_pairs={{0,4},{4,0},{1,5},{5,1},{2,6},{6,2},{3,7},{7,3},{8,12},{12,8},{9,1... | collective-permute-start | bytes 15925256 | tf_op jit(solution)/shard_map/ppermute | solution.py:47
  265.8 52.1 %collective-permute-start.26 = (bf16[144,2304]{1,0:T(8,128)(2,1)S(1)}, bf16[144,2304]{1,0:T(8,128)(2,1)S(1)}, u32[]{:S(2)}, u32[]{:S(2)}) collective-permute-start(bf16[144,2304]{1,0:T(8,128)(2,1)S(1)} %slice.423), channel_id=1, source_target_pairs={{0,8},{8,0},{16,24},{24,16},{1,9},{9,1},{17,25},{25,17},{2,10},{10... | collective-permute-start | bytes 1990664 | tf_op jit(solution)/shard_map/ppermute | solution.py:38
  331.1 65.4 %collective-permute-start.13 = (bf16[256,2304]{1,0:T(8,128)(2,1)S(1)}, bf16[256,2304]{1,0:T(8,128)(2,1)S(1)}, u32[]{:S(2)}, u32[]{:S(2)}) collective-permute-start(bf16[256,2304]{1,0:T(8,128)(2,1)S(1)} %add_convert_fusion.30), channel_id=1, source_target_pairs={{1,0},{2,3},{5,4},{6,7},{9,8},{10,11},{13,12},{14,15},{17,16},{18,... | collective-permute-start | bytes 3538952 | tf_op jit(solution)/shard_map/ppermute | solution.py:105
  333.9 87.9 %collective-permute-start.34 = (bf16[256,2304]{1,0:T(8,128)(2,1)S(1)}, bf16[256,2304]{1,0:T(8,128)(2,1)S(1)}, u32[]{:S(2)}, u32[]{:S(2)}) collective-permute-start(bf16[256,2304]{1,0:T(8,128)(2,1)S(1)} %add_convert_fusion.26), channel_id=1, source_target_pairs={{1,0},{2,3},{5,4},{6,7},{9,8},{10,11},{13,12},{14,15},{17,16},{18,... | collective-permute-start | bytes 3538952 | tf_op jit(solution)/shard_map/ppermute | solution.py:105
  337.1 112.7 %collective-permute-start.47 = (bf16[256,2304]{1,0:T(8,128)(2,1)S(1)}, bf16[256,2304]{1,0:T(8,128)(2,1)S(1)}, u32[]{:S(2)}, u32[]{:S(2)}) collective-permute-start(bf16[256,2304]{1,0:T(8,128)(2,1)S(1)} %add_convert_fusion.18), channel_id=1, source_target_pairs={{1,0},{2,3},{5,4},{6,7},{9,8},{10,11},{13,12},{14,15},{17,16},{18,... | collective-permute-start | bytes 3538952 | tf_op jit(solution)/shard_map/ppermute | solution.py:105
  396.5 75.8 %collective-permute-start.41 = (bf16[256,2304]{1,0:T(8,128)(2,1)S(1)}, bf16[256,2304]{1,0:T(8,128)(2,1)S(1)}, u32[]{:S(2)}, u32[]{:S(2)}) collective-permute-start(bf16[256,2304]{1,0:T(8,128)(2,1)S(1)} %add_convert_fusion.22), channel_id=1, source_target_pairs={{1,0},{2,3},{5,4},{6,7},{9,8},{10,11},{13,12},{14,15},{17,16},{18,... | collective-permute-start | bytes 3538952 | tf_op jit(solution)/shard_map/ppermute | solution.py:105
  421.8 90.2 %collective-permute-start.28 = (bf16[4,288,2304]{2,1,0:T(8,128)(2,1)S(1)}, bf16[4,288,2304]{2,1,0:T(8,128)(2,1)}, u32[]{:S(2)}, u32[]{:S(2)}) collective-permute-start(bf16[4,288,2304]{2,1,0:T(8,128)(2,1)S(1)} %bitcast_dynamic-update-slice_fusion.19), channel_id=1, source_target_pairs={{0,4},{4,0},{1,5},{5,1},{2,6},{6,2},{3,7},{7,3},{8,12},{12,8},{9,1... | collective-permute-start | bytes 15925256 | tf_op jit(solution)/shard_map/ppermute | solution.py:47
  532.8 46.8 %collective-permute-start.48 = (bf16[256,2304]{1,0:T(8,128)(2,1)S(1)}, bf16[256,2304]{1,0:T(8,128)(2,1)}, u32[]{:S(2)}, u32[]{:S(2)}) collective-permute-start(bf16[256,2304]{1,0:T(8,128)(2,1)S(1)} %convolution_convert_fusion.4), channel_id=1, source_target_pairs={{0,1},{3,2},{4,5},{7,6},{8,9},{11,10},{12,13},{15,14},{16,17},{19,... | collective-permute-start | bytes 3538952 | tf_op jit(solution)/shard_map/ppermute | solution.py:101
  563.4 47.9 %collective-permute-start.29 = (bf16[256,2304]{1,0:T(8,128)(2,1)S(1)}, bf16[256,2304]{1,0:T(8,128)(2,1)S(1)}, u32[]{:S(2)}, u32[]{:S(2)}) collective-permute-start(bf16[256,2304]{1,0:T(8,128)(2,1)S(1)} %convolution_convert_fusion.7), channel_id=1, source_target_pairs={{0,1},{3,2},{4,5},{7,6},{8,9},{11,10},{12,13},{15,14},{16,17},{19,... | collective-permute-start | bytes 3538952 | tf_op jit(solution)/shard_map/ppermute | solution.py:101
  578.3 54.7 %collective-permute-start.42 = (bf16[256,2304]{1,0:T(8,128)(2,1)S(1)}, bf16[256,2304]{1,0:T(8,128)(2,1)S(1)}, u32[]{:S(2)}, u32[]{:S(2)}) collective-permute-start(bf16[256,2304]{1,0:T(8,128)(2,1)S(1)} %convolution_convert_fusion.5), channel_id=1, source_target_pairs={{0,1},{3,2},{4,5},{7,6},{8,9},{11,10},{12,13},{15,14},{16,17},{19,... | collective-permute-start | bytes 3538952 | tf_op jit(solution)/shard_map/ppermute | solution.py:101
  581.2 52.8 %collective-permute-start.49 = (bf16[256,2304]{1,0:T(8,128)(2,1)S(1)}, bf16[256,2304]{1,0:T(8,128)(2,1)S(1)}, u32[]{:S(2)}, u32[]{:S(2)}) collective-permute-start(bf16[256,2304]{1,0:T(8,128)(2,1)S(1)} %add_convert_fusion.17), channel_id=1, source_target_pairs={{1,2},{2,1},{5,6},{6,5},{9,10},{10,9},{13,14},{14,13},{17,18},{18,... | collective-permute-start | bytes 3538952 | tf_op jit(solution)/shard_map/ppermute | solution.py:103
  586.3 49.4 %collective-permute-start.36 = (bf16[256,2304]{1,0:T(8,128)(2,1)S(1)}, bf16[256,2304]{1,0:T(8,128)(2,1)S(1)}, u32[]{:S(2)}, u32[]{:S(2)}) collective-permute-start(bf16[256,2304]{1,0:T(8,128)(2,1)S(1)} %add_convert_fusion.25), channel_id=1, source_target_pairs={{1,2},{2,1},{5,6},{6,5},{9,10},{10,9},{13,14},{14,13},{17,18},{18,... | collective-permute-start | bytes 3538952 | tf_op jit(solution)/shard_map/ppermute | solution.py:103
  635.9 57.0 %collective-permute-start.37 = (bf16[256,2304]{1,0:T(8,128)(2,1)S(1)}, bf16[256,2304]{1,0:T(8,128)(2,1)S(1)}, u32[]{:S(2)}, u32[]{:S(2)}) collective-permute-start(bf16[256,2304]{1,0:T(8,128)(2,1)S(1)} %add_convert_fusion.24), channel_id=1, source_target_pairs={{1,0},{2,3},{5,4},{6,7},{9,8},{10,11},{13,12},{14,15},{17,16},{18,... | collective-permute-start | bytes 3538952 | tf_op jit(solution)/shard_map/ppermute | solution.py:105
  638.0 80.3 %collective-permute-start.31 = (bf16[256,2304]{1,0:T(8,128)(2,1)S(1)}, bf16[256,2304]{1,0:T(8,128)(2,1)S(1)}, u32[]{:S(2)}, u32[]{:S(2)}) collective-permute-start(bf16[256,2304]{1,0:T(8,128)(2,1)S(1)} %add_convert_fusion.28), channel_id=1, source_target_pairs={{1,0},{2,3},{5,4},{6,7},{9,8},{10,11},{13,12},{14,15},{17,16},{18,... | collective-permute-start | bytes 3538952 | tf_op jit(solution)/shard_map/ppermute | solution.py:105
  639.6 99.4 %collective-permute-start.44 = (bf16[256,2304]{1,0:T(8,128)(2,1)S(1)}, bf16[256,2304]{1,0:T(8,128)(2,1)S(1)}, u32[]{:S(2)}, u32[]{:S(2)}) collective-permute-start(bf16[256,2304]{1,0:T(8,128)(2,1)S(1)} %add_convert_fusion.20), channel_id=1, source_target_pairs={{1,0},{2,3},{5,4},{6,7},{9,8},{10,11},{13,12},{14,15},{17,16},{18,... | collective-permute-start | bytes 3538952 | tf_op jit(solution)/shard_map/ppermute | solution.py:105
  854.3 59.2 %collective-permute-start.67 = (bf16[256,2304]{1,0:T(8,128)(2,1)}, bf16[256,2304]{1,0:T(8,128)(2,1)}, u32[]{:S(2)}, u32[]{:S(2)}) collective-permute-start(bf16[256,2304]{1,0:T(8,128)(2,1)} %fusion.51), channel_id=1, source_target_pairs={{0,1},{3,2},{4,5},{7,6},{8,9},{11,10},{12,13},{15,14},{16,17},{19,... | collective-permute-start | bytes 3538952 | tf_op jit(solution)/shard_map/ppermute | solution.py:101
  869.2 84.7 %collective-permute-start.51 = (bf16[256,2304]{1,0:T(8,128)(2,1)}, bf16[256,2304]{1,0:T(8,128)(2,1)}, u32[]{:S(2)}, u32[]{:S(2)}) collective-permute-start(bf16[256,2304]{1,0:T(8,128)(2,1)} %fusion.48), channel_id=1, source_target_pairs={{0,1},{3,2},{4,5},{7,6},{8,9},{11,10},{12,13},{15,14},{16,17},{19,... | collective-permute-start | bytes 3538952 | tf_op jit(solution)/shard_map/ppermute | solution.py:101
  877.8 55.2 %collective-permute-start.64 = (bf16[256,2304]{1,0:T(8,128)(2,1)}, bf16[256,2304]{1,0:T(8,128)(2,1)}, u32[]{:S(2)}, u32[]{:S(2)}) collective-permute-start(bf16[256,2304]{1,0:T(8,128)(2,1)} %fusion.50), channel_id=1, source_target_pairs={{0,1},{3,2},{4,5},{7,6},{8,9},{11,10},{12,13},{15,14},{16,17},{19,... | collective-permute-start | bytes 3538952 | tf_op jit(solution)/shard_map/ppermute | solution.py:101
  906.3 46.6 %collective-permute-start.54 = (bf16[256,2304]{1,0:T(8,128)(2,1)S(1)}, bf16[256,2304]{1,0:T(8,128)(2,1)S(1)}, u32[]{:S(2)}, u32[]{:S(2)}) collective-permute-start(bf16[256,2304]{1,0:T(8,128)(2,1)S(1)} %fusion.49), channel_id=1, source_target_pairs={{0,1},{3,2},{4,5},{7,6},{8,9},{11,10},{12,13},{15,14},{16,17},{19,... | collective-permute-start | bytes 3538952 | tf_op jit(solution)/shard_map/ppermute | solution.py:101
  912.9 248.5 %collective-permute-start.77 = (bf16[4,288,2304]{2,1,0:T(8,128)(2,1)}, bf16[4,288,2304]{2,1,0:T(8,128)(2,1)S(1)}, u32[]{:S(2)}, u32[]{:S(2)}) collective-permute-start(bf16[4,288,2304]{2,1,0:T(8,128)(2,1)} %dynamic-slice_bitcast_fusion.2), channel_id=1, source_target_pairs={{0,4},{4,0},{1,5},{5,1},{2,6},{6,2},{3,7},{7,3},{8,12},{12,8},{9,1... | collective-permute-start | bytes 15925256 | tf_op jit(solution)/shard_map/ppermute | solution.py:72
  958.4 63.5 %collective-permute-start.56 = (bf16[256,2304]{1,0:T(8,128)(2,1)S(1)}, bf16[256,2304]{1,0:T(8,128)(2,1)S(1)}, u32[]{:S(2)}, u32[]{:S(2)}) collective-permute-start(bf16[256,2304]{1,0:T(8,128)(2,1)S(1)} %add_convert_fusion.12), channel_id=1, source_target_pairs={{1,0},{2,3},{5,4},{6,7},{9,8},{10,11},{13,12},{14,15},{17,16},{18,... | collective-permute-start | bytes 3538952 | tf_op jit(solution)/shard_map/ppermute | solution.py:105
  960.1 87.1 %collective-permute-start.69 = (bf16[256,2304]{1,0:T(8,128)(2,1)S(1)}, bf16[256,2304]{1,0:T(8,128)(2,1)S(1)}, u32[]{:S(2)}, u32[]{:S(2)}) collective-permute-start(bf16[256,2304]{1,0:T(8,128)(2,1)S(1)} %add_convert_fusion.4), channel_id=1, source_target_pairs={{1,0},{2,3},{5,4},{6,7},{9,8},{10,11},{13,12},{14,15},{17,16},{18,... | collective-permute-start | bytes 3538952 | tf_op jit(solution)/shard_map/ppermute | solution.py:105
  962.0 107.9 %collective-permute-start.53 = (bf16[256,2304]{1,0:T(8,128)(2,1)S(1)}, bf16[256,2304]{1,0:T(8,128)(2,1)S(1)}, u32[]{:S(2)}, u32[]{:S(2)}) collective-permute-start(bf16[256,2304]{1,0:T(8,128)(2,1)S(1)} %add_convert_fusion.14), channel_id=1, source_target_pairs={{1,0},{2,3},{5,4},{6,7},{9,8},{10,11},{13,12},{14,15},{17,16},{18,... | collective-permute-start | bytes 3538952 | tf_op jit(solution)/shard_map/ppermute | solution.py:105
  1133.2 51.5 %collective-permute-start.61 = (bf16[256,2304]{1,0:T(8,128)(2,1)S(1)}, bf16[256,2304]{1,0:T(8,128)(2,1)S(1)}, u32[]{:S(2)}, u32[]{:S(2)}) collective-permute-start(bf16[256,2304]{1,0:T(8,128)(2,1)S(1)} %convolution_convert_fusion.10), channel_id=1, source_target_pairs={{0,1},{3,2},{4,5},{7,6},{8,9},{11,10},{12,13},{15,14},{16,17},{19,... | collective-permute-start | bytes 3538952 | tf_op jit(solution)/shard_map/ppermute | solution.py:101
  1142.0 68.1 %collective-permute-start.71 = (bf16[256,2304]{1,0:T(8,128)(2,1)}, bf16[256,2304]{1,0:T(8,128)(2,1)}, u32[]{:S(2)}, u32[]{:S(2)}) collective-permute-start(bf16[256,2304]{1,0:T(8,128)(2,1)} %convolution_convert_fusion.9), channel_id=1, source_target_pairs={{0,1},{3,2},{4,5},{7,6},{8,9},{11,10},{12,13},{15,14},{16,17},{19,... | collective-permute-start | bytes 3538952 | tf_op jit(solution)/shard_map/ppermute | solution.py:101
  1147.1 87.5 %collective-permute-start.74 = (bf16[256,2304]{1,0:T(8,128)(2,1)}, bf16[256,2304]{1,0:T(8,128)(2,1)}, u32[]{:S(2)}, u32[]{:S(2)}) collective-permute-start(bf16[256,2304]{1,0:T(8,128)(2,1)} %convolution_convert_fusion.8), channel_id=1, source_target_pairs={{0,1},{3,2},{4,5},{7,6},{8,9},{11,10},{12,13},{15,14},{16,17},{19,... | collective-permute-start | bytes 3538952 | tf_op jit(solution)/shard_map/ppermute | solution.py:101
  1159.7 81.1 %collective-permute-start.59 = (bf16[256,2304]{1,0:T(8,128)(2,1)S(1)}, bf16[256,2304]{1,0:T(8,128)(2,1)}, u32[]{:S(2)}, u32[]{:S(2)}) collective-permute-start(bf16[256,2304]{1,0:T(8,128)(2,1)S(1)} %add_convert_fusion.11), channel_id=1, source_target_pairs={{1,2},{2,1},{5,6},{6,5},{9,10},{10,9},{13,14},{14,13},{17,18},{18,... | collective-permute-start | bytes 3538952 | tf_op jit(solution)/shard_map/ppermute | solution.py:103
  1185.0 60.0 %collective-permute-start.62 = (bf16[256,2304]{1,0:T(8,128)(2,1)S(1)}, bf16[256,2304]{1,0:T(8,128)(2,1)}, u32[]{:S(2)}, u32[]{:S(2)}) collective-permute-start(bf16[256,2304]{1,0:T(8,128)(2,1)S(1)} %add_convert_fusion.9), channel_id=1, source_target_pairs={{1,2},{2,1},{5,6},{6,5},{9,10},{10,9},{13,14},{14,13},{17,18},{18,... | collective-permute-start | bytes 3538952 | tf_op jit(solution)/shard_map/ppermute | solution.py:103
  1192.3 61.7 %collective-permute-start.79 = (bf16[4,288,2304]{2,1,0:T(8,128)(2,1)}, bf16[4,288,2304]{2,1,0:T(8,128)(2,1)S(1)}, u32[]{:S(2)}, u32[]{:S(2)}) collective-permute-start(bf16[4,288,2304]{2,1,0:T(8,128)(2,1)} %dynamic-slice_bitcast_fusion.1), channel_id=1, source_target_pairs={{0,4},{4,0},{1,5},{5,1},{2,6},{6,2},{3,7},{7,3},{8,12},{12,8},{9,1... | collective-permute-start | bytes 15925256 | tf_op jit(solution)/shard_map/ppermute | solution.py:72
  1248.8 54.0 %collective-permute-start.63 = (bf16[256,2304]{1,0:T(8,128)(2,1)}, bf16[256,2304]{1,0:T(8,128)(2,1)}, u32[]{:S(2)}, u32[]{:S(2)}) collective-permute-start(bf16[256,2304]{1,0:T(8,128)(2,1)} %add_convert_fusion.8), channel_id=1, source_target_pairs={{1,0},{2,3},{5,4},{6,7},{9,8},{10,11},{13,12},{14,15},{17,16},{18,... | collective-permute-start | bytes 3538952 | tf_op jit(solution)/shard_map/ppermute | solution.py:105
  1251.4 76.7 %collective-permute-start.73 = (bf16[256,2304]{1,0:T(8,128)(2,1)}, bf16[256,2304]{1,0:T(8,128)(2,1)}, u32[]{:S(2)}, u32[]{:S(2)}) collective-permute-start(bf16[256,2304]{1,0:T(8,128)(2,1)} %add_convert_fusion.2), channel_id=1, source_target_pairs={{1,0},{2,3},{5,4},{6,7},{9,8},{10,11},{13,12},{14,15},{17,16},{18,... | collective-permute-start | bytes 3538952 | tf_op jit(solution)/shard_map/ppermute | solution.py:105
  1253.9 97.4 %collective-permute-start.76 = (bf16[256,2304]{1,0:T(8,128)(2,1)}, bf16[256,2304]{1,0:T(8,128)(2,1)}, u32[]{:S(2)}, u32[]{:S(2)}) collective-permute-start(bf16[256,2304]{1,0:T(8,128)(2,1)} %add_convert_fusion), channel_id=1, source_target_pairs={{1,0},{2,3},{5,4},{6,7},{9,8},{10,11},{13,12},{14,15},{17,16},{18,... | collective-permute-start | bytes 3538952 | tf_op jit(solution)/shard_map/ppermute | solution.py:105
  1274.0 115.7 %collective-permute-start.101 = (bf16[288,2304]{1,0:T(8,128)(2,1)}, bf16[288,2304]{1,0:T(8,128)(2,1)}, u32[]{:S(2)}, u32[]{:S(2)}) collective-permute-start(bf16[288,2304]{1,0:T(8,128)(2,1)} %pad_maximum_fusion.8), channel_id=1, source_target_pairs={{0,16},{8,24},{16,0},{24,8},{1,17},{9,25},{17,1},{25,9},{2,18},{10... | collective-permute-start | bytes 3981320 | tf_op jit(solution)/shard_map/ppermute | solution.py:90
  1280.2 109.5 %collective-permute-start.100 = (bf16[288,2304]{1,0:T(8,128)(2,1)}, bf16[288,2304]{1,0:T(8,128)(2,1)S(1)}, u32[]{:S(2)}, u32[]{:S(2)}) collective-permute-start(bf16[288,2304]{1,0:T(8,128)(2,1)} %pad_maximum_fusion.7), channel_id=1, source_target_pairs={{0,8},{8,0},{16,24},{24,16},{1,9},{9,1},{17,25},{25,17},{2,10},{10... | collective-permute-start | bytes 3981320 | tf_op jit(solution)/shard_map/ppermute | solution.py:91
  1302.8 63.7 %collective-permute-start.81 = (bf16[4,288,2304]{2,1,0:T(8,128)(2,1)}, bf16[4,288,2304]{2,1,0:T(8,128)(2,1)}, u32[]{:S(2)}, u32[]{:S(2)}) collective-permute-start(bf16[4,288,2304]{2,1,0:T(8,128)(2,1)} %dynamic-slice_bitcast_fusion), channel_id=1, source_target_pairs={{0,4},{4,0},{1,5},{5,1},{2,6},{6,2},{3,7},{7,3},{8,12},{12,8},{9,1... | collective-permute-start | bytes 15925256 | tf_op jit(solution)/shard_map/ppermute | solution.py:72
  1393.8 125.0 %collective-permute-start.95 = (bf16[288,2304]{1,0:T(8,128)(2,1)S(1)}, bf16[288,2304]{1,0:T(8,128)(2,1)S(1)}, u32[]{:S(2)}, u32[]{:S(2)}) collective-permute-start(bf16[288,2304]{1,0:T(8,128)(2,1)S(1)} %pad_maximum_fusion.4), channel_id=1, source_target_pairs={{0,16},{8,24},{16,0},{24,8},{1,17},{9,25},{17,1},{25,9},{2,18},{10... | collective-permute-start | bytes 3981320 | tf_op jit(solution)/shard_map/ppermute | solution.py:90
  1412.5 106.9 %collective-permute-start.94 = (bf16[288,2304]{1,0:T(8,128)(2,1)S(1)}, bf16[288,2304]{1,0:T(8,128)(2,1)S(1)}, u32[]{:S(2)}, u32[]{:S(2)}) collective-permute-start(bf16[288,2304]{1,0:T(8,128)(2,1)S(1)} %pad_maximum_fusion.3), channel_id=1, source_target_pairs={{0,8},{8,0},{16,24},{24,16},{1,9},{9,1},{17,25},{25,17},{2,10},{10... | collective-permute-start | bytes 3981320 | tf_op jit(solution)/shard_map/ppermute | solution.py:91
  1413.2 117.7 %collective-permute-start.98 = (bf16[288,2304]{1,0:T(8,128)(2,1)S(1)}, bf16[288,2304]{1,0:T(8,128)(2,1)S(1)}, u32[]{:S(2)}, u32[]{:S(2)}) collective-permute-start(bf16[288,2304]{1,0:T(8,128)(2,1)S(1)} %pad_maximum_fusion.6), channel_id=1, source_target_pairs={{0,16},{8,24},{16,0},{24,8},{1,17},{9,25},{17,1},{25,9},{2,18},{10... | collective-permute-start | bytes 3981320 | tf_op jit(solution)/shard_map/ppermute | solution.py:90
  1480.1 50.7 %collective-permute-start.97 = (bf16[288,2304]{1,0:T(8,128)(2,1)S(1)}, bf16[288,2304]{1,0:T(8,128)(2,1)S(1)}, u32[]{:S(2)}, u32[]{:S(2)}) collective-permute-start(bf16[288,2304]{1,0:T(8,128)(2,1)S(1)} %pad_maximum_fusion.5), channel_id=1, source_target_pairs={{0,8},{8,0},{16,24},{24,16},{1,9},{9,1},{17,25},{25,17},{2,10},{10... | collective-permute-start | bytes 3981320 | tf_op jit(solution)/shard_map/ppermute | solution.py:91
  (311 other events, 7660.1 us)

commit v2 on v1

--- a/solution.py
+++ b/solution.py
@@ -3,6 +3,8 @@
 import jax
 import jax.numpy as jnp
 from jax import lax
+from jax.experimental import pallas as pl
+from jax.experimental.pallas import tpu as pltpu
 from jax.sharding import PartitionSpec as P
 
 HEAD = 256
@@ -195,7 +197,370 @@
     return d_queries, d_keys, d_values
 
 
-def per_device(
+MESH = pl.DeviceIdType.MESH
+UNIT = 256
+TILE = 256
+
+
+def ffn_kernel(
+    heads_ref, scale_ref, x_hbm, cot_hbm, w_out_hbm, own_hbm,
+    out_hbm, ffn_in_hbm, hidden_hbm, d_ffn_hbm, d_gate_hbm, d_up_hbm, d_attn_hbm, d_heads_hbm,
+    d_mid_hbm, gain_ref, attn_hbm, slope_hbm, value_hbm,
+    weights, w_out, send, near, across, total, xb, cb, ab, act, stage, d_mid, d_heads,
+    line_send, line_recv, credit, local, ag_send, ag_recv, ag_local,
+):
+    dp, core, z = lax.axis_index("dp"), lax.axis_index("ctx"), lax.axis_index("mp")
+    width, units = xb.shape[1], weights.shape[2]
+    rows_own = own_hbm.shape[1]
+    half = rows_own // 2
+    inner = (z == 1) | (z == 2)
+    outer = (z == 0) | (z == 3)
+    x_peer, y_peer = (dp ^ 1, core, z), (dp ^ 2, core, z)
+    core_peer = (dp, 1 - core, z)
+    near_peer = (dp, core, z ^ 1)
+    far_peer = (dp, core, 3 - z)
+
+    barrier = pltpu.get_barrier_semaphore()
+    for peer in (x_peer, y_peer, core_peer, near_peer, far_peer):
+        pl.semaphore_signal(barrier, inc=1, device_id=peer, device_id_type=MESH)
+    pl.semaphore_wait(barrier, 5)
+
+    def block(mask, other=False, low=0, size=rows_own):
+        owner = (dp ^ mask) * 2 + ((1 - core) if other else core)
+        return pl.ds(pl.multiple_of(owner * rows_own + low, 16), size)
+
+    def gather(w, name, recv=False):
+        table = {
+            "x": (0, block(0), x_peer, block(1)),
+            "y": (1, block(0), y_peer, block(2)),
+            "top": (2, block(2, False, 0, half), x_peer, block(3, False, 0, half)),
+            "low": (3, block(1, False, half, half), y_peer, block(3, False, half, half)),
+            "own_c": (4, block(0), core_peer, block(0, True)),
+            "x_c": (5, block(1), core_peer, block(1, True)),
+            "y_c": (6, block(2), core_peer, block(2, True)),
+            "top_c": (7, block(3, False, 0, half), core_peer, block(3, True, 0, half)),
+            "low_c": (8, block(3, False, half, half), core_peer, block(3, True, half, half)),
+        }
+        index, out_rows, peer, in_rows = table[name]
+        rows = in_rows if recv else out_rows
+        src = own_hbm.at[w] if name in ("x", "y", "own_c") else weights.at[w, rows]
+        return pltpu.make_async_remote_copy(
+            src_ref=src, dst_ref=weights.at[w, rows], send_sem=ag_send.at[w, index],
+            recv_sem=ag_recv.at[w, index], device_id=peer, device_id_type=MESH,
+        )
+
+    def own_copy(w):
+        return pltpu.make_async_copy(own_hbm.at[w], weights.at[w, block(0)], ag_local.at[w])
+
+    def gather_first(w):
+        for name in ("x", "y", "own_c"):
+            gather(w, name).start()
+        own_copy(w).start()
+
+    def gather_second(w):
+        gather(w, "x", True).wait_recv()
+        gather(w, "low").start()
+        gather(w, "x_c").start()
+        gather(w, "y", True).wait_recv()
+        gather(w, "top").start()
+        gather(w, "y_c").start()
+
+    def gather_third(w):
+        for name in ("top", "low"):
+            gather(w, name, True).wait_recv()
+            gather(w, name + "_c").start()
+
+    def gather_end(w):
+        for name in ("own_c", "x_c", "y_c", "top_c", "low_c"):
+            gather(w, name, True).wait_recv()
+        own_copy(w).wait()
+        for name in ("x", "y", "top", "low", "own_c", "x_c", "y_c", "top_c", "low_c"):
+            gather(w, name).wait_send()
+
+    def hop(kind, i):
+        src = (send.at[i % 3], send.at[i % 3], total.at[i % 4])[kind]
+        dst = (near.at[i % 3], across.at[i % 2], total.at[i % 4])[kind]
+        return pltpu.make_async_remote_copy(
+            src_ref=src, dst_ref=dst, send_sem=line_send.at[kind, i % 4],
+            recv_sem=line_recv.at[kind, i % 4],
+            device_id=far_peer if kind == 1 else near_peer, device_id_type=MESH,
+        )
+
+    def add_rows(dst, a, b):
+        @pl.loop(0, UNIT // 16)
+        def _(r):
+            rows = pl.ds(pl.multiple_of(r * 16, 16), 16)
+            dst[rows] = (a[rows].astype(F32) + b[rows].astype(F32)).astype(BF)
+
+    def boundary(k, up=True, cross=True, back=True, done=True):
+        @pl.when(outer)
+        def _():
+            if done:
+                hop(2, k - 3).wait_recv()
+            if cross:
+                hop(0, k - 1).wait_send()
+            if up:
+                hop(0, k).start()
+
+        @pl.when(inner)
+        def _():
+            if cross:
+                i = k - 1
+                hop(0, i).wait_recv()
+                add_rows(send.at[i % 3], send.at[i % 3], near.at[i % 3])
+                if isinstance(i, int):
+                    if i >= 2:
+                        pl.semaphore_wait(credit, 1)
+                else:
+                    pl.semaphore_wait(credit, 1)
+                hop(1, i).start()
+            if back:
+                i = k - 2
+                hop(1, i).wait_recv()
+                hop(1, i).wait_send()
+                add_rows(total.at[i % 4], send.at[i % 3], across.at[i % 2])
+                if not isinstance(i, int) or i < 10:
+                    pl.semaphore_signal(credit, inc=1, device_id=far_peer, device_id_type=MESH)
+                hop(2, i).start()
+            if done:
+                hop(2, k - 3).wait_send()
+
+    def rows_of(u):
+        return pl.ds(pl.multiple_of(u * UNIT, UNIT), UNIT)
+
+    def load(ref, u, dst, sem):
+        return pltpu.make_async_copy(ref.at[rows_of(u)], dst, local.at[sem])
+
+    def store(src, ref, u, sem):
+        return pltpu.make_async_copy(src, ref.at[rows_of(u)], local.at[sem])
+
+    def tile(n):
+        return pl.ds(pl.multiple_of(n * TILE, TILE), TILE)
+
+    def each_rows(body):
+        @pl.loop(0, UNIT // 16)
+        def _(r):
+            body(pl.ds(pl.multiple_of(r * 16, 16), 16))
+
+    def scale(i):
+        return scale_ref[i : i + 1]
+
+    def add_gain(index, v):
+        gain_ref[index] += v[:8] + v[8:]
+
+    def project_out(u, k):
+        dst = send.at[k % 3]
+
+        @pl.loop(0, width // TILE)
+        def _(n):
+            dst[:, tile(n)] = dot_t(heads_ref[rows_of(u)], w_out[tile(n)]).astype(BF)
+
+    def middle(rows, u4):
+        attn = total[u4, rows].astype(F32) if u4 is not None else ab[rows].astype(F32)
+        r_two = inverse_rms(attn)
+        return attn, r_two, xb[rows].astype(F32) + attn * r_two * scale(1)
+
+    def forward(u, k):
+        load(x_hbm, u, xb, 0).start()
+        store(total.at[u], attn_hbm, u, 1).start()
+        load(x_hbm, u, xb, 0).wait()
+
+        def body(rows):
+            _, _, mid = middle(rows, u)
+            act[rows] = (mid * inverse_rms(mid) * scale(2)).astype(BF)
+
+        each_rows(body)
+        store(act, ffn_in_hbm, u, 2).start()
+
+        @pl.loop(0, units // TILE)
+        def _(f):
+            gate = dot(act[...], weights[0, :, tile(f)])
+            up = dot(act[...], weights[1, :, tile(f)])
+            value, slope = gelu_parts(gate)
+            stage[0, :, tile(f)] = (value * up).astype(BF)
+            stage[1, :, tile(f)] = (slope * up).astype(BF)
+            stage[2, :, tile(f)] = value.astype(BF)
+
+        saves = ((0, hidden_hbm), (1, slope_hbm), (2, value_hbm))
+        for i, ref in saves:
+            store(stage.at[i], ref, u, 3 + i).start()
+        dst = send.at[k % 3]
+
+        @pl.loop(0, width // TILE)
+        def _(n):
+            dst[:, tile(n)] = dot_t(stage[0], weights[2, tile(n)]).astype(BF)
+
+        for i, ref in saves:
+            store(stage.at[i], ref, u, 3 + i).wait()
+        store(total.at[u], attn_hbm, u, 1).wait()
+        store(act, ffn_in_hbm, u, 2).wait()
+
+    def backward(u, k):
+        loads = (
+            load(x_hbm, u, xb, 0), load(attn_hbm, u, ab, 1), load(cot_hbm, u, cb, 2),
+            load(slope_hbm, u, stage.at[1], 4), load(value_hbm, u, stage.at[2], 5),
+        )
+        for copy in loads:
+            copy.start()
+        for copy in loads:
+            copy.wait()
+
+        def body(rows):
+            _, _, mid = middle(rows, None)
+            ffn = total[u, rows].astype(F32)
+            r = inverse_rms(ffn)
+            dy = cb[rows].astype(F32)
+            xb[rows] = (mid + ffn * r * scale(3)).astype(BF)
+            scaled = scale(3) * dy
+            mean = jnp.mean(scaled * ffn, axis=-1, keepdims=True)
+            act[rows] = (r * scaled - ffn * (r * r * r) * mean).astype(BF)
+            add_gain(2, ffn * r * dy)
+
+        each_rows(body)
+        store(xb, out_hbm, u, 0).start()
+        store(act, d_ffn_hbm, u, 1).start()
+
+        @pl.loop(0, units // TILE)
+        def _(f):
+            d_hidden = dot(act[...], weights[2, :, tile(f)])
+            stage[1, :, tile(f)] = (d_hidden * stage[1, :, tile(f)].astype(F32)).astype(BF)
+            stage[2, :, tile(f)] = (d_hidden * stage[2, :, tile(f)].astype(F32)).astype(BF)
+
+        store(stage.at[1], d_gate_hbm, u, 4).start()
+        store(stage.at[2], d_up_hbm, u, 5).start()
+        dst = send.at[k % 3]
+
+        @pl.loop(0, width // TILE)
+        def _(n):
+            part = dot_t(stage[1], weights[0, tile(n)]) + dot_t(stage[2], weights[1, tile(n)])
+            dst[:, tile(n)] = part.astype(BF)
+
+        store(xb, out_hbm, u, 0).wait()
+        store(act, d_ffn_hbm, u, 1).wait()
+        store(stage.at[1], d_gate_hbm, u, 4).wait()
+        store(stage.at[2], d_up_hbm, u, 5).wait()
+
+    def last(u):
+        loads = (load(x_hbm, u, xb, 0), load(attn_hbm, u, ab, 1), load(cot_hbm, u, cb, 2))
+        for copy in loads:
+            copy.start()
+        for copy in loads:
+            copy.wait()
+
+        def body(rows):
+            attn, r_two, mid = middle(rows, None)
+            r = inverse_rms(mid)
+            dy = total[u, rows].astype(F32)
+            scaled = scale(2) * dy
+            mean = jnp.mean(scaled * mid, axis=-1, keepdims=True)
+            grad = cb[rows].astype(F32) + r * scaled - mid * (r * r * r) * mean
+            add_gain(1, mid * r * dy)
+            d_mid[rows] = grad
+            scaled = scale(1) * grad
+            mean = jnp.mean(scaled * attn, axis=-1, keepdims=True)
+            act[rows] = (r_two * scaled - attn * (r_two * r_two * r_two) * mean).astype(BF)
+            add_gain(0, attn * r_two * grad)
+
+        each_rows(body)
+        store(d_mid, d_mid_hbm, u, 0).start()
+        store(act, d_attn_hbm, u, 1).start()
+        for h in range(w_out.shape[1] // TILE):
+            columns = slice(h * TILE, (h + 1) * TILE)
+            d_heads[:, columns] = dot(act[...], w_out[:, columns]).astype(BF)
+        store(d_heads, d_heads_hbm, u, 2).start()
+        store(d_mid, d_mid_hbm, u, 0).wait()
+        store(act, d_attn_hbm, u, 1).wait()
+        store(d_heads, d_heads_hbm, u, 2).wait()
+
+    gather_first(0)
+    pltpu.make_async_copy(w_out_hbm, w_out, local.at[0]).start()
+    gain_ref[...] = jnp.zeros_like(gain_ref)
+    pltpu.make_async_copy(w_out_hbm, w_out, local.at[0]).wait()
+    project_out(0, 0)
+    boundary(0, cross=False, back=False, done=False)
+    project_out(1, 1)
+    project_out(2, 2)
+    boundary(1, back=False, done=False)
+    gather_second(0)
+    gather_first(1)
+    boundary(2, done=False)
+    project_out(3, 3)
+    gather_third(0)
+    gather_second(1)
+    gather_first(2)
+    boundary(3)
+    gather_third(1)
+    gather_second(2)
+    gather_third(2)
+    for w in range(3):
+        gather_end(w)
+    forward(0, 4)
+
+    @pl.loop(4, 7)
+    def _(k):
+        boundary(k)
+        forward(k - 3, k + 1)
+
+    @pl.loop(7, 11)
+    def _(k):
+        boundary(k)
+        backward(k - 7, k + 1)
+
+    for k in (11, 12, 13, 14):
+        boundary(k, up=k < 12, cross=k < 13, back=k < 14)
+        last(k - 11)
+
+
+def ffn_call(heads_out, scales, x, cot, w_out, own):
+    tokens, width = x.shape
+    units = own.shape[2]
+    assert tokens == 4 * UNIT
+    full = jax.ShapeDtypeStruct((tokens, width), BF)
+    wide = jax.ShapeDtypeStruct((tokens, units), BF)
+    outs = (
+        full, full, wide, full, wide, wide, full,
+        jax.ShapeDtypeStruct((tokens, w_out.shape[1]), BF),
+        jax.ShapeDtypeStruct((tokens, width), F32),
+        jax.ShapeDtypeStruct((3, 8, width), F32),
+        full, wide, wide,
+    )
+    anywhere, vmem = pl.BlockSpec(memory_space=pl.ANY), pl.BlockSpec(memory_space=pltpu.VMEM)
+    dma = pltpu.SemaphoreType.DMA
+    return pl.pallas_call(
+        ffn_kernel,
+        out_shape=outs,
+        in_specs=[vmem, vmem, anywhere, anywhere, anywhere, anywhere],
+        out_specs=[anywhere] * 9 + [vmem] + [anywhere] * 3,
+        scratch_shapes=[
+            pltpu.VMEM((3, width, units), BF),
+            pltpu.VMEM(w_out.shape, BF),
+            pltpu.VMEM((3, UNIT, width), BF),
+            pltpu.VMEM((3, UNIT, width), BF),
+            pltpu.VMEM((2, UNIT, width), BF),
+            pltpu.VMEM((4, UNIT, width), BF),
+            pltpu.VMEM((UNIT, width), BF),
+            pltpu.VMEM((UNIT, width), BF),
+            pltpu.VMEM((UNIT, width), BF),
+            pltpu.VMEM((UNIT, width), BF),
+            pltpu.VMEM((3, UNIT, units), BF),
+            pltpu.VMEM((UNIT, width), F32),
+            pltpu.VMEM((UNIT, w_out.shape[1]), BF),
+            dma((3, 4)),
+            dma((3, 4)),
+            pltpu.SemaphoreType.REGULAR,
+            dma((6,)),
+            dma((3, 9)),
+            dma((3, 9)),
+            dma((3,)),
+        ],
+        compiler_params=pltpu.CompilerParams(
+            collective_id=1, has_side_effects=True, vmem_limit_bytes=60 * 2**20
+        ),
+        name="ffn",
+    )(heads_out, scales, x, cot, w_out, own)
+
+
+def fast_device(
     sizes,
     inputs,
     segment_ids,
@@ -220,9 +585,6 @@
     gain_one, gain_two, gain_three, gain_four = [gains[:, i] for i in range(4)]
     w_qkv, mark = gather_rows(qkv_own, sizes, None)
     w_out, mark = gather_rows(low[3], sizes, mark)
-    w_gate, mark = gather_rows(low[4], sizes, mark)
-    w_up, mark = gather_rows(low[5], sizes, mark)
-    w_down, mark = gather_rows(low[6], sizes, mark)
 
     start = lax.axis_index("ctx") * tokens
     causal = (start + jnp.arange(tokens))[:, None] >= jnp.arange(full_len)[None, :]
@@ -257,6 +619,142 @@
             )
         )
 
+    flat = (batches * tokens, width)
+    heads_all = jnp.concatenate([s["heads_out"] for s in state])
+    outs = ffn_call(
+        heads_all, (1.0 + gains).T, inputs.reshape(flat), cotangent.reshape(flat), w_out,
+        jnp.stack(low[4:]),
+    )
+    output, ffn_in, hidden, d_ffn, d_gate, d_up, d_attn, d_heads_all, d_mid, gain_parts = outs[:10]
+    units = [(mb, cut) for mb in range(batches) for cut in range(cuts)]
+    work = []
+    for i, (mb, cut) in enumerate(units):
+        work.append(dict(rows=slice(cut * unit, (cut + 1) * unit), mb=mb, all=slice(i * unit, (i + 1) * unit)))
+
+    g_down = t_dot(d_ffn, hidden)
+    g_gate = t_dot(ffn_in, d_gate)
+    g_up = t_dot(ffn_in, d_up)
+    s_down, mark = scatter_rows(g_down, sizes, None)
+    s_gate, mark = scatter_rows(g_gate, sizes, mark)
+    s_up, mark = scatter_rows(g_up, sizes, mark)
+
+    for mb in range(batches):
+        s = state[mb]
+        d_heads = d_heads_all[mb * tokens : (mb + 1) * tokens]
+        d_out = jnp.concatenate(jnp.split(d_heads, heads, axis=1))
+        d_queries, d_keys, d_values = attend_back(
+            s["saved"], s["queries"], s["keys"], s["values"], d_out
+        )
+        d_kv = scatter_ctx(jnp.concatenate([d_keys, d_values], axis=1), sizes)
+        pieces = [rotate(q, s["cosine"], -s["sine"]) for q in jnp.split(d_queries, heads)]
+        pieces += [rotate(d_kv[:, :HEAD], s["cosine"], -s["sine"]), d_kv[:, HEAD:]]
+        s["d_proj"] = jnp.concatenate(pieces, axis=1).astype(BF)
+    for w in work:
+        part = dot_t(state[w["mb"]]["d_proj"][w["rows"]], w_qkv).astype(BF)
+        w["d_attn_in"] = sum_mp(part, sizes)
+
+    g_out = t_dot(d_attn, heads_all)
+    g_qkv = t_dot(
+        jnp.concatenate([s["attn_in"] for s in state]),
+        jnp.concatenate([s["d_proj"] for s in state]),
+    )
+    s_out, mark = scatter_rows(g_out, sizes, mark)
+    s_qkv, mark = scatter_rows(g_qkv, sizes, mark)
+
+    for w in work:
+        s = state[w["mb"]]
+        back, w["g_one"] = norm_back(
+            s["x"][w["rows"]], s["r_one"][w["rows"]], gain_one, w["d_attn_in"].astype(F32)
+        )
+        w["input_grad"] = (d_mid[w["all"]] + back).astype(BF)
+
+    gain_grads = jnp.concatenate(
+        [sum(w["g_one"] for w in work)[None], jnp.sum(gain_parts, axis=1)]
+    )
+    gain_grads = sum_small(gain_grads, ("ctx", "dp"), sizes)
+    summed = (
+        s_qkv[:, :q_cols], s_qkv[:, q_cols : q_cols + k_cols], s_qkv[:, q_cols + k_cols :],
+        s_out, s_gate, s_up, s_down,
+    )
+    weight_sq = sum(jnp.sum(g * g) for g in (s_qkv, s_out, s_gate, s_up, s_down))
+    weight_sq = sum_small(weight_sq.reshape(1, 1), ("ctx", "dp", "mp"), sizes)[0, 0]
+    norm_value = jnp.sqrt(weight_sq + jnp.sum(gain_grads * gain_grads))
+    factor = 1.0 / jnp.maximum(norm_value, 1.0)
+    own = masters[7].shape[0]
+    place = (lax.axis_index("dp") * sizes["ctx"] + lax.axis_index("ctx")) * own
+    own_gains = lax.dynamic_slice_in_dim(gain_grads, place, own, 1)
+    summed += tuple(own_gains[i] for i in range(4))
+    new_moments = tuple(0.5 * m + 0.5 * factor * g for m, g in zip(moments, summed))
+    changes = tuple(-RATE * (m + 0.01 * w) for w, m in zip(masters[:7], new_moments[:7]))
+
+    return (
+        output.reshape(inputs.shape),
+        jnp.concatenate([w["input_grad"] for w in work]).reshape(inputs.shape), norm_value.reshape(1), *changes, *new_moments
+    )
+
+
+def per_device(
+    sizes,
+    inputs,
+    segment_ids,
+    positions,
+    cotangent,
+    *params,
+):
+    masters, moments = params[:11], params[11:]
+    batches, seqs, tokens, width = inputs.shape
+    assert seqs == 1
+    full_len = segment_ids.shape[2]
+    q_cols, k_cols = masters[0].shape[1], masters[1].shape[1]
+    heads = q_cols // HEAD
+    assert k_cols == HEAD
+    cuts = 2 if tokens >= 512 else 1
+    unit = tokens // cuts
+
+    low = [w.astype(BF) for w in masters[:7]]
+    qkv_own = jnp.concatenate(low[:3], axis=1)
+    gains_own = jnp.stack([g.astype(BF) for g in masters[7:]], axis=1)
+    gains = lax.all_gather(gains_own, ("dp", "ctx"), axis=0, tiled=True).astype(F32)
+    gain_one, gain_two, gain_three, gain_four = [gains[:, i] for i in range(4)]
+    w_qkv, mark = gather_rows(qkv_own, sizes, None)
+    w_out, mark = gather_rows(low[3], sizes, mark)
+    w_gate, mark = gather_rows(low[4], sizes, mark)
+    w_up, mark = gather_rows(low[5], sizes, mark)
+    w_down, mark = gather_rows(low[6], sizes, mark)
+
+    start = lax.axis_index("ctx") * tokens
+    causal = (start + jnp.arange(tokens))[:, None] >= jnp.arange(full_len)[None, :]
+    frequency = jnp.exp(
+        jnp.arange(HEAD // 2, dtype=F32) * (-2.0 * math.log(10000.0) / HEAD)
+    )
+
+    state = []
+    for mb in range(batches):
+        x = inputs[mb, 0].astype(F32)
+        r_one = inverse_rms(x)
+        attn_in = (x * r_one * (1.0 + gain_one)).astype(BF)
+        angles = positions[mb, 0].astype(F32)[:, None] * frequency
+        cosine, sine = jnp.cos(angles), jnp.sin(angles)
+        seg = segment_ids[mb, 0]
+        seg_local = lax.dynamic_slice_in_dim(seg, start, tokens)
+        allowed = causal & (seg_local[:, None] == seg[None, :])
+        proj = dot(attn_in, w_qkv)
+        queries = jnp.concatenate(
+            [rotate(proj[:, h * HEAD : (h + 1) * HEAD], cosine, sine) for h in range(heads)]
+        ).astype(BF)
+        keys = rotate(proj[:, q_cols : q_cols + HEAD], cosine, sine).astype(BF)
+        values = proj[:, q_cols + HEAD :].astype(BF)
+        both = swap_ctx(jnp.concatenate([keys, values], axis=1), sizes)
+        keys_all, values_all = both[:, :HEAD], both[:, HEAD:]
+        out, saved = attend(queries, keys_all, values_all, allowed)
+        heads_out = jnp.concatenate(jnp.split(out, heads, axis=0), axis=1)
+        state.append(
+            dict(
+                x=x, r_one=r_one, attn_in=attn_in, cosine=cosine, sine=sine, queries=queries,
+                keys=keys_all, values=values_all, saved=saved, heads_out=heads_out,
+            )
+        )
+
     units = [(mb, cut) for mb in range(batches) for cut in range(cuts)]
     work = []
     for mb, cut in units:
@@ -374,7 +872,9 @@
     data = P(None, "dp", "ctx", None)
 
     def run(*args):
-        return per_device(sizes, *args)
+        batches, _, tokens, _ = args[0].shape
+        fast = sizes == dict(dp=4, ctx=2, mp=4) and batches == 2 and tokens == 2 * UNIT
+        return (fast_device if fast else per_device)(sizes, *args)
 
     return jax.shard_map(
         run,

time: 1600 us -> 1160 us (0.72)
  waiting for transfers between devices: 841 us -> 356 us
  Pallas kernels: 0 us -> 432 us
  matrix products: 277 us -> 90.1 us
  local copies, waits for them, and re-layouts: 112 us -> 41 us
  starting transfers between devices: 131 us -> 63.2 us
  other arithmetic: 207 us -> 156 us
    pallas_call x0 -> x1, Pallas kernels: none -> 432 us  [ffn_call(): pl.pallas_call(ffn_kernel, out_shape=outs, in_specs=[vmem, vmem, anywhere...]
    ppermute x16 -> x4, waiting for transfers between devices: 395 us -> 85.3 us  [sum_mp(): back = lax.ppermute(total, 'mp', [(1, 0), (2, 3)])]
    ppermute x16 -> x4, waiting for transfers between devices: 211 us -> 78.6 us  [sum_mp(): near = lax.ppermute(part, 'mp', [(0, 1), (3, 2)])]
    dot_general x24 -> x8, matrix products: 108 us -> 16.8 us  [dot_t(): lax.dot_general(a, b, (((1,), (1,)), ((), ())), preferred_element_type=F32)]
    dot_general x22 -> x6, matrix products: 96.9 us -> 10.4 us  [dot(): lax.dot_general(a, b, (((1,), (0,)), ((), ())), preferred_element_type=F32)]
    ppermute x5 -> x2, waiting for transfers between devices: 80.4 us -> 9.49 us  [gather_rows(): far_top = lax.ppermute(from_y[:half], **flip('dp', dp, 1))]
    ppermute x16 -> x4, starting transfers between devices: 34.2 us -> 6.2 us  [sum_mp(): near = lax.ppermute(part, 'mp', [(0, 1), (3, 2)])]
    ppermute x5, waiting for transfers between devices: 53.7 us -> 81 us  [scatter_rows(): far_top = lax.ppermute(part(3, 0, half).astype(BF), **flip('dp', dp, 1))]
  transfers between devices with their start and end apart: 110 -> 59, of which waited for: 50 -> 28; matrix products, arithmetic and copies ran while one was open for 26% -> 18% of each run, Pallas kernels for 0% -> 0%
where the time goes in v2:
time: 1160 us
  Pallas kernels  432 us (37%)
  waiting for transfers between devices  356 us (31%)
  other arithmetic  156 us (13%)
  matrix products  90.1 us (8%)
  starting transfers between devices  63.2 us (5%)
  local copies, waits for them, and re-layouts  41 us (4%)
  between operations  11.8 us (1%)
    pallas_call x1, Pallas kernels, ffn_call(): pl.pallas_call(ffn_kernel, out_shape=outs, in_specs=[vmem, vmem, anywhere...  432 us
    ppermute x5, waiting for transfers between devices, scatter_rows(): far_low = lax.ppermute(part(3, half, rows).astype(BF), **flip('dp', dp, 2))  85.5 us
    ppermute x4, waiting for transfers between devices, sum_mp(): back = lax.ppermute(total, 'mp', [(1, 0), (2, 3)])  85.3 us
    ppermute x5, waiting for transfers between devices, scatter_rows(): far_top = lax.ppermute(part(3, 0, half).astype(BF), **flip('dp', dp, 1))  81 us
    ppermute x4, waiting for transfers between devices, sum_mp(): near = lax.ppermute(part, 'mp', [(0, 1), (3, 2)])  78.6 us
    dot_general x9, matrix products, t_dot(): lax.dot_general(a, b, (((0,), (0,)), ((), ())), preferred_element_type=F32)  62.8 us
    mul x6, other arithmetic, fast_device(): -RATE * (m + 0.01 * w)  24.1 us
  transfers between devices with their start and end apart: 59, of which 28 were waited for; matrix products, arithmetic and copies ran while one was open for 18% of the time, Pallas kernels for 0%

profile of v2, /device:TPU:0, one launch (start us, length us, event | category | flops | bytes accessed | tf_op | source)
XLA Modules:
  0.0 1159.2 jit_solution(4016092810811589481)
XLA Ops:
  4.8 2.9 collective-permute-start
  9.8 4.1 fusion.6
  13.9 4.5 slice_convert_fusion.1
  22.3 8.2 all-gather
  37.0 4.6 fusion.8
  41.7 3.6 convert_bitcast_fusion
  57.8 5.4 collective-permute-done.2
  67.4 4.1 collective-permute-done.9
  97.3 432.0 %ffn.1 = (bf16[1024,2304]{1,0:T(8,128)(2,1)}, bf16[1024,2304]{1,0:T(8,128)(2,1)}, bf16[1024,2304]{1,0:T(8,128)(2,1)}, bf16[1024,2304]{1,0:T(8,128)(2,1)}, bf16[1...) custom-call(bf16[1024,512]{1,0:T(8,128)(2,1)} %maximum_maximum_fusio, ...), custom_call_target="tpu_custom_call" | custom-call | tf_op jit(solution)/shard_map/ffn/pallas_call | solution.py:529
  530.6 4.3 multiply_reduce_fusion.1
  557.3 16.2 %convolution_convert_fusion.2 = bf16[2304,2304]{1,0:T(8,128)(2,1)} fusion(bf16[1024,2304]{1,0:T(8,128)(2,1)S(1)} %bitcast.501, bf16[1024,2304]{1,0:T(8,128)(2,1)} %get-tuple-element.42), kind=kOutput, calls=%fused_computation.2 | convolution fusion | flops 10876944384 | bytes 20054016 | tf_op jit(solution)/shard_map/dot_general | solution.py:148
  573.5 14.1 %convolution_convert_fusion.1 = bf16[2304,2304]{1,0:T(8,128)(2,1)} fusion(bf16[1024,2304]{1,0:T(8,128)(2,1)S(1)} %bitcast.501, bf16[1024,2304]{1,0:T(8,128)(2,1)S(1)} %bitcast.503), kind=kOutput, calls=%fused_computation.1 | convolution fusion | flops 10876944384 | bytes 20054016 | tf_op jit(solution)/shard_map/dot_general | solution.py:148
  587.6 12.0 %convolution_convert_fusion = bf16[2304,2304]{1,0:T(8,128)(2,1)S(1)} fusion(bf16[1024,2304]{1,0:T(8,128)(2,1)S(1)} %bitcast.499, bf16[1024,2304]{1,0:T(8,128)(2,1)S(1)} %bitcast.497), kind=kOutput, calls=%fused_computation | convolution fusion | flops 10876944384 | bytes 20054016 | tf_op jit(solution)/shard_map/dot_general | solution.py:148
  599.6 3.0 dynamic-slice_bitcast_fusion.2
  605.4 6.8 convolution_convert_fusion.4
  613.4 2.8 fusion.238
  616.2 3.5 fusion.237
  640.6 12.6 %collective-permute-done.13 = bf16[256,2304]{1,0:T(8,128)(2,1)S(1)} collective-permute-done((bf16[256,2304]{1,0:T(8,128)(2,1)S(1)}, bf16[256,2304]{1,0:T(8,128)(2,1)S(1)}, u32[]{:S(2)}, u32[]{:S(2)}) %collective-permute-start.13) | collective-permute-done | bytes 1179680 | tf_op jit(solution)/shard_map/ppermute | solution.py:103
  655.3 23.1 %collective-permute-done.16 = bf16[256,2304]{1,0:T(8,128)(2,1)S(1)} collective-permute-done((bf16[256,2304]{1,0:T(8,128)(2,1)S(1)}, bf16[256,2304]{1,0:T(8,128)(2,1)S(1)}, u32[]{:S(2)}, u32[]{:S(2)}) %collective-permute-start.16) | collective-permute-done | bytes 1179680 | tf_op jit(solution)/shard_map/ppermute | solution.py:103
  680.4 23.3 %collective-permute-done.20 = bf16[256,2304]{1,0:T(8,128)(2,1)S(1)} collective-permute-done((bf16[256,2304]{1,0:T(8,128)(2,1)S(1)}, bf16[256,2304]{1,0:T(8,128)(2,1)S(1)}, u32[]{:S(2)}, u32[]{:S(2)}) %collective-permute-start.20) | collective-permute-done | bytes 1179680 | tf_op jit(solution)/shard_map/ppermute | solution.py:103
  709.1 19.6 %collective-permute-done.23 = bf16[256,2304]{1,0:T(8,128)(2,1)S(1)} collective-permute-done((bf16[256,2304]{1,0:T(8,128)(2,1)S(1)}, bf16[256,2304]{1,0:T(8,128)(2,1)S(1)}, u32[]{:S(2)}, u32[]{:S(2)}) %collective-permute-start.23) | collective-permute-done | bytes 1179680 | tf_op jit(solution)/shard_map/ppermute | solution.py:103
  744.6 3.0 add_convert_fusion
  749.0 9.7 convolution_convert_fusion.3
  758.7 9.7 collective-permute-done.15
  768.4 25.3 %collective-permute-done.18 = bf16[256,2304]{1,0:T(8,128)(2,1)} collective-permute-done((bf16[256,2304]{1,0:T(8,128)(2,1)S(1)}, bf16[256,2304]{1,0:T(8,128)(2,1)}, u32[]{:S(2)}, u32[]{:S(2)}) %collective-permute-start.18) | collective-permute-done | bytes 1179680 | tf_op jit(solution)/shard_map/ppermute | solution.py:107
  793.6 25.3 %collective-permute-done.22 = bf16[256,2304]{1,0:T(8,128)(2,1)} collective-permute-done((bf16[256,2304]{1,0:T(8,128)(2,1)S(1)}, bf16[256,2304]{1,0:T(8,128)(2,1)}, u32[]{:S(2)}, u32[]{:S(2)}) %collective-permute-start.22) | collective-permute-done | bytes 1179680 | tf_op jit(solution)/shard_map/ppermute | solution.py:107
  818.9 25.1 %collective-permute-done.25 = bf16[256,2304]{1,0:T(8,128)(2,1)} collective-permute-done((bf16[256,2304]{1,0:T(8,128)(2,1)}, bf16[256,2304]{1,0:T(8,128)(2,1)}, u32[]{:S(2)}, u32[]{:S(2)}) %collective-permute-start.25) | collective-permute-done | bytes 1179680 | tf_op jit(solution)/shard_map/ppermute | solution.py:107
  844.1 6.3 fusion.39
  855.4 15.6 %collective-permute-done.29 = bf16[144,2304]{1,0:T(8,128)(2,1)S(1)} collective-permute-done((bf16[144,2304]{1,0:T(8,128)(2,1)S(1)}, bf16[144,2304]{1,0:T(8,128)(2,1)S(1)}, u32[]{:S(2)}, u32[]{:S(2)}) %collective-permute-start.29) | collective-permute-done | bytes 663584 | tf_op jit(solution)/shard_map/ppermute | solution.py:88
  871.8 5.2 dynamic-slice_bitcast_fusion
  877.1 3.5 fusion.29
  885.4 3.4 fusion.37
  892.1 10.0 collective-permute-done.48
  912.0 36.7 %collective-permute-done.31 = bf16[144,2304]{1,0:T(8,128)(2,1)S(1)} collective-permute-done((bf16[144,2304]{1,0:T(8,128)(2,1)S(1)}, bf16[144,2304]{1,0:T(8,128)(2,1)S(1)}, u32[]{:S(2)}, u32[]{:S(2)}) %collective-permute-start.31) | collective-permute-done | bytes 663584 | tf_op jit(solution)/shard_map/ppermute | solution.py:88
  948.9 3.3 fusion.82
  953.3 2.8 multiply_reduce_fusion.2
  958.3 11.8 %collective-permute-done.42 = bf16[144,2304]{1,0:T(8,128)(2,1)S(1)} collective-permute-done((bf16[144,2304]{1,0:T(8,128)(2,1)}, bf16[144,2304]{1,0:T(8,128)(2,1)S(1)}, u32[]{:S(2)}, u32[]{:S(2)}) %collective-permute-start.42) | collective-permute-done | bytes 663584 | tf_op jit(solution)/shard_map/ppermute | solution.py:89
  973.5 3.4 fusion.75
  980.3 32.6 %collective-permute-done.45 = bf16[144,2304]{1,0:T(8,128)(2,1)S(1)} collective-permute-done((bf16[144,2304]{1,0:T(8,128)(2,1)}, bf16[144,2304]{1,0:T(8,128)(2,1)S(1)}, u32[]{:S(2)}, u32[]{:S(2)}) %collective-permute-start.45) | collective-permute-done | bytes 663584 | tf_op jit(solution)/shard_map/ppermute | solution.py:89
  1018.3 26.2 %collective-permute-done.39 = bf16[144,512]{1,0:T(8,128)(2,1)S(1)} collective-permute-done((bf16[144,512]{1,0:T(8,128)(2,1)S(1)}, bf16[144,512]{1,0:T(8,128)(2,1)S(1)}, u32[]{:S(2)}, u32[]{:S(2)}) %collective-permute-start.39) | collective-permute-done | bytes 147488 | tf_op jit(solution)/shard_map/ppermute | solution.py:89
  1045.5 4.9 collective-permute-done.35
  1052.3 28.7 %collective-permute-done.37 = bf16[144,1024]{1,0:T(8,128)(2,1)S(1)} collective-permute-done((bf16[144,1024]{1,0:T(8,128)(2,1)S(1)}, bf16[144,1024]{1,0:T(8,128)(2,1)S(1)}, u32[]{:S(2)}, u32[]{:S(2)}) %collective-permute-start.37) | collective-permute-done | bytes 294944 | tf_op jit(solution)/shard_map/ppermute | solution.py:88
  1084.6 6.4 collective-permute-done.41
  1096.6 3.7 multiply_reduce_fusion.3
  1136.4 2.9 add_multiply_fusion.3
  1139.4 5.4 add_multiply_fusion.2
  1144.8 5.4 add_multiply_fusion.1
  1150.2 5.4 add_multiply_fusion
  (527 shorter events, 215.1 us)
Async XLA Ops:
  4.8 42.8 %collective-permute-start = (bf16[288,1024]{1,0:T(8,128)(2,1)}, bf16[288,1024]{1,0:T(8,128)(2,1)}, u32[]{:S(2)}, u32[]{:S(2)}) collective-permute-start(bf16[288,1024]{1,0:T(8,128)(2,1)} %pad_maximum_fusion.8), channel_id=1, source_target_pairs={{0,8},{8,0},{16,24},{24,16},{1,9},{9,1},{17,25},{25,17},{2,10},{10... | collective-permute-start | bytes 1769480 | tf_op jit(solution)/shard_map/ppermute | solution.py:38
  7.7 41.9 %collective-permute-start.1 = (bf16[288,1024]{1,0:T(8,128)(2,1)}, bf16[288,1024]{1,0:T(8,128)(2,1)}, u32[]{:S(2)}, u32[]{:S(2)}) collective-permute-start(bf16[288,1024]{1,0:T(8,128)(2,1)} %pad_maximum_fusion.8), channel_id=1, source_target_pairs={{0,16},{8,24},{16,0},{24,8},{1,17},{9,25},{17,1},{25,9},{2,18},{10... | collective-permute-start | bytes 1769480 | tf_op jit(solution)/shard_map/ppermute | solution.py:39
  47.6 18.6 %collective-permute-start.7 = (bf16[288,512]{1,0:T(8,128)(2,1)S(1)}, bf16[288,512]{1,0:T(8,128)(2,1)S(1)}, u32[]{:S(2)}, u32[]{:S(2)}) collective-permute-start(bf16[288,512]{1,0:T(8,128)(2,1)S(1)} %copy-done.44), channel_id=1, source_target_pairs={{0,8},{8,0},{16,24},{24,16},{1,9},{9,1},{17,25},{25,17},{2,10},{10... | collective-permute-start | bytes 884744 | tf_op jit(solution)/shard_map/ppermute | solution.py:38
  49.1 16.0 %collective-permute-start.8 = (bf16[288,512]{1,0:T(8,128)(2,1)S(1)}, bf16[288,512]{1,0:T(8,128)(2,1)S(1)}, u32[]{:S(2)}, u32[]{:S(2)}) collective-permute-start(bf16[288,512]{1,0:T(8,128)(2,1)S(1)} %copy-done.44), channel_id=1, source_target_pairs={{0,16},{8,24},{16,0},{24,8},{1,17},{9,25},{17,1},{25,9},{2,18},{10... | collective-permute-start | bytes 884744 | tf_op jit(solution)/shard_map/ppermute | solution.py:39
  50.6 12.5 %collective-permute-start.2 = (bf16[144,1024]{1,0:T(8,128)(2,1)S(1)}, bf16[144,1024]{1,0:T(8,128)(2,1)S(1)}, u32[]{:S(2)}, u32[]{:S(2)}) collective-permute-start(bf16[144,1024]{1,0:T(8,128)(2,1)S(1)} %slice.339), channel_id=1, source_target_pairs={{0,8},{8,0},{16,24},{24,16},{1,9},{9,1},{17,25},{25,17},{2,10},{10... | collective-permute-start | bytes 884744 | tf_op jit(solution)/shard_map/ppermute | solution.py:40
  53.2 11.2 collective-permute-start.3
  65.1 12.9 %collective-permute-start.4 = (bf16[4,288,1024]{2,1,0:T(8,128)(2,1)}, bf16[4,288,1024]{2,1,0:T(8,128)(2,1)S(1)}, u32[]{:S(2)}, u32[]{:S(2)}) collective-permute-start(bf16[4,288,1024]{2,1,0:T(8,128)(2,1)} %bitcast_dynamic-update-slice_fusion.10), channel_id=1, source_target_pairs={{0,4},{4,0},{1,5},{5,1},{2,6},{6,2},{3,7},{7,3},{8,12},{12,8},{9,1... | collective-permute-start | bytes 7077896 | tf_op jit(solution)/shard_map/ppermute | solution.py:49
  555.9 56.3 %collective-permute-start.12 = (bf16[512,512]{1,0:T(8,128)(2,1)}, bf16[512,512]{1,0:T(8,128)(2,1)}, u32[]{:S(2)}, u32[]{:S(2)}) collective-permute-start(bf16[512,512]{1,0:T(8,128)(2,1)} %fusion.93), channel_id=1, source_target_pairs={{0,4},{4,0},{1,5},{5,1},{2,6},{6,2},{3,7},{7,3},{8,12},{12,8},{9,1... | collective-permute-start | bytes 1572872 | tf_op jit(solution)/shard_map/ppermute | solution.py:136
  556.8 74.0 %collective-permute-start.19 = (bf16[512,512]{1,0:T(8,128)(2,1)}, bf16[512,512]{1,0:T(8,128)(2,1)}, u32[]{:S(2)}, u32[]{:S(2)}) collective-permute-start(bf16[512,512]{1,0:T(8,128)(2,1)} %fusion.89), channel_id=1, source_target_pairs={{0,4},{4,0},{1,5},{5,1},{2,6},{6,2},{3,7},{7,3},{8,12},{12,8},{9,1... | collective-permute-start | bytes 1572872 | tf_op jit(solution)/shard_map/ppermute | solution.py:136
  605.3 101.4 %collective-permute-start.26 = (bf16[4,288,2304]{2,1,0:T(8,128)(2,1)}, bf16[4,288,2304]{2,1,0:T(8,128)(2,1)}, u32[]{:S(2)}, u32[]{:S(2)}) collective-permute-start(bf16[4,288,2304]{2,1,0:T(8,128)(2,1)} %dynamic-slice_bitcast_fusion.2), channel_id=1, source_target_pairs={{0,4},{4,0},{1,5},{5,1},{2,6},{6,2},{3,7},{7,3},{8,12},{12,8},{9,1... | collective-permute-start | bytes 15925256 | tf_op jit(solution)/shard_map/ppermute | solution.py:74
  625.4 27.8 %collective-permute-start.13 = (bf16[256,2304]{1,0:T(8,128)(2,1)S(1)}, bf16[256,2304]{1,0:T(8,128)(2,1)S(1)}, u32[]{:S(2)}, u32[]{:S(2)}) collective-permute-start(bf16[256,2304]{1,0:T(8,128)(2,1)S(1)} %convolution_convert_fusion.8), channel_id=1, source_target_pairs={{0,1},{3,2},{4,5},{7,6},{8,9},{11,10},{12,13},{15,14},{16,17},{19,... | collective-permute-start | bytes 3538952 | tf_op jit(solution)/shard_map/ppermute | solution.py:103
  627.0 51.5 %collective-permute-start.16 = (bf16[256,2304]{1,0:T(8,128)(2,1)S(1)}, bf16[256,2304]{1,0:T(8,128)(2,1)S(1)}, u32[]{:S(2)}, u32[]{:S(2)}) collective-permute-start(bf16[256,2304]{1,0:T(8,128)(2,1)S(1)} %convolution_convert_fusion.7), channel_id=1, source_target_pairs={{0,1},{3,2},{4,5},{7,6},{8,9},{11,10},{12,13},{15,14},{16,17},{19,... | collective-permute-start | bytes 3538952 | tf_op jit(solution)/shard_map/ppermute | solution.py:103
  635.9 67.9 %collective-permute-start.20 = (bf16[256,2304]{1,0:T(8,128)(2,1)S(1)}, bf16[256,2304]{1,0:T(8,128)(2,1)S(1)}, u32[]{:S(2)}, u32[]{:S(2)}) collective-permute-start(bf16[256,2304]{1,0:T(8,128)(2,1)S(1)} %convolution_convert_fusion.6), channel_id=1, source_target_pairs={{0,1},{3,2},{4,5},{7,6},{8,9},{11,10},{12,13},{15,14},{16,17},{19,... | collective-permute-start | bytes 3538952 | tf_op jit(solution)/shard_map/ppermute | solution.py:103
  639.0 89.7 %collective-permute-start.23 = (bf16[256,2304]{1,0:T(8,128)(2,1)S(1)}, bf16[256,2304]{1,0:T(8,128)(2,1)S(1)}, u32[]{:S(2)}, u32[]{:S(2)}) collective-permute-start(bf16[256,2304]{1,0:T(8,128)(2,1)S(1)} %convolution_convert_fusion.5), channel_id=1, source_target_pairs={{0,1},{3,2},{4,5},{7,6},{8,9},{11,10},{12,13},{15,14},{16,17},{19,... | collective-permute-start | bytes 3538952 | tf_op jit(solution)/shard_map/ppermute | solution.py:103
  653.5 81.9 %collective-permute-start.14 = (bf16[256,2304]{1,0:T(8,128)(2,1)S(1)}, bf16[256,2304]{1,0:T(8,128)(2,1)}, u32[]{:S(2)}, u32[]{:S(2)}) collective-permute-start(bf16[256,2304]{1,0:T(8,128)(2,1)S(1)} %add_convert_fusion.7), channel_id=1, source_target_pairs={{1,2},{2,1},{5,6},{6,5},{9,10},{10,9},{13,14},{14,13},{17,18},{18,... | collective-permute-start | bytes 3538952 | tf_op jit(solution)/shard_map/ppermute | solution.py:105
  678.7 59.8 %collective-permute-start.17 = (bf16[256,2304]{1,0:T(8,128)(2,1)S(1)}, bf16[256,2304]{1,0:T(8,128)(2,1)}, u32[]{:S(2)}, u32[]{:S(2)}) collective-permute-start(bf16[256,2304]{1,0:T(8,128)(2,1)S(1)} %add_convert_fusion.5), channel_id=1, source_target_pairs={{1,2},{2,1},{5,6},{6,5},{9,10},{10,9},{13,14},{14,13},{17,18},{18,... | collective-permute-start | bytes 3538952 | tf_op jit(solution)/shard_map/ppermute | solution.py:105
  705.0 36.4 %collective-permute-start.21 = (bf16[256,2304]{1,0:T(8,128)(2,1)}, bf16[256,2304]{1,0:T(8,128)(2,1)}, u32[]{:S(2)}, u32[]{:S(2)}) collective-permute-start(bf16[256,2304]{1,0:T(8,128)(2,1)} %add_convert_fusion.3), channel_id=1, source_target_pairs={{1,2},{2,1},{5,6},{6,5},{9,10},{10,9},{13,14},{14,13},{17,18},{18,... | collective-permute-start | bytes 3538952 | tf_op jit(solution)/shard_map/ppermute | solution.py:105
  708.0 23.7 %collective-permute-start.27 = (bf16[144,2304]{1,0:T(8,128)(2,1)S(1)}, bf16[144,2304]{1,0:T(8,128)(2,1)S(1)}, u32[]{:S(2)}, u32[]{:S(2)}) collective-permute-start(bf16[144,2304]{1,0:T(8,128)(2,1)S(1)} %fusion.85), channel_id=1, source_target_pairs={{0,8},{8,0},{16,24},{24,16},{1,9},{9,1},{17,25},{25,17},{2,10},{10... | collective-permute-start | bytes 1990664 | tf_op jit(solution)/shard_map/ppermute | solution.py:88
  730.0 14.6 %collective-permute-start.24 = (bf16[256,2304]{1,0:T(8,128)(2,1)}, bf16[256,2304]{1,0:T(8,128)(2,1)}, u32[]{:S(2)}, u32[]{:S(2)}) collective-permute-start(bf16[256,2304]{1,0:T(8,128)(2,1)} %add_convert_fusion.1), channel_id=1, source_target_pairs={{1,2},{2,1},{5,6},{6,5},{9,10},{10,9},{13,14},{14,13},{17,18},{18,... | collective-permute-start | bytes 3538952 | tf_op jit(solution)/shard_map/ppermute | solution.py:105
  735.4 115.1 %collective-permute-start.28 = (bf16[4,288,2304]{2,1,0:T(8,128)(2,1)}, bf16[4,288,2304]{2,1,0:T(8,128)(2,1)S(1)}, u32[]{:S(2)}, u32[]{:S(2)}) collective-permute-start(bf16[4,288,2304]{2,1,0:T(8,128)(2,1)} %dynamic-slice_bitcast_fusion.1), channel_id=1, source_target_pairs={{0,4},{4,0},{1,5},{5,1},{2,6},{6,2},{3,7},{7,3},{8,12},{12,8},{9,1... | collective-permute-start | bytes 15925256 | tf_op jit(solution)/shard_map/ppermute | solution.py:74
  737.0 31.4 %collective-permute-start.15 = (bf16[256,2304]{1,0:T(8,128)(2,1)S(1)}, bf16[256,2304]{1,0:T(8,128)(2,1)}, u32[]{:S(2)}, u32[]{:S(2)}) collective-permute-start(bf16[256,2304]{1,0:T(8,128)(2,1)S(1)} %add_convert_fusion.6), channel_id=1, source_target_pairs={{1,0},{2,3},{5,4},{6,7},{9,8},{10,11},{13,12},{14,15},{17,16},{18,... | collective-permute-start | bytes 3538952 | tf_op jit(solution)/shard_map/ppermute | solution.py:107
  740.1 53.5 %collective-permute-start.18 = (bf16[256,2304]{1,0:T(8,128)(2,1)S(1)}, bf16[256,2304]{1,0:T(8,128)(2,1)}, u32[]{:S(2)}, u32[]{:S(2)}) collective-permute-start(bf16[256,2304]{1,0:T(8,128)(2,1)S(1)} %add_convert_fusion.4), channel_id=1, source_target_pairs={{1,0},{2,3},{5,4},{6,7},{9,8},{10,11},{13,12},{14,15},{17,16},{18,... | collective-permute-start | bytes 3538952 | tf_op jit(solution)/shard_map/ppermute | solution.py:107
  743.3 75.6 %collective-permute-start.22 = (bf16[256,2304]{1,0:T(8,128)(2,1)S(1)}, bf16[256,2304]{1,0:T(8,128)(2,1)}, u32[]{:S(2)}, u32[]{:S(2)}) collective-permute-start(bf16[256,2304]{1,0:T(8,128)(2,1)S(1)} %add_convert_fusion.2), channel_id=1, source_target_pairs={{1,0},{2,3},{5,4},{6,7},{9,8},{10,11},{13,12},{14,15},{17,16},{18,... | collective-permute-start | bytes 3538952 | tf_op jit(solution)/shard_map/ppermute | solution.py:107
  747.6 96.4 %collective-permute-start.25 = (bf16[256,2304]{1,0:T(8,128)(2,1)}, bf16[256,2304]{1,0:T(8,128)(2,1)}, u32[]{:S(2)}, u32[]{:S(2)}) collective-permute-start(bf16[256,2304]{1,0:T(8,128)(2,1)} %add_convert_fusion), channel_id=1, source_target_pairs={{1,0},{2,3},{5,4},{6,7},{9,8},{10,11},{13,12},{14,15},{17,16},{18,... | collective-permute-start | bytes 3538952 | tf_op jit(solution)/shard_map/ppermute | solution.py:107
  854.1 16.8 %collective-permute-start.29 = (bf16[144,2304]{1,0:T(8,128)(2,1)S(1)}, bf16[144,2304]{1,0:T(8,128)(2,1)S(1)}, u32[]{:S(2)}, u32[]{:S(2)}) collective-permute-start(bf16[144,2304]{1,0:T(8,128)(2,1)S(1)} %fusion.84), channel_id=1, source_target_pairs={{0,8},{8,0},{16,24},{24,16},{1,9},{9,1},{17,25},{25,17},{2,10},{10... | collective-permute-start | bytes 1990664 | tf_op jit(solution)/shard_map/ppermute | solution.py:88
  855.3 25.4 %collective-permute-start.56 = (f32[4,2304]{1,0:T(4,128)S(1)}, f32[4,2304]{1,0:T(4,128)S(1)}, u32[]{:S(2)}, u32[]{:S(2)}) collective-permute-start(f32[4,2304]{1,0:T(4,128)S(1)} %pad_maximum_fusion.27), channel_id=1, source_target_pairs={{0,4},{4,0},{1,5},{5,1},{2,6},{6,2},{3,7},{7,3},{8,12},{12,8},{9,1... | collective-permute-start | bytes 110600 | tf_op jit(solution)/shard_map/ppermute | solution.py:116
  877.0 28.6 %collective-permute-start.30 = (bf16[4,288,2304]{2,1,0:T(8,128)(2,1)}, bf16[4,288,2304]{2,1,0:T(8,128)(2,1)}, u32[]{:S(2)}, u32[]{:S(2)}) collective-permute-start(bf16[4,288,2304]{2,1,0:T(8,128)(2,1)} %dynamic-slice_bitcast_fusion), channel_id=1, source_target_pairs={{0,4},{4,0},{1,5},{5,1},{2,6},{6,2},{3,7},{7,3},{8,12},{12,8},{9,1... | collective-permute-start | bytes 15925256 | tf_op jit(solution)/shard_map/ppermute | solution.py:74
  884.3 17.8 %collective-permute-start.48 = (bf16[144,2304]{1,0:T(8,128)(2,1)S(1)}, bf16[144,2304]{1,0:T(8,128)(2,1)S(1)}, u32[]{:S(2)}, u32[]{:S(2)}) collective-permute-start(bf16[144,2304]{1,0:T(8,128)(2,1)S(1)} %get-tuple-element.199), channel_id=1, source_target_pairs={{0,16},{8,24},{16,0},{24,8},{1,17},{9,25},{17,1},{25,9},{2,18},{10... | collective-permute-start | bytes 1990664 | tf_op jit(solution)/shard_map/ppermute | solution.py:89
  888.8 21.9 %collective-permute-start.58 = (f32[4,2304]{1,0:T(4,128)S(1)}, f32[4,2304]{1,0:T(4,128)S(1)}, u32[]{:S(2)}, u32[]{:S(2)}) collective-permute-start(f32[4,2304]{1,0:T(4,128)S(1)} %add.805), channel_id=1, source_target_pairs={{0,16},{8,24},{16,0},{24,8},{1,17},{9,25},{17,1},{25,9},{2,18},{10... | collective-permute-start | bytes 110600 | tf_op jit(solution)/shard_map/ppermute | solution.py:116
  891.0 62.2 %collective-permute-start.50 = (bf16[288,2304]{1,0:T(8,128)(2,1)}, bf16[288,2304]{1,0:T(8,128)(2,1)S(1)}, u32[]{:S(2)}, u32[]{:S(2)}) collective-permute-start(bf16[288,2304]{1,0:T(8,128)(2,1)} %pad_maximum_fusion.7), channel_id=1, source_target_pairs={{0,16},{8,24},{16,0},{24,8},{1,17},{9,25},{17,1},{25,9},{2,18},{10... | collective-permute-start | bytes 3981320 | tf_op jit(solution)/shard_map/ppermute | solution.py:92
  904.6 48.7 %collective-permute-start.49 = (bf16[288,2304]{1,0:T(8,128)(2,1)}, bf16[288,2304]{1,0:T(8,128)(2,1)S(1)}, u32[]{:S(2)}, u32[]{:S(2)}) collective-permute-start(bf16[288,2304]{1,0:T(8,128)(2,1)} %pad_maximum_fusion.6), channel_id=1, source_target_pairs={{0,8},{8,0},{16,24},{24,16},{1,9},{9,1},{17,25},{25,17},{2,10},{10... | collective-permute-start | bytes 3981320 | tf_op jit(solution)/shard_map/ppermute | solution.py:93
  906.9 41.9 %collective-permute-start.31 = (bf16[144,2304]{1,0:T(8,128)(2,1)S(1)}, bf16[144,2304]{1,0:T(8,128)(2,1)S(1)}, u32[]{:S(2)}, u32[]{:S(2)}) collective-permute-start(bf16[144,2304]{1,0:T(8,128)(2,1)S(1)} %fusion.83), channel_id=1, source_target_pairs={{0,8},{8,0},{16,24},{24,16},{1,9},{9,1},{17,25},{25,17},{2,10},{10... | collective-permute-start | bytes 1990664 | tf_op jit(solution)/shard_map/ppermute | solution.py:88
  948.8 8.4 collective-permute-start.32
  952.3 17.9 %collective-permute-start.42 = (bf16[144,2304]{1,0:T(8,128)(2,1)}, bf16[144,2304]{1,0:T(8,128)(2,1)S(1)}, u32[]{:S(2)}, u32[]{:S(2)}) collective-permute-start(bf16[144,2304]{1,0:T(8,128)(2,1)} %get-tuple-element.207), channel_id=1, source_target_pairs={{0,16},{8,24},{16,0},{24,8},{1,17},{9,25},{17,1},{25,9},{2,18},{10... | collective-permute-start | bytes 1990664 | tf_op jit(solution)/shard_map/ppermute | solution.py:89
  956.2 126.3 %collective-permute-start.44 = (bf16[288,2304]{1,0:T(8,128)(2,1)S(1)}, bf16[288,2304]{1,0:T(8,128)(2,1)S(1)}, u32[]{:S(2)}, u32[]{:S(2)}) collective-permute-start(bf16[288,2304]{1,0:T(8,128)(2,1)S(1)} %pad_maximum_fusion.3), channel_id=1, source_target_pairs={{0,16},{8,24},{16,0},{24,8},{1,17},{9,25},{17,1},{25,9},{2,18},{10... | collective-permute-start | bytes 3981320 | tf_op jit(solution)/shard_map/ppermute | solution.py:92
  957.3 14.3 %collective-permute-start.33 = (bf16[144,512]{1,0:T(8,128)(2,1)S(1)}, bf16[144,512]{1,0:T(8,128)(2,1)S(1)}, u32[]{:S(2)}, u32[]{:S(2)}) collective-permute-start(bf16[144,512]{1,0:T(8,128)(2,1)S(1)} %fusion.180), channel_id=1, source_target_pairs={{0,8},{8,0},{16,24},{24,16},{1,9},{9,1},{17,25},{25,17},{2,10},{10... | collective-permute-start | bytes 442376 | tf_op jit(solution)/shard_map/ppermute | solution.py:88
  973.4 43.2 %collective-permute-start.34 = (bf16[4,288,1024]{2,1,0:T(8,128)(2,1)S(1)}, bf16[4,288,1024]{2,1,0:T(8,128)(2,1)S(1)}, u32[]{:S(2)}, u32[]{:S(2)}) collective-permute-start(bf16[4,288,1024]{2,1,0:T(8,128)(2,1)S(1)} %dynamic-slice_bitcast_fusion.3), channel_id=1, source_target_pairs={{0,4},{4,0},{1,5},{5,1},{2,6},{6,2},{3,7},{7,3},{8,12},{12,8},{9,1... | collective-permute-start | bytes 7077896 | tf_op jit(solution)/shard_map/ppermute | solution.py:74
  976.9 35.9 %collective-permute-start.45 = (bf16[144,2304]{1,0:T(8,128)(2,1)}, bf16[144,2304]{1,0:T(8,128)(2,1)S(1)}, u32[]{:S(2)}, u32[]{:S(2)}) collective-permute-start(bf16[144,2304]{1,0:T(8,128)(2,1)} %get-tuple-element.203), channel_id=1, source_target_pairs={{0,16},{8,24},{16,0},{24,8},{1,17},{9,25},{17,1},{25,9},{2,18},{10... | collective-permute-start | bytes 1990664 | tf_op jit(solution)/shard_map/ppermute | solution.py:89
  978.0 105.6 %collective-permute-start.43 = (bf16[288,2304]{1,0:T(8,128)(2,1)S(1)}, bf16[288,2304]{1,0:T(8,128)(2,1)S(1)}, u32[]{:S(2)}, u32[]{:S(2)}) collective-permute-start(bf16[288,2304]{1,0:T(8,128)(2,1)S(1)} %pad_maximum_fusion.2), channel_id=1, source_target_pairs={{0,8},{8,0},{16,24},{24,16},{1,9},{9,1},{17,25},{25,17},{2,10},{10... | collective-permute-start | bytes 3981320 | tf_op jit(solution)/shard_map/ppermute | solution.py:93
  979.2 117.4 %collective-permute-start.47 = (bf16[288,2304]{1,0:T(8,128)(2,1)S(1)}, bf16[288,2304]{1,0:T(8,128)(2,1)S(1)}, u32[]{:S(2)}, u32[]{:S(2)}) collective-permute-start(bf16[288,2304]{1,0:T(8,128)(2,1)S(1)} %pad_maximum_fusion.5), channel_id=1, source_target_pairs={{0,16},{8,24},{16,0},{24,8},{1,17},{9,25},{17,1},{25,9},{2,18},{10... | collective-permute-start | bytes 3981320 | tf_op jit(solution)/shard_map/ppermute | solution.py:92
  1015.5 28.9 %collective-permute-start.39 = (bf16[144,512]{1,0:T(8,128)(2,1)S(1)}, bf16[144,512]{1,0:T(8,128)(2,1)S(1)}, u32[]{:S(2)}, u32[]{:S(2)}) collective-permute-start(bf16[144,512]{1,0:T(8,128)(2,1)S(1)} %get-tuple-element.225), channel_id=1, source_target_pairs={{0,16},{8,24},{16,0},{24,8},{1,17},{9,25},{17,1},{25,9},{2,18},{10... | collective-permute-start | bytes 442376 | tf_op jit(solution)/shard_map/ppermute | solution.py:89
  1017.1 33.3 %collective-permute-start.35 = (bf16[144,1024]{1,0:T(8,128)(2,1)S(1)}, bf16[144,1024]{1,0:T(8,128)(2,1)S(1)}, u32[]{:S(2)}, u32[]{:S(2)}) collective-permute-start(bf16[144,1024]{1,0:T(8,128)(2,1)S(1)} %get-tuple-element.215), channel_id=1, source_target_pairs={{0,16},{8,24},{16,0},{24,8},{1,17},{9,25},{17,1},{25,9},{2,18},{10... | collective-permute-start | bytes 884744 | tf_op jit(solution)/shard_map/ppermute | solution.py:89
  1044.4 52.2 %collective-permute-start.46 = (bf16[288,2304]{1,0:T(8,128)(2,1)S(1)}, bf16[288,2304]{1,0:T(8,128)(2,1)S(1)}, u32[]{:S(2)}, u32[]{:S(2)}) collective-permute-start(bf16[288,2304]{1,0:T(8,128)(2,1)S(1)} %pad_maximum_fusion.4), channel_id=1, source_target_pairs={{0,8},{8,0},{16,24},{24,16},{1,9},{9,1},{17,25},{25,17},{2,10},{10... | collective-permute-start | bytes 3981320 | tf_op jit(solution)/shard_map/ppermute | solution.py:93
  1050.3 30.7 %collective-permute-start.37 = (bf16[144,1024]{1,0:T(8,128)(2,1)S(1)}, bf16[144,1024]{1,0:T(8,128)(2,1)S(1)}, u32[]{:S(2)}, u32[]{:S(2)}) collective-permute-start(bf16[144,1024]{1,0:T(8,128)(2,1)S(1)} %get-tuple-element.214), channel_id=1, source_target_pairs={{0,8},{8,0},{16,24},{24,16},{1,9},{9,1},{17,25},{25,17},{2,10},{10... | collective-permute-start | bytes 884744 | tf_op jit(solution)/shard_map/ppermute | solution.py:88
  1081.1 9.9 collective-permute-start.41
  1082.5 12.2 %collective-permute-start.40 = (bf16[288,512]{1,0:T(8,128)(2,1)S(1)}, bf16[288,512]{1,0:T(8,128)(2,1)S(1)}, u32[]{:S(2)}, u32[]{:S(2)}) collective-permute-start(bf16[288,512]{1,0:T(8,128)(2,1)S(1)} %pad_maximum_fusion.21), channel_id=1, source_target_pairs={{0,8},{8,0},{16,24},{24,16},{1,9},{9,1},{17,25},{25,17},{2,10},{10... | collective-permute-start | bytes 884744 | tf_op jit(solution)/shard_map/ppermute | solution.py:93
  1083.6 17.4 %collective-permute-start.38 = (bf16[288,1024]{1,0:T(8,128)(2,1)S(1)}, bf16[288,1024]{1,0:T(8,128)(2,1)S(1)}, u32[]{:S(2)}, u32[]{:S(2)}) collective-permute-start(bf16[288,1024]{1,0:T(8,128)(2,1)S(1)} %pad_maximum_fusion.10), channel_id=1, source_target_pairs={{0,16},{8,24},{16,0},{24,8},{1,17},{9,25},{17,1},{25,9},{2,18},{10... | collective-permute-start | bytes 1769480 | tf_op jit(solution)/shard_map/ppermute | solution.py:92
  1091.0 11.2 collective-permute-start.36
  (141 other events, 2571.5 us)

commit v3 on v2

--- a/solution.py
+++ b/solution.py
@@ -206,7 +206,7 @@
     heads_ref, scale_ref, x_hbm, cot_hbm, w_out_hbm, own_hbm,
     out_hbm, ffn_in_hbm, hidden_hbm, d_ffn_hbm, d_gate_hbm, d_up_hbm, d_attn_hbm, d_heads_hbm,
     d_mid_hbm, gain_ref, attn_hbm, slope_hbm, value_hbm,
-    weights, w_out, send, near, across, total, xb, cb, ab, act, stage, d_mid, d_heads,
+    weights, w_out, send, near, across, total, xb, cb, ab, act, act_t, stage, d_heads,
     line_send, line_recv, credit, local, ag_send, ag_recv, ag_local,
 ):
     dp, core, z = lax.axis_index("dp"), lax.axis_index("ctx"), lax.axis_index("mp")
@@ -334,6 +334,14 @@
     def store(src, ref, u, sem):
         return pltpu.make_async_copy(src, ref.at[rows_of(u)], local.at[sem])
 
+    def store_t(ref, u, sem):
+        return pltpu.make_async_copy(act_t, ref.at[:, rows_of(u)], local.at[sem])
+
+    def turn():
+        @pl.loop(0, width // TILE)
+        def _(n):
+            act_t[tile(n)] = act[:, tile(n)].T
+
     def tile(n):
         return pl.ds(pl.multiple_of(n * TILE, TILE), TILE)
 
@@ -370,7 +378,8 @@
             act[rows] = (mid * inverse_rms(mid) * scale(2)).astype(BF)
 
         each_rows(body)
-        store(act, ffn_in_hbm, u, 2).start()
+        turn()
+        store_t(ffn_in_hbm, u, 2).start()
 
         @pl.loop(0, units // TILE)
         def _(f):
@@ -393,7 +402,7 @@
         for i, ref in saves:
             store(stage.at[i], ref, u, 3 + i).wait()
         store(total.at[u], attn_hbm, u, 1).wait()
-        store(act, ffn_in_hbm, u, 2).wait()
+        store_t(ffn_in_hbm, u, 2).wait()
 
     def backward(u, k):
         loads = (
@@ -418,7 +427,8 @@
 
         each_rows(body)
         store(xb, out_hbm, u, 0).start()
-        store(act, d_ffn_hbm, u, 1).start()
+        turn()
+        store_t(d_ffn_hbm, u, 1).start()
 
         @pl.loop(0, units // TILE)
         def _(f):
@@ -436,7 +446,7 @@
             dst[:, tile(n)] = part.astype(BF)
 
         store(xb, out_hbm, u, 0).wait()
-        store(act, d_ffn_hbm, u, 1).wait()
+        store_t(d_ffn_hbm, u, 1).wait()
         store(stage.at[1], d_gate_hbm, u, 4).wait()
         store(stage.at[2], d_up_hbm, u, 5).wait()
 
@@ -455,21 +465,22 @@
             mean = jnp.mean(scaled * mid, axis=-1, keepdims=True)
             grad = cb[rows].astype(F32) + r * scaled - mid * (r * r * r) * mean
             add_gain(1, mid * r * dy)
-            d_mid[rows] = grad
+            cb[rows] = grad.astype(BF)
             scaled = scale(1) * grad
             mean = jnp.mean(scaled * attn, axis=-1, keepdims=True)
             act[rows] = (r_two * scaled - attn * (r_two * r_two * r_two) * mean).astype(BF)
             add_gain(0, attn * r_two * grad)
 
         each_rows(body)
-        store(d_mid, d_mid_hbm, u, 0).start()
-        store(act, d_attn_hbm, u, 1).start()
+        store(cb, d_mid_hbm, u, 0).start()
+        turn()
+        store_t(d_attn_hbm, u, 1).start()
         for h in range(w_out.shape[1] // TILE):
             columns = slice(h * TILE, (h + 1) * TILE)
             d_heads[:, columns] = dot(act[...], w_out[:, columns]).astype(BF)
         store(d_heads, d_heads_hbm, u, 2).start()
-        store(d_mid, d_mid_hbm, u, 0).wait()
-        store(act, d_attn_hbm, u, 1).wait()
+        store(cb, d_mid_hbm, u, 0).wait()
+        store_t(d_attn_hbm, u, 1).wait()
         store(d_heads, d_heads_hbm, u, 2).wait()
 
     gather_first(0)
@@ -517,10 +528,11 @@
     assert tokens == 4 * UNIT
     full = jax.ShapeDtypeStruct((tokens, width), BF)
     wide = jax.ShapeDtypeStruct((tokens, units), BF)
+    flipped = jax.ShapeDtypeStruct((width, tokens), BF)
     outs = (
-        full, full, wide, full, wide, wide, full,
+        full, flipped, wide, flipped, wide, wide, flipped,
         jax.ShapeDtypeStruct((tokens, w_out.shape[1]), BF),
-        jax.ShapeDtypeStruct((tokens, width), F32),
+        full,
         jax.ShapeDtypeStruct((3, 8, width), F32),
         full, wide, wide,
     )
@@ -542,8 +554,8 @@
             pltpu.VMEM((UNIT, width), BF),
             pltpu.VMEM((UNIT, width), BF),
             pltpu.VMEM((UNIT, width), BF),
+            pltpu.VMEM((width, UNIT), BF),
             pltpu.VMEM((3, UNIT, units), BF),
-            pltpu.VMEM((UNIT, width), F32),
             pltpu.VMEM((UNIT, w_out.shape[1]), BF),
             dma((3, 4)),
             dma((3, 4)),
@@ -560,6 +572,403 @@
     )(heads_out, scales, x, cot, w_out, own)
 
 
+def grad_kernel(
+    seg_row, seg_col, cosine, sine, scale_ref, x_hbm, d_mid_hbm, q_hbm, k_hbm, v_hbm, d_heads_hbm, w_qkv_hbm,
+    d_ffn_t, hidden_hbm, ffn_in_t, d_gate_hbm, d_up_hbm, d_attn_t, heads_hbm, attn_in_t,
+    in_grad_hbm, own_hbm, by_x_hbm, by_y_hbm, gain_ref, core_hbm, far_hbm,
+    w_qkv, left, right, core_out, sums, arrived, own_sum,
+    queries, keys, values, d_out, d_proj, d_keys, d_values, kv_out, kv_in,
+    send, near, across, total, xb, mb_buf,
+    line_send, line_recv, kv_sem, local, load_sem, rs_send, rs_recv, rs_local, own_sem,
+):
+    dp, core, z = lax.axis_index("dp"), lax.axis_index("ctx"), lax.axis_index("mp")
+    width = xb.shape[1]
+    rows_own = own_hbm.shape[1]
+    half = rows_own // 2
+    tokens = 2 * UNIT
+    inner = (z == 1) | (z == 2)
+    outer = (z == 0) | (z == 3)
+    x_peer, y_peer = (dp ^ 1, core, z), (dp ^ 2, core, z)
+    core_peer = (dp, 1 - core, z)
+    near_peer = (dp, core, z ^ 1)
+    far_peer = (dp, core, 3 - z)
+
+    barrier = pltpu.get_barrier_semaphore()
+    for peer in (x_peer, y_peer, core_peer, near_peer, far_peer):
+        pl.semaphore_signal(barrier, inc=1, device_id=peer, device_id_type=MESH)
+
+    def tile(n):
+        return pl.ds(pl.multiple_of(n * TILE, TILE), TILE)
+
+    def remote(src, dst, sems, index, peer):
+        return pltpu.make_async_remote_copy(
+            src_ref=src, dst_ref=dst, send_sem=sems[0].at[index], recv_sem=sems[1].at[index],
+            device_id=peer, device_id_type=MESH,
+        )
+
+    jobs = (
+        (d_ffn_t, hidden_hbm), (ffn_in_t, d_gate_hbm), (ffn_in_t, d_up_hbm),
+        (d_attn_t, heads_hbm), (attn_in_t, None),
+    )
+
+    def columns(i):
+        return (w_qkv.shape[1] if i == 4 else jobs[i][1].shape[1])
+
+    def operands(i):
+        pair = []
+        if i != 2:
+            pair.append(pltpu.make_async_copy(jobs[i][0], left, rs_local.at[0]))
+        if i != 4:
+            pair.append(pltpu.make_async_copy(jobs[i][1], right.at[:, : columns(i)], rs_local.at[1]))
+        return pair
+
+    def core_copy(i, m):
+        n = columns(i)
+        return remote(
+            core_out.at[m % 2, :, :n], core_hbm.at[i, m, :, :n], (rs_send, rs_recv), (i, m), core_peer
+        )
+
+    def arrive(i, m):
+        n = columns(i)
+        return pltpu.make_async_copy(core_hbm.at[i, m, :, :n], arrived.at[m % 2, :, :n], rs_local.at[2 + m % 2])
+
+    def far_copy(i, way):
+        n = columns(i)
+        rows = slice(0, half) if way == 0 else slice(half, rows_own)
+        return remote(
+            sums.at[i % 2, 2, rows, :n], far_hbm.at[i, rows, :n], (rs_send, rs_recv), (i, 4 + way),
+            (x_peer, y_peer)[way],
+        )
+
+    def final_copy(i, way):
+        n = columns(i)
+        dst = (by_x_hbm, by_y_hbm)[way]
+        return remote(
+            sums.at[i % 2, way, :, :n], dst.at[i, :, :n], (rs_send, rs_recv), (i, 6 + way),
+            (x_peer, y_peer)[way],
+        )
+
+    def own_store(i):
+        n = columns(i)
+        return pltpu.make_async_copy(own_sum.at[:, :n], own_hbm.at[i, :, :n], own_sem.at[0])
+
+    def block_rows(mask, other):
+        owner = (dp ^ mask) * 2 + ((1 - core) if other else core)
+        return pl.ds(pl.multiple_of(owner * rows_own, 16), rows_own)
+
+    def scatter_start(i):
+        for copy in operands(i):
+            copy.wait()
+        source = d_proj if i == 4 else right
+        steps = columns(i) // TILE
+
+        for m in (3, 2, 1, 0):
+            if m < 2:
+                core_copy(i, m + 2).wait_send()
+            elif i > 0:
+                core_copy(i - 1, m - 2).wait_send()
+
+            @pl.loop(0, steps)
+            def _(n):
+                core_out[m % 2, :, tile(n)] = dot(left[block_rows(m, True)], source[:, tile(n)]).astype(BF)
+
+            core_copy(i, m).start()
+        if i > 1:
+            for way in (0, 1):
+                far_copy(i - 2, way).wait_send()
+                final_copy(i - 2, way).wait_send()
+        if i > 0:
+            own_store(i - 1).wait()
+        core_copy(i, 3).wait_recv()
+        arrive(i, 3).start()
+        for m in (3, 2, 1, 0):
+            if m:
+                core_copy(i, m - 1).wait_recv()
+                arrive(i, m - 1).start()
+            arrive(i, m).wait()
+
+            @pl.loop(0, steps)
+            def _(n):
+                part = dot(left[block_rows(m, False)], source[:, tile(n)])
+                part = part + arrived[m % 2, :, tile(n)].astype(F32)
+                if m:
+                    sums[i % 2, m - 1, :, tile(n)] = part.astype(BF)
+                else:
+                    own_sum[:, tile(n)] = part
+
+            if m == 3:
+                far_copy(i, 0).start()
+                far_copy(i, 1).start()
+        own_store(i).start()
+        if i + 1 < len(jobs):
+            for copy in operands(i + 1):
+                copy.start()
+
+    def scatter_end(i):
+        n = columns(i)
+        for way in (0, 1):
+            far_copy(i, way).wait_recv()
+        copy = pltpu.make_async_copy(far_hbm.at[i, :, :n], arrived.at[0, :, :n], rs_local.at[4])
+        copy.start()
+        copy.wait()
+        for way in (1, 0):
+            base = 0 if way == 1 else half
+
+            @pl.loop(0, half // 16)
+            def _(r):
+                rows = pl.ds(pl.multiple_of(base + r * 16, 16), 16)
+                total_rows = sums[i % 2, way, rows, :n].astype(F32) + arrived[0, rows, :n].astype(F32)
+                sums[i % 2, way, rows, :n] = total_rows.astype(BF)
+
+            final_copy(i, way).start()
+
+    def hop(kind, i):
+        src = (send.at[i % 3], send.at[i % 3], total.at[i])[kind]
+        dst = (near.at[i % 3], across.at[i], total.at[i])[kind]
+        peer = far_peer if kind == 1 else near_peer
+        return remote(src, dst, (line_send, line_recv), (kind, i), peer)
+
+    def add_rows(dst, a, b):
+        @pl.loop(0, UNIT // 16)
+        def _(r):
+            rows = pl.ds(pl.multiple_of(r * 16, 16), 16)
+            dst[rows] = (a[rows].astype(F32) + b[rows].astype(F32)).astype(BF)
+
+    def boundary(k):
+        @pl.when(outer)
+        def _():
+            if 0 <= k - 3 < 4:
+                hop(2, k - 3).wait_recv()
+            if 0 <= k - 1 < 4:
+                hop(0, k - 1).wait_send()
+            if k < 4:
+                hop(0, k).start()
+
+        @pl.when(inner)
+        def _():
+            if 0 <= k - 1 < 4:
+                i = k - 1
+                hop(0, i).wait_recv()
+                add_rows(send.at[i % 3], send.at[i % 3], near.at[i % 3])
+                hop(1, i).start()
+            if 0 <= k - 2 < 4:
+                i = k - 2
+                hop(1, i).wait_recv()
+                hop(1, i).wait_send()
+                add_rows(total.at[i], send.at[i % 3], across.at[i])
+                hop(2, i).start()
+            if 0 <= k - 3 < 4:
+                hop(2, k - 3).wait_send()
+
+    def attention_loads(mb):
+        head_rows = [
+            pltpu.make_async_copy(
+                d_heads_hbm.at[pl.ds(mb * tokens, tokens), pl.ds(h * HEAD, HEAD)], d_out.at[h], load_sem.at[3 + h]
+            )
+            for h in range(2)
+        ]
+        return head_rows + [
+            pltpu.make_async_copy(ref.at[mb], dst, load_sem.at[j])
+            for j, (ref, dst) in enumerate(((q_hbm, queries), (k_hbm, keys), (v_hbm, values)))
+        ]
+
+    def unrotate(v, rows):
+        a, b = v[:, : HEAD // 2], v[:, HEAD // 2 :]
+        c, s = cosine[rows], sine[rows]
+        return jnp.concatenate([a * c + b * s, b * c - a * s], axis=1)
+
+    def kv_copy(mb):
+        return remote(kv_out, kv_in.at[mb], (kv_sem.at[0], kv_sem.at[1]), (mb,), core_peer)
+
+    def attention_back(mb):
+        for copy in attention_loads(mb):
+            copy.wait()
+        d_keys[...] = jnp.zeros_like(d_keys)
+        d_values[...] = jnp.zeros_like(d_values)
+        length = keys.shape[0]
+        for h in range(2):
+
+            @pl.loop(0, tokens // UNIT)
+            def _(b):
+                rows = pl.ds(pl.multiple_of(b * UNIT, UNIT), UNIT)
+                query, grad = queries[h, rows], d_out[h, rows]
+                first = core * tokens + b * UNIT
+                key_at = lax.broadcasted_iota(jnp.int32, (length, UNIT), 0)
+                query_at = lax.broadcasted_iota(jnp.int32, (length, UNIT), 1) + first
+                same = seg_col[mb] == seg_row[mb, :, rows]
+                tanh = jnp.tanh(dot_t(keys[...], query) * (SCALE / CAP))
+                weight = jnp.where((key_at <= query_at) & same, jnp.exp(CAP * tanh), 0.0)
+                probs = weight * (1.0 / jnp.sum(weight, axis=0, keepdims=True))
+                d_probs = dot_t(values[...], grad)
+                mean = jnp.sum(probs * d_probs, axis=0, keepdims=True)
+                d_raw = (probs * (d_probs - mean) * (1.0 - tanh * tanh)).astype(BF)
+                d_values[...] += dot(probs.astype(BF), grad)
+                d_keys[...] += dot(d_raw, query)
+                d_query = t_dot(d_raw, keys[...]) * SCALE
+                place = pl.ds(pl.multiple_of(mb * tokens + b * UNIT, UNIT), UNIT)
+                d_proj[place, h * HEAD : (h + 1) * HEAD] = unrotate(d_query, place).astype(BF)
+
+        theirs = pl.ds(pl.multiple_of((1 - core) * tokens, UNIT), tokens)
+        mine = pl.ds(pl.multiple_of(core * tokens, UNIT), tokens)
+        if mb:
+            kv_copy(mb - 1).wait_send()
+        kv_out[:, :HEAD] = (d_keys[theirs] * SCALE).astype(BF)
+        kv_out[:, HEAD:] = d_values[theirs].astype(BF)
+        kv_copy(mb).start()
+        kv_copy(mb).wait_recv()
+        place = pl.ds(mb * tokens, tokens)
+        d_key = d_keys[mine] * SCALE + kv_in[mb, :, :HEAD].astype(F32)
+        d_value = d_values[mine] + kv_in[mb, :, HEAD:].astype(F32)
+        d_proj[place, 2 * HEAD : 3 * HEAD] = unrotate(d_key, place).astype(BF)
+        d_proj[place, 3 * HEAD :] = d_value.astype(BF)
+
+    def project(u):
+        @pl.loop(0, width // TILE)
+        def _(n):
+            send[u % 3, :, tile(n)] = dot_t(d_proj[u * UNIT : (u + 1) * UNIT], w_qkv[tile(n)]).astype(BF)
+
+    def last_loads(u):
+        rows = pl.ds(u * UNIT, UNIT)
+        return (
+            pltpu.make_async_copy(x_hbm.at[rows], xb, local.at[0]),
+            pltpu.make_async_copy(d_mid_hbm.at[rows], mb_buf, local.at[1]),
+        )
+
+    def last(u):
+        for copy in last_loads(u):
+            copy.wait()
+
+        @pl.loop(0, UNIT // 16)
+        def _(r):
+            rows = pl.ds(pl.multiple_of(r * 16, 16), 16)
+            x = xb[rows].astype(F32)
+            r_one = inverse_rms(x)
+            dy = total[u, rows].astype(F32)
+            scaled = scale_ref[0:1] * dy
+            mean = jnp.mean(scaled * x, axis=-1, keepdims=True)
+            back = r_one * scaled - x * (r_one * r_one * r_one) * mean
+            mb_buf[rows] = (mb_buf[rows].astype(F32) + back).astype(BF)
+            part = x * r_one * dy
+            gain_ref[...] += part[:8] + part[8:]
+
+        store = pltpu.make_async_copy(mb_buf, in_grad_hbm.at[pl.ds(u * UNIT, UNIT)], local.at[2])
+        store.start()
+        store.wait()
+        if u < 3:
+            for copy in last_loads(u + 1):
+                copy.start()
+
+    qkv_copy = pltpu.make_async_copy(w_qkv_hbm, w_qkv, local.at[2])
+    for copy in (*attention_loads(0), qkv_copy, *operands(0), *last_loads(0)):
+        copy.start()
+    gain_ref[...] = jnp.zeros_like(gain_ref)
+    pl.semaphore_wait(barrier, 5)
+    attention_back(0)
+    for copy in attention_loads(1):
+        copy.start()
+    qkv_copy.wait()
+    project(0)
+    boundary(0)
+    scatter_start(0)
+    project(1)
+    boundary(1)
+    attention_back(1)
+    scatter_end(0)
+    project(2)
+    boundary(2)
+    project(3)
+    scatter_start(1)
+    boundary(3)
+    scatter_end(1)
+    last(0)
+    scatter_start(2)
+    boundary(4)
+    last(1)
+    scatter_end(2)
+    scatter_start(4 - 1)
+    boundary(5)
+    last(2)
+    scatter_end(3)
+    scatter_start(4)
+    boundary(6)
+    last(3)
+    scatter_end(4)
+    kv_copy(1).wait_send()
+    own_store(4).wait()
+    for m in range(2):
+        core_copy(4, m).wait_send()
+    for i in range(5):
+        for way in (0, 1):
+            if i > 2:
+                far_copy(i, way).wait_send()
+                final_copy(i, way).wait_send()
+            final_copy(i, way).wait_recv()
+
+
+def grad_call(seg_row, seg_col, cosine, sine, scales, arrays):
+    x, w_qkv = arrays[0], arrays[6]
+    tokens, width = x.shape
+    rows = width // 8
+    wide = arrays[8].shape[1]
+    full = jax.ShapeDtypeStruct((tokens, width), BF)
+    part = jax.ShapeDtypeStruct((5, rows, wide), BF)
+    outs = (
+        full,
+        jax.ShapeDtypeStruct((5, rows, wide), F32),
+        part,
+        part,
+        jax.ShapeDtypeStruct((8, width), F32),
+        jax.ShapeDtypeStruct((5, 4, rows, wide), BF),
+        part,
+    )
+    anywhere, vmem = pl.BlockSpec(memory_space=pl.ANY), pl.BlockSpec(memory_space=pltpu.VMEM)
+    dma = pltpu.SemaphoreType.DMA
+    half, length = tokens // 2, tokens
+    return pl.pallas_call(
+        grad_kernel,
+        out_shape=outs,
+        in_specs=[vmem] * 5 + [anywhere] * 15,
+        out_specs=[anywhere] * 4 + [vmem] + [anywhere] * 2,
+        scratch_shapes=[
+            pltpu.VMEM(w_qkv.shape, BF),
+            pltpu.VMEM((width, tokens), BF),
+            pltpu.VMEM((tokens, wide), BF),
+            pltpu.VMEM((2, rows, wide), BF),
+            pltpu.VMEM((2, 3, rows, wide), BF),
+            pltpu.VMEM((2, rows, wide), BF),
+            pltpu.VMEM((rows, wide), F32),
+            pltpu.VMEM((2, half, HEAD), BF),
+            pltpu.VMEM((length, HEAD), BF),
+            pltpu.VMEM((length, HEAD), BF),
+            pltpu.VMEM((2, half, HEAD), BF),
+            pltpu.VMEM((tokens, 4 * HEAD), BF),
+            pltpu.VMEM((length, HEAD), F32),
+            pltpu.VMEM((length, HEAD), F32),
+            pltpu.VMEM((half, 2 * HEAD), BF),
+            pltpu.VMEM((2, half, 2 * HEAD), BF),
+            pltpu.VMEM((3, UNIT, width), BF),
+            pltpu.VMEM((3, UNIT, width), BF),
+            pltpu.VMEM((4, UNIT, width), BF),
+            pltpu.VMEM((4, UNIT, width), BF),
+            pltpu.VMEM((UNIT, width), BF),
+            pltpu.VMEM((UNIT, width), BF),
+            dma((3, 4)),
+            dma((3, 4)),
+            dma((2, 2)),
+            dma((3,)),
+            dma((5,)),
+            dma((5, 8)),
+            dma((5, 8)),
+            dma((5,)),
+            dma((1,)),
+        ],
+        compiler_params=pltpu.CompilerParams(
+            collective_id=2, has_side_effects=True, vmem_limit_bytes=63 * 10**6
+        ),
+        name="grads",
+    )(seg_row, seg_col, cosine, sine, scales, *arrays)
+
+
 def fast_device(
     sizes,
     inputs,
@@ -574,9 +983,8 @@
     full_len = segment_ids.shape[2]
     q_cols, k_cols = masters[0].shape[1], masters[1].shape[1]
     heads = q_cols // HEAD
+    width_ff = masters[4].shape[1]
     assert k_cols == HEAD
-    cuts = 2 if tokens >= 512 else 1
-    unit = tokens // cuts
 
     low = [w.astype(BF) for w in masters[:7]]
     qkv_own = jnp.concatenate(low[:3], axis=1)
@@ -625,52 +1033,34 @@
         heads_all, (1.0 + gains).T, inputs.reshape(flat), cotangent.reshape(flat), w_out,
         jnp.stack(low[4:]),
     )
-    output, ffn_in, hidden, d_ffn, d_gate, d_up, d_attn, d_heads_all, d_mid, gain_parts = outs[:10]
-    units = [(mb, cut) for mb in range(batches) for cut in range(cuts)]
-    work = []
-    for i, (mb, cut) in enumerate(units):
-        work.append(dict(rows=slice(cut * unit, (cut + 1) * unit), mb=mb, all=slice(i * unit, (i + 1) * unit)))
-
-    g_down = t_dot(d_ffn, hidden)
-    g_gate = t_dot(ffn_in, d_gate)
-    g_up = t_dot(ffn_in, d_up)
-    s_down, mark = scatter_rows(g_down, sizes, None)
-    s_gate, mark = scatter_rows(g_gate, sizes, mark)
-    s_up, mark = scatter_rows(g_up, sizes, mark)
-
-    for mb in range(batches):
-        s = state[mb]
-        d_heads = d_heads_all[mb * tokens : (mb + 1) * tokens]
-        d_out = jnp.concatenate(jnp.split(d_heads, heads, axis=1))
-        d_queries, d_keys, d_values = attend_back(
-            s["saved"], s["queries"], s["keys"], s["values"], d_out
-        )
-        d_kv = scatter_ctx(jnp.concatenate([d_keys, d_values], axis=1), sizes)
-        pieces = [rotate(q, s["cosine"], -s["sine"]) for q in jnp.split(d_queries, heads)]
-        pieces += [rotate(d_kv[:, :HEAD], s["cosine"], -s["sine"]), d_kv[:, HEAD:]]
-        s["d_proj"] = jnp.concatenate(pieces, axis=1).astype(BF)
-    for w in work:
-        part = dot_t(state[w["mb"]]["d_proj"][w["rows"]], w_qkv).astype(BF)
-        w["d_attn_in"] = sum_mp(part, sizes)
-
-    g_out = t_dot(d_attn, heads_all)
-    g_qkv = t_dot(
-        jnp.concatenate([s["attn_in"] for s in state]),
-        jnp.concatenate([s["d_proj"] for s in state]),
-    )
-    s_out, mark = scatter_rows(g_out, sizes, mark)
-    s_qkv, mark = scatter_rows(g_qkv, sizes, mark)
-
-    for w in work:
-        s = state[w["mb"]]
-        back, w["g_one"] = norm_back(
-            s["x"][w["rows"]], s["r_one"][w["rows"]], gain_one, w["d_attn_in"].astype(F32)
-        )
-        w["input_grad"] = (d_mid[w["all"]] + back).astype(BF)
-
-    gain_grads = jnp.concatenate(
-        [sum(w["g_one"] for w in work)[None], jnp.sum(gain_parts, axis=1)]
-    )
+    output, ffn_in_t, hidden, d_ffn_t, d_gate, d_up, d_attn_t, d_heads, d_mid, gain_parts = outs[:10]
+
+    def batch(key):
+        return jnp.stack([s[key] for s in state])
+
+    def tokens_of(key):
+        return jnp.concatenate([s[key] for s in state])
+
+    seg_all = segment_ids[:, 0]
+    seg_row = lax.dynamic_slice_in_dim(seg_all, start, tokens, 1)[:, None]
+    outs = grad_call(
+        seg_row, seg_all[:, :, None], tokens_of("cosine"), tokens_of("sine"), (1.0 + gains).T,
+        (
+            inputs.reshape(flat), d_mid, batch("queries").reshape(batches, heads, tokens, HEAD),
+            batch("keys"), batch("values"), d_heads, w_qkv, d_ffn_t, hidden, ffn_in_t, d_gate, d_up,
+            d_attn_t, heads_all, tokens_of("attn_in").T,
+        ),
+    )
+    input_grad, own_sum, by_x, by_y, gain_part = outs[:5]
+
+    def final_sum(i, cols):
+        picked = [v[i, :, :cols].astype(F32) for v in (own_sum, by_x, by_y)]
+        return picked[0] + picked[1] + picked[2]
+
+    qkv_cols = w_qkv.shape[1]
+    s_down, s_gate, s_up = [final_sum(i, width_ff) for i in range(3)]
+    s_out, s_qkv = final_sum(3, q_cols), final_sum(4, qkv_cols)
+    gain_grads = jnp.concatenate([jnp.sum(gain_part, axis=0)[None], jnp.sum(gain_parts, axis=1)])
     gain_grads = sum_small(gain_grads, ("ctx", "dp"), sizes)
     summed = (
         s_qkv[:, :q_cols], s_qkv[:, q_cols : q_cols + k_cols], s_qkv[:, q_cols + k_cols :],
@@ -689,7 +1079,7 @@
 
     return (
         output.reshape(inputs.shape),
-        jnp.concatenate([w["input_grad"] for w in work]).reshape(inputs.shape), norm_value.reshape(1), *changes, *new_moments
+        input_grad.reshape(inputs.shape), norm_value.reshape(1), *changes, *new_moments
     )
 
 

time: 1160 us -> 845 us (0.73)
  waiting for transfers between devices: 356 us -> 13.1 us
  Pallas kernels: 432 us -> 655 us
  matrix products: 90.1 us -> 9.93 us
  other arithmetic: 156 us -> 76.6 us
  starting transfers between devices: 63.2 us -> 28.4 us
    ppermute x39 -> x0, waiting for transfers between devices: 339 us -> none  [the longest x5 85.5 us: scatter_rows(): far_low = lax.ppermute(part(3, half, rows).astype(BF), **flip('dp', dp, 2))]
    pallas_call x0 -> x1, Pallas kernels: none -> 222 us  [grad_call(): pl.pallas_call(grad_kernel, out_shape=outs, in_specs=[vmem] * 5 + [anywhe...]
    dot_general x9 -> x0, matrix products: 62.8 us -> none  [t_dot(): lax.dot_general(a, b, (((0,), (0,)), ((), ())), preferred_element_type=F32)]
    ppermute x39 -> x0, starting transfers between devices: 40.1 us -> none  [the longest x4 6.91 us: sum_mp(): across = lax.ppermute(pair, 'mp', [(1, 2), (2, 1)])]
    convert_element_type x19 -> x0, other arithmetic: 32.4 us -> none  [the longest x4 8.05 us: sum_mp(): total = (pair.astype(F32) + across.astype(F32)).astype(BF)]
    unnamed x25 -> x4, other arithmetic: 18.1 us -> 1.36 us
    dot_general x8 -> x2, matrix products: 16.8 us -> 2.93 us  [dot_t(): lax.dot_general(a, b, (((1,), (1,)), ((), ())), preferred_element_type=F32)]
    another operation x12 -> x7, other arithmetic: 19.1 us -> 5.46 us
  transfers between devices with their start and end apart: 59 -> 20, of which waited for: 28 -> 8; matrix products, arithmetic and copies ran while one was open for 18% -> 7% of each run, Pallas kernels for 0% -> 0%
where the time goes in v3:
time: 845 us; the launch traced here: 834 us
  Pallas kernels  655 us (78%)
  other arithmetic  76.6 us (9%)
  local copies, waits for them, and re-layouts  31.9 us (4%)
  starting transfers between devices  28.4 us (3%)
  waiting for transfers between devices  13.1 us (2%)
  between operations  10.2 us (1%)
  matrix products  9.93 us (1%)
    pallas_call x1, Pallas kernels, ffn_call(): pl.pallas_call(ffn_kernel, out_shape=outs, in_specs=[vmem, vmem, anywhere...  434 us
    pallas_call x1, Pallas kernels, grad_call(): pl.pallas_call(grad_kernel, out_shape=outs, in_specs=[vmem] * 5 + [anywhe...  222 us
    mul x4, other arithmetic, fast_device(): -RATE * (m + 0.01 * w)  22.2 us
  transfers between devices with their start and end apart: 20, of which 8 were waited for; matrix products, arithmetic and copies ran while one was open for 7% of the time, Pallas kernels for 0%

profile of v3, /device:TPU:0, one launch (start us, length us, event | category | flops | bytes accessed | tf_op | source)
XLA Modules:
  0.0 833.9 jit_solution(5663160740010096881)
XLA Ops:
  5.0 2.9 collective-permute-start
  7.9 1.5 collective-permute-start.1
  15.6 1.3 slice_convert_fusion.3
  17.6 8.4 %all-gather = bf16[8,288,4]{1,2,0:T(4,128)(2,1)S(1)} all-gather(bf16[1,288,4]{1,2,0:T(4,128)(2,1)S(1)} %maximum_bitcast_fusion.1), channel_id=1, replica_groups=mesh['dp'=4,'ctx'=2,'mp'=4] {'dp','ctx'}, dimensions={0}, use_global_device_ids=true | all-gather | bytes 20736 | tf_op jit(solution)/shard_map/all_gather | solution.py:992
  26.6 1.5 reshape.240
  29.6 2.2 broadcast_in_dim_squeeze.6.seg_col
  31.8 1.2 convert_bitcast_fusion.4
  33.0 2.5 fusion.100
  35.5 2.8 copy.97
  38.9 4.3 copy.98
  43.2 2.3 fusion.9
  45.9 1.3 copy-done.3
  47.3 2.1 convert_bitcast_fusion.2
  49.4 2.2 pad_maximum_fusion.own_hbm
  52.2 1.5 fusion.6
  55.4 1.7 collective-permute-start.8
  57.1 1.5 collective-permute-start.7
  63.9 1.3 collective-permute-done.8
  65.2 1.7 collective-permute-start.9
  67.0 1.6 collective-permute-start.10
  68.6 4.7 collective-permute-done.2
  73.5 2.0 collective-permute-done.9
  75.7 2.8 maximum_bitcast_fusion.attn_in_t
  80.2 2.7 fusion.18
  83.0 2.7 fusion.15
  85.8 2.5 fusion.65
  88.3 2.6 fusion.70
  94.3 1.5 fusion.105
  96.9 1.5 fusion.104
  100.3 433.6 %ffn.1 = (bf16[1024,2304]{1,0:T(8,128)(2,1)}, bf16[2304,1024]{1,0:T(8,128)(2,1)}, bf16[1024,2304]{1,0:T(8,128)(2,1)}, bf16[2304,1024]{1,0:T(8,128)(2,1)}, bf16[1...) custom-call(bf16[1024,512]{1,0:T(8,128)(2,1)} %maximum_maximum_fusio, ...), custom_call_target="tpu_custom_call" | custom-call | tf_op jit(solution)/shard_map/ffn/pallas_call | solution.py:541
  534.9 1.5 pad_maximum_fusion.2
  536.4 221.7 %grads.1 = (bf16[1024,2304]{1,0:T(8,128)(2,1)}, f32[5,288,2304]{2,1,0:T(8,128)}, bf16[5,288,2304]{2,1,0:T(8,128)(2,1)}, bf16[5,288,2304]{2,1,0:T(8,128)(2,1)}, f...) custom-call(s32[2,1,512]{2,1,0:T(1,128)} %constant_dynamic-slice_fusion.1.seg_row, ...), custom_call_target="tpu_custom_call" | custom-call | tf_op jit(solution)/shard_map/grads/pallas_call | solution.py:927
  759.1 7.0 multiply_reduce_fusion
  767.0 3.7 multiply_reduce_fusion.3
  770.7 1.3 collective-permute-start.19
  772.1 2.0 multiply_reduce_fusion.4
  779.3 2.1 collective-permute-start.13
  781.4 1.6 collective-permute-done.13
  783.6 2.1 collective-permute-start.14
  785.7 1.6 collective-permute-done.14
  787.9 4.8 collective-permute-start.15
  793.7 3.4 collective-permute-start.16
  797.1 1.2 collective-permute-done.16
  800.4 3.0 add_multiply_fusion.3
  805.9 2.5 add_multiply_fusion.4
  809.5 15.6 %add_multiply_fusion = (f32[288,2304]{1,0:T(8,128)}, f32[288,2304]{1,0:T(8,128)}, f32[288,2304]{1,0:T(8,128)}, f32[288,2304]{1,0:T(8,128)}, f32[288,2304]{1,0:T(8,128)}, /*index=5*/f32[288,2304]{1,0:T(8,128)}) fusion(f32[288,2304]{1,0:T(8,128)} %param.36, bf16[5,288,2304]{2,1,0:T(8,128)(2,1)} %get-tuple-element.50, bf16[5,288,2304]{2,1,0:T(8,128)(2,1)S(1)} %bitcast.132, ...), kind=kLoop, calls=%fused_computation.27 | loop fusion | flops 19906560 | bytes 47775748 | tf_op jit(solution)/shard_map/mul | solution.py:1078
  825.1 5.0 copy.120
  830.1 2.2 copy.121
  (173 shorter events, 38.8 us)
Async XLA Ops:
  0.7 9.3 %copy-start.20 = (s32[2,1,1024]{2,1,0:T(1,128)S(1)}, s32[2,1,1024]{2,1,0:T(1,128)}, u32[]{:S(2)}) copy-start(s32[2,1,1024]{2,1,0:T(1,128)} %param.27) | copy-start | bytes 24580
  0.7 10.6 %copy-start.29 = (f32[288]{0:T(512)S(1)}, f32[288]{0:T(512)}, u32[]{:S(2)}) copy-start(f32[288]{0:T(512)} %param.37) | copy-start | bytes 3460
  0.7 28.2 %copy-start.9 = (f32[288,512]{1,0:T(8,128)S(1)}, f32[288,512]{1,0:T(8,128)}, u32[]{:S(2)}) copy-start(f32[288,512]{1,0:T(8,128)} %param.33) | copy-start | bytes 1769476
  0.7 31.1 %copy-start.4 = (f32[288,2304]{1,0:T(8,128)S(1)}, f32[288,2304]{1,0:T(8,128)}, u32[]{:S(2)}) copy-start(f32[288,2304]{1,0:T(8,128)} %param.34) | copy-start | bytes 7962628
  5.0 50.4 %collective-permute-start = (bf16[288,1024]{1,0:T(8,128)(2,1)}, bf16[288,1024]{1,0:T(8,128)(2,1)}, u32[]{:S(2)}, u32[]{:S(2)}) collective-permute-start(bf16[288,1024]{1,0:T(8,128)(2,1)} %pad_maximum_fusion.4), channel_id=1, source_target_pairs={{0,8},{8,0},{16,24},{24,16},{1,9},{9,1},{17,25},{25,17},{2,10},{10... | collective-permute-start | bytes 1769480 | tf_op jit(solution)/shard_map/ppermute | solution.py:38
  7.9 52.2 %collective-permute-start.1 = (bf16[288,1024]{1,0:T(8,128)(2,1)}, bf16[288,1024]{1,0:T(8,128)(2,1)}, u32[]{:S(2)}, u32[]{:S(2)}) collective-permute-start(bf16[288,1024]{1,0:T(8,128)(2,1)} %pad_maximum_fusion.4), channel_id=1, source_target_pairs={{0,16},{8,24},{16,0},{24,8},{1,17},{9,25},{17,1},{25,9},{2,18},{10... | collective-permute-start | bytes 1769480 | tf_op jit(solution)/shard_map/ppermute | solution.py:39
  29.6 3.4 copy-start
  38.9 6.6 copy-start.21
  43.2 2.6 copy-start.11
  43.2 2.6 copy-start.13
  49.4 2.8 copy-start.1
  52.2 3.2 copy-start.16
  55.4 9.8 %collective-permute-start.8 = (bf16[288,512]{1,0:T(8,128)(2,1)S(1)}, bf16[288,512]{1,0:T(8,128)(2,1)S(1)}, u32[]{:S(2)}, u32[]{:S(2)}) collective-permute-start(bf16[288,512]{1,0:T(8,128)(2,1)S(1)} %copy-done.16), channel_id=1, source_target_pairs={{0,16},{8,24},{16,0},{24,8},{1,17},{9,25},{17,1},{25,9},{2,18},{10... | collective-permute-start | bytes 884744 | tf_op jit(solution)/shard_map/ppermute | solution.py:39
  57.1 9.9 %collective-permute-start.7 = (bf16[288,512]{1,0:T(8,128)(2,1)S(1)}, bf16[288,512]{1,0:T(8,128)(2,1)S(1)}, u32[]{:S(2)}, u32[]{:S(2)}) collective-permute-start(bf16[288,512]{1,0:T(8,128)(2,1)S(1)} %copy-done.16), channel_id=1, source_target_pairs={{0,8},{8,0},{16,24},{24,16},{1,9},{9,1},{17,25},{25,17},{2,10},{10... | collective-permute-start | bytes 884744 | tf_op jit(solution)/shard_map/ppermute | solution.py:38
  59.6 13.7 %collective-permute-start.3 = (bf16[144,1024]{1,0:T(8,128)(2,1)S(1)}, bf16[144,1024]{1,0:T(8,128)(2,1)S(1)}, u32[]{:S(2)}, u32[]{:S(2)}) collective-permute-start(bf16[144,1024]{1,0:T(8,128)(2,1)S(1)} %slice.226), channel_id=1, source_target_pairs={{0,16},{8,24},{16,0},{24,8},{1,17},{9,25},{17,1},{25,9},{2,18},{10... | collective-permute-start | bytes 884744 | tf_op jit(solution)/shard_map/ppermute | solution.py:41
  61.1 12.2 %collective-permute-start.2 = (bf16[144,1024]{1,0:T(8,128)(2,1)S(1)}, bf16[144,1024]{1,0:T(8,128)(2,1)S(1)}, u32[]{:S(2)}, u32[]{:S(2)}) collective-permute-start(bf16[144,1024]{1,0:T(8,128)(2,1)S(1)} %slice.225), channel_id=1, source_target_pairs={{0,8},{8,0},{16,24},{24,16},{1,9},{9,1},{17,25},{25,17},{2,10},{10... | collective-permute-start | bytes 884744 | tf_op jit(solution)/shard_map/ppermute | solution.py:40
  65.2 10.3 %collective-permute-start.9 = (bf16[144,512]{1,0:T(8,128)(2,1)S(1)}, bf16[144,512]{1,0:T(8,128)(2,1)S(1)}, u32[]{:S(2)}, u32[]{:S(2)}) collective-permute-start(bf16[144,512]{1,0:T(8,128)(2,1)S(1)} %slice.245), channel_id=1, source_target_pairs={{0,8},{8,0},{16,24},{24,16},{1,9},{9,1},{17,25},{25,17},{2,10},{10... | collective-permute-start | bytes 442376 | tf_op jit(solution)/shard_map/ppermute | solution.py:40
  67.0 8.6 %collective-permute-start.10 = (bf16[144,512]{1,0:T(8,128)(2,1)S(1)}, bf16[144,512]{1,0:T(8,128)(2,1)S(1)}, u32[]{:S(2)}, u32[]{:S(2)}) collective-permute-start(bf16[144,512]{1,0:T(8,128)(2,1)S(1)} %slice.246), channel_id=1, source_target_pairs={{0,16},{8,24},{16,0},{24,8},{1,17},{9,25},{17,1},{25,9},{2,18},{10... | collective-permute-start | bytes 442376 | tf_op jit(solution)/shard_map/ppermute | solution.py:41
  73.3 6.5 collective-permute-start.4
  75.6 4.1 collective-permute-start.11
  79.9 3.1 copy-start.5
  80.2 2.7 copy-start.2
  83.0 2.9 copy-start.22
  83.0 2.9 copy-start.23
  91.0 5.6 collective-permute-start.6
  91.6 2.4 collective-permute-start.5
  759.1 7.1 collective-permute-start.17
  766.2 4.5 collective-permute-start.18
  767.0 42.5 %slice-start = ((s8[6635520]{0:T(1024)(128)(4,1)}), s8[2441216]{0:T(1024)(128)(4,1)S(1)}, s32[]{:S(2)}) async-start(s8[6635520]{0:T(1024)(128)(4,1)} %bitcast.131), calls=%async_computation | async-start | bytes 4882432
  770.7 32.9 %copy-start.25 = (f32[288]{0:T(512)S(1)}, f32[288]{0:T(512)}, u32[]{:S(2)}) copy-start(f32[288]{0:T(512)} %param.51) | copy-start | bytes 3460
  770.7 33.5 %copy-start.26 = (f32[288]{0:T(512)S(1)}, f32[288]{0:T(512)}, u32[]{:S(2)}) copy-start(f32[288]{0:T(512)} %param.50) | copy-start | bytes 3460
  770.7 34.0 %copy-start.27 = (f32[288]{0:T(512)S(1)}, f32[288]{0:T(512)}, u32[]{:S(2)}) copy-start(f32[288]{0:T(512)} %param.49) | copy-start | bytes 3460
  770.7 34.6 %copy-start.28 = (f32[288]{0:T(512)S(1)}, f32[288]{0:T(512)}, u32[]{:S(2)}) copy-start(f32[288]{0:T(512)} %param.48) | copy-start | bytes 3460
  770.7 35.2 %copy-start.8 = (f32[288,512]{1,0:T(8,128)S(1)}, f32[288,512]{1,0:T(8,128)}, u32[]{:S(2)}) copy-start(f32[288,512]{1,0:T(8,128)} %param.30) | copy-start | bytes 1769476
  770.7 28.2 %collective-permute-start.19 = (f32[4,2304]{1,0:T(4,128)S(1)}, f32[4,2304]{1,0:T(4,128)S(1)}, u32[]{:S(2)}, u32[]{:S(2)}) collective-permute-start(f32[4,2304]{1,0:T(4,128)S(1)} %add.273), channel_id=1, source_target_pairs={{0,16},{8,24},{16,0},{24,8},{1,17},{9,25},{17,1},{25,9},{2,18},{10... | collective-permute-start | bytes 110600 | tf_op jit(solution)/shard_map/ppermute | solution.py:116
  777.3 1.3 collective-permute-start.12
  779.3 3.7 collective-permute-start.13
  783.6 3.7 collective-permute-start.14
  787.9 5.1 collective-permute-start.15
  793.7 4.6 collective-permute-start.16
  799.6 8.8 %copy-start.18 = (f32[288,256]{1,0:T(8,128)S(1)}, f32[288,256]{1,0:T(8,128)}, u32[]{:S(2)}) copy-start(f32[288,256]{1,0:T(8,128)} %param.42) | copy-start | bytes 884740
  800.3 8.0 copy-start.7
  800.4 8.0 copy-start.14
  800.4 8.0 copy-start.15
  800.4 8.0 copy-start.17
  800.4 9.1 %slice-start.1 = ((s8[6635520]{0:T(1024)(128)(4,1)}), s8[4194304]{0:T(1024)(128)(4,1)S(1)}, s32[]{:S(2)}) async-start(s8[6635520]{0:T(1024)(128)(4,1)} %bitcast.131), calls=%async_computation.1 | async-start | bytes 8388608
  825.1 5.0 slice-start.2
  825.1 5.0 slice-start.3
  (6 other events, 12.3 us)

commit v4 on v3

--- a/solution.py
+++ b/solution.py
@@ -202,16 +202,18 @@
 TILE = 256
 
 
-def ffn_kernel(
-    heads_ref, scale_ref, x_hbm, cot_hbm, w_out_hbm, own_hbm,
+def layer_kernel(
+    first_row, gains_own, cos_hbm, sin_hbm, x_hbm, cot_hbm, own_qkv, own_out, own_gate, own_up, own_down,
     out_hbm, ffn_in_hbm, hidden_hbm, d_ffn_hbm, d_gate_hbm, d_up_hbm, d_attn_hbm, d_heads_hbm,
-    d_mid_hbm, gain_ref, attn_hbm, slope_hbm, value_hbm,
-    weights, w_out, send, near, across, total, xb, cb, ab, act, act_t, stage, d_heads,
-    line_send, line_recv, credit, local, ag_send, ag_recv, ag_local,
+    d_mid_hbm, gain_ref, scale_ref, attn_in_hbm, heads_hbm, pack_hbm, w_qkv_hbm, w_out_hbm,
+    attn_hbm, slope_hbm, value_hbm,
+    weights, w_qkv, send, near, across, total, xb, cb, ab, act, act_t, stage, d_heads, angle,
+    line_send, line_recv, credit, local, ag_send, ag_recv, ag_local, gain_send, gain_recv, kv_sem,
 ):
     dp, core, z = lax.axis_index("dp"), lax.axis_index("ctx"), lax.axis_index("mp")
+    w_out = w_qkv.at[:, : w_out_hbm.shape[1]]
     width, units = xb.shape[1], weights.shape[2]
-    rows_own = own_hbm.shape[1]
+    rows_own = own_qkv.shape[0]
     half = rows_own // 2
     inner = (z == 1) | (z == 2)
     outer = (z == 0) | (z == 3)
@@ -221,13 +223,16 @@
     far_peer = (dp, core, 3 - z)
 
     barrier = pltpu.get_barrier_semaphore()
-    for peer in (x_peer, y_peer, core_peer, near_peer, far_peer):
+    group = [(dp ^ (m // 2), (1 - core) if m % 2 else core, z) for m in range(1, 8)]
+    for peer in (*group, near_peer, far_peer):
         pl.semaphore_signal(barrier, inc=1, device_id=peer, device_id_type=MESH)
-    pl.semaphore_wait(barrier, 5)
 
     def block(mask, other=False, low=0, size=rows_own):
         owner = (dp ^ mask) * 2 + ((1 - core) if other else core)
         return pl.ds(pl.multiple_of(owner * rows_own + low, 16), size)
+
+    owns = (own_qkv, own_out, own_gate, own_up, own_down)
+    wholes = (w_qkv, w_out_hbm, weights.at[0], weights.at[1], weights.at[2])
 
     def gather(w, name, recv=False):
         table = {
@@ -243,14 +248,14 @@
         }
         index, out_rows, peer, in_rows = table[name]
         rows = in_rows if recv else out_rows
-        src = own_hbm.at[w] if name in ("x", "y", "own_c") else weights.at[w, rows]
+        src = owns[w] if name in ("x", "y", "own_c") else wholes[w].at[rows]
         return pltpu.make_async_remote_copy(
-            src_ref=src, dst_ref=weights.at[w, rows], send_sem=ag_send.at[w, index],
+            src_ref=src, dst_ref=wholes[w].at[rows], send_sem=ag_send.at[w, index],
             recv_sem=ag_recv.at[w, index], device_id=peer, device_id_type=MESH,
         )
 
     def own_copy(w):
-        return pltpu.make_async_copy(own_hbm.at[w], weights.at[w, block(0)], ag_local.at[w])
+        return pltpu.make_async_copy(owns[w], wholes[w].at[block(0)], ag_local.at[w])
 
     def gather_first(w):
         for name in ("x", "y", "own_c"):
@@ -337,10 +342,12 @@
     def store_t(ref, u, sem):
         return pltpu.make_async_copy(act_t, ref.at[:, rows_of(u)], local.at[sem])
 
-    def turn():
+    def turn(source=None):
+        source = act if source is None else source
+
         @pl.loop(0, width // TILE)
         def _(n):
-            act_t[tile(n)] = act[:, tile(n)].T
+            act_t[tile(n)] = source[:, tile(n)].T
 
     def tile(n):
         return pl.ds(pl.multiple_of(n * TILE, TILE), TILE)
@@ -361,14 +368,14 @@
 
         @pl.loop(0, width // TILE)
         def _(n):
-            dst[:, tile(n)] = dot_t(heads_ref[rows_of(u)], w_out[tile(n)]).astype(BF)
+            dst[:, tile(n)] = dot_t(act[:, 2 * HEAD * u : 2 * HEAD * (u + 1)], w_out[tile(n)]).astype(BF)
 
     def middle(rows, u4):
         attn = total[u4, rows].astype(F32) if u4 is not None else ab[rows].astype(F32)
         r_two = inverse_rms(attn)
         return attn, r_two, xb[rows].astype(F32) + attn * r_two * scale(1)
 
-    def forward(u, k):
+    def forward(u, k, ready=None):
         load(x_hbm, u, xb, 0).start()
         store(total.at[u], attn_hbm, u, 1).start()
         load(x_hbm, u, xb, 0).wait()
@@ -393,6 +400,8 @@
         saves = ((0, hidden_hbm), (1, slope_hbm), (2, value_hbm))
         for i, ref in saves:
             store(stage.at[i], ref, u, 3 + i).start()
+        if ready is not None:
+            ready()
         dst = send.at[k % 3]
 
         @pl.loop(0, width // TILE)
@@ -483,29 +492,183 @@
         store_t(d_attn_hbm, u, 1).wait()
         store(d_heads, d_heads_hbm, u, 2).wait()
 
+    def gain_copy(m, recv=False):
+        peer = group[m - 1]
+        owner = (peer[0] * 2 + peer[1]) if recv else (dp * 2 + core)
+        return pltpu.make_async_remote_copy(
+            src_ref=gains_own, dst_ref=send.at[2, pl.ds(pl.multiple_of(owner * 16, 16), 16)],
+            send_sem=gain_send.at[m], recv_sem=gain_recv.at[m], device_id=peer, device_id_type=MESH,
+        )
+
+    def gains_sum():
+        whole = gains_own[...].astype(F32)
+        for m in range(1, 8):
+            gain_copy(m, True).wait_recv()
+        for m in range(1, 8):
+            owner = group[m - 1][0] * 2 + group[m - 1][1]
+            whole += send[2, pl.ds(pl.multiple_of(owner * 16, 16), 16)].astype(F32)
+        scale_ref[...] = 1.0 + whole[:8]
+        for m in range(1, 8):
+            gain_copy(m).wait_send()
+
+    loaded = (stage.at[0], stage.at[1], stage.at[2], act)
+
+    def first_norm(u):
+        load(x_hbm, u, loaded[u], u).wait()
+
+        def body(rows):
+            x = loaded[u][rows].astype(F32)
+            total[u, rows] = (x * inverse_rms(x) * scale(0)).astype(BF)
+
+        each_rows(body)
+
+    def first_turn(u):
+        if u:
+            store_t(attn_in_hbm, u - 1, 4).wait()
+        turn(total.at[u])
+        store_t(attn_in_hbm, u, 4).start()
+
+    def angles(u):
+        rows = rows_of(u)
+        return (
+            pltpu.make_async_copy(cos_hbm.at[rows], angle.at[u % 2, 0], local.at[2 * (u % 2)]),
+            pltpu.make_async_copy(sin_hbm.at[rows], angle.at[u % 2, 1], local.at[2 * (u % 2) + 1]),
+        )
+
+    packs = (cb, ab)
+
+    def kv_columns(kind, peer=False):
+        side = (1 - core) if peer else core
+        return pl.ds(pl.multiple_of(kind * 4 * HEAD + side * 2 * HEAD, HEAD), 2 * HEAD)
+
+    def kv_copy(mb, kind, recv=False):
+        part = packs[mb].at[:, kv_columns(kind, recv)]
+        return pltpu.make_async_remote_copy(
+            src_ref=part, dst_ref=part, send_sem=kv_sem.at[0, mb, kind], recv_sem=kv_sem.at[1, mb, kind],
+            device_id=core_peer, device_id_type=MESH,
+        )
+
+    def projections(u):
+        mb, b = divmod(u, 2)
+        for copy in angles(u):
+            copy.wait()
+        if u < 3:
+            for copy in angles(u + 1):
+                copy.start()
+        c, s = angle[u % 2, 0], angle[u % 2, 1]
+        for j in range(4):
+            v = dot(total[u], w_qkv[:, j * HEAD : (j + 1) * HEAD])
+            if j < 2:
+                xb[:, (mb * 4 + j * 2 + b) * HEAD : (mb * 4 + j * 2 + b + 1) * HEAD] = rotate(v, c, s).astype(BF)
+            else:
+                place = pl.multiple_of((j - 2) * 4 * HEAD + (core * 2 + b) * HEAD, HEAD)
+                packs[mb][:, pl.ds(place, HEAD)] = (rotate(v, c, s) if j == 2 else v).astype(BF)
+
+    def attention(mb):
+        for kind in (0, 1):
+            kv_copy(mb, kind, True).wait_recv()
+
+        @pl.loop(0, 4)
+        def _(i):
+            h, b = i // 2, i % 2
+            query = xb[:, pl.ds(pl.multiple_of(mb * 4 * HEAD + i * HEAD, HEAD), HEAD)]
+            lowest = first_row[mb, :, pl.ds(pl.multiple_of(b * UNIT, UNIT), UNIT)]
+            query_at = lax.broadcasted_iota(jnp.int32, (UNIT, UNIT), 1) + core * 2 * UNIT + b * UNIT
+            weight, length = [], 0.0
+            for j in range(4):
+                key_at = lax.broadcasted_iota(jnp.int32, (UNIT, UNIT), 0) + j * UNIT
+                score = dot_t(packs[mb][:, j * HEAD : (j + 1) * HEAD], query) * (SCALE / CAP)
+                ok = (key_at <= query_at) & (key_at >= lowest)
+                weight.append(jnp.where(ok, jnp.exp(CAP * jnp.tanh(score)), 0.0))
+                length = length + jnp.sum(weight[j], axis=0, keepdims=True)
+            inverse = 1.0 / length
+            out = 0.0
+            for j in range(4):
+                value = packs[mb][:, (4 + j) * HEAD : (5 + j) * HEAD]
+                out = out + t_dot((weight[j] * inverse).astype(BF), value)
+            place = pl.multiple_of((mb * 2 + b) * 2 * HEAD + h * HEAD, HEAD)
+            act[:, pl.ds(place, HEAD)] = out.astype(BF)
+
+    def heads_store(u):
+        return pltpu.make_async_copy(
+            act.at[:, 2 * HEAD * u : 2 * HEAD * (u + 1)], heads_hbm.at[rows_of(u)], local.at[u]
+        )
+
+    def pack_store(i):
+        return pltpu.make_async_copy((xb, cb, ab)[i], pack_hbm.at[i], ag_local.at[5 + i])
+
+    for u in range(4):
+        load(x_hbm, u, loaded[u], u).start()
+    gain_ref[...] = jnp.zeros_like(gain_ref)
+    pl.semaphore_wait(barrier, 9)
+    for m in range(1, 8):
+        gain_copy(m).start()
     gather_first(0)
-    pltpu.make_async_copy(w_out_hbm, w_out, local.at[0]).start()
-    gain_ref[...] = jnp.zeros_like(gain_ref)
-    pltpu.make_async_copy(w_out_hbm, w_out, local.at[0]).wait()
+    gains_sum()
+    for u in range(4):
+        first_norm(u)
+    for copy in angles(0):
+        copy.start()
+    first_turn(0)
+    gather_second(0)
+    first_turn(1)
+    first_turn(2)
+    gather_third(0)
+    gather_first(1)
+    first_turn(3)
+    gather_end(0)
+    qkv_store = pltpu.make_async_copy(w_qkv, w_qkv_hbm, local.at[5])
+    qkv_store.start()
+    for u in range(4):
+        projections(u)
+        if u % 2:
+            for kind in (0, 1):
+                kv_copy(u // 2, kind).start()
+    gather_second(1)
+    gather_first(2)
+    attention(0)
+    gather_third(1)
+    gather_end(1)
+    qkv_store.wait()
+    store_t(attn_in_hbm, 3, 4).wait()
+    out_load = pltpu.make_async_copy(w_out_hbm, w_out, local.at[4])
+    out_load.start()
+    out_load.wait()
     project_out(0, 0)
     boundary(0, cross=False, back=False, done=False)
     project_out(1, 1)
+    attention(1)
     project_out(2, 2)
+    for i in range(3):
+        pack_store(i).start()
+    for u in range(4):
+        heads_store(u).start()
+    gather_second(2)
+    gather_first(3)
     boundary(1, back=False, done=False)
-    gather_second(0)
-    gather_first(1)
+    gather_third(2)
+    for kind in (0, 1):
+        for mb in (0, 1):
+            kv_copy(mb, kind).wait_send()
+    for i in range(3):
+        pack_store(i).wait()
+    for u in range(4):
+        heads_store(u).wait()
     boundary(2, done=False)
     project_out(3, 3)
-    gather_third(0)
-    gather_second(1)
-    gather_first(2)
+    gather_second(3)
+    gather_first(4)
     boundary(3)
-    gather_third(1)
-    gather_second(2)
-    gather_third(2)
-    for w in range(3):
-        gather_end(w)
-    forward(0, 4)
+    gather_third(3)
+    gather_end(2)
+    gather_end(3)
+
+    def ready():
+        gather_second(4)
+        gather_third(4)
+        gather_end(4)
+
+    forward(0, 4, ready)
 
     @pl.loop(4, 7)
     def _(k):
@@ -522,30 +685,36 @@
         last(k - 11)
 
 
-def ffn_call(heads_out, scales, x, cot, w_out, own):
+def layer_call(first_row, gains_own, cosine, sine, x, cot, owns):
     tokens, width = x.shape
-    units = own.shape[2]
+    units = owns[2].shape[1]
+    qkv_cols, out_cols = owns[0].shape[1], owns[1].shape[1]
     assert tokens == 4 * UNIT
     full = jax.ShapeDtypeStruct((tokens, width), BF)
     wide = jax.ShapeDtypeStruct((tokens, units), BF)
     flipped = jax.ShapeDtypeStruct((width, tokens), BF)
+    heads = jax.ShapeDtypeStruct((tokens, out_cols), BF)
     outs = (
-        full, flipped, wide, flipped, wide, wide, flipped,
-        jax.ShapeDtypeStruct((tokens, w_out.shape[1]), BF),
-        full,
+        full, flipped, wide, flipped, wide, wide, flipped, heads, full,
         jax.ShapeDtypeStruct((3, 8, width), F32),
+        jax.ShapeDtypeStruct((8, width), F32),
+        flipped,
+        heads,
+        jax.ShapeDtypeStruct((3, UNIT, width), BF),
+        jax.ShapeDtypeStruct((width, qkv_cols), BF),
+        jax.ShapeDtypeStruct((width, out_cols), BF),
         full, wide, wide,
     )
     anywhere, vmem = pl.BlockSpec(memory_space=pl.ANY), pl.BlockSpec(memory_space=pltpu.VMEM)
     dma = pltpu.SemaphoreType.DMA
     return pl.pallas_call(
-        ffn_kernel,
+        layer_kernel,
         out_shape=outs,
-        in_specs=[vmem, vmem, anywhere, anywhere, anywhere, anywhere],
-        out_specs=[anywhere] * 9 + [vmem] + [anywhere] * 3,
+        in_specs=[vmem] * 2 + [anywhere] * 9,
+        out_specs=[anywhere] * 9 + [vmem] * 2 + [anywhere] * 8,
         scratch_shapes=[
             pltpu.VMEM((3, width, units), BF),
-            pltpu.VMEM(w_out.shape, BF),
+            pltpu.VMEM((width, qkv_cols), BF),
             pltpu.VMEM((3, UNIT, width), BF),
             pltpu.VMEM((3, UNIT, width), BF),
             pltpu.VMEM((2, UNIT, width), BF),
@@ -556,24 +725,28 @@
             pltpu.VMEM((UNIT, width), BF),
             pltpu.VMEM((width, UNIT), BF),
             pltpu.VMEM((3, UNIT, units), BF),
-            pltpu.VMEM((UNIT, w_out.shape[1]), BF),
+            pltpu.VMEM((UNIT, out_cols), BF),
+            pltpu.VMEM((2, 2, UNIT, HEAD // 2), F32),
             dma((3, 4)),
             dma((3, 4)),
             pltpu.SemaphoreType.REGULAR,
             dma((6,)),
-            dma((3, 9)),
-            dma((3, 9)),
-            dma((3,)),
+            dma((5, 9)),
+            dma((5, 9)),
+            dma((8,)),
+            dma((8,)),
+            dma((8,)),
+            dma((2, 2, 2)),
         ],
         compiler_params=pltpu.CompilerParams(
-            collective_id=1, has_side_effects=True, vmem_limit_bytes=60 * 2**20
+            collective_id=1, has_side_effects=True, vmem_limit_bytes=63 * 10**6
         ),
-        name="ffn",
-    )(heads_out, scales, x, cot, w_out, own)
+        name="layer",
+    )(first_row, gains_own, cosine, sine, x, cot, *owns)
 
 
 def grad_kernel(
-    seg_row, seg_col, cosine, sine, scale_ref, x_hbm, d_mid_hbm, q_hbm, k_hbm, v_hbm, d_heads_hbm, w_qkv_hbm,
+    first_row, cosine, sine, scale_ref, x_hbm, d_mid_hbm, pack_hbm, d_heads_hbm, w_qkv_hbm,
     d_ffn_t, hidden_hbm, ffn_in_t, d_gate_hbm, d_up_hbm, d_attn_t, heads_hbm, attn_in_t,
     in_grad_hbm, own_hbm, by_x_hbm, by_y_hbm, gain_ref, core_hbm, far_hbm,
     w_qkv, left, right, core_out, sums, arrived, own_sum,
@@ -767,10 +940,17 @@
             )
             for h in range(2)
         ]
-        return head_rows + [
-            pltpu.make_async_copy(ref.at[mb], dst, load_sem.at[j])
-            for j, (ref, dst) in enumerate(((q_hbm, queries), (k_hbm, keys), (v_hbm, values)))
-        ]
+
+        def block(i, j, dst, rows, sem):
+            src = pack_hbm.at[i, :, j * HEAD : (j + 1) * HEAD]
+            return pltpu.make_async_copy(src, dst.at[pl.ds(rows * UNIT, UNIT)], load_sem.at[sem])
+
+        return (
+            head_rows
+            + [block(0, mb * 4 + j, queries.at[j // 2], j % 2, 5 + j) for j in range(4)]
+            + [block(1 + mb, j, keys, j, 9 + j) for j in range(4)]
+            + [block(1 + mb, 4 + j, values, j, 13 + j) for j in range(4)]
+        )
 
     def unrotate(v, rows):
         a, b = v[:, : HEAD // 2], v[:, HEAD // 2 :]
@@ -795,9 +975,9 @@
                 first = core * tokens + b * UNIT
                 key_at = lax.broadcasted_iota(jnp.int32, (length, UNIT), 0)
                 query_at = lax.broadcasted_iota(jnp.int32, (length, UNIT), 1) + first
-                same = seg_col[mb] == seg_row[mb, :, rows]
+                lowest = first_row[mb, :, rows]
                 tanh = jnp.tanh(dot_t(keys[...], query) * (SCALE / CAP))
-                weight = jnp.where((key_at <= query_at) & same, jnp.exp(CAP * tanh), 0.0)
+                weight = jnp.where((key_at <= query_at) & (key_at >= lowest), jnp.exp(CAP * tanh), 0.0)
                 probs = weight * (1.0 / jnp.sum(weight, axis=0, keepdims=True))
                 d_probs = dot_t(values[...], grad)
                 mean = jnp.sum(probs * d_probs, axis=0, keepdims=True)
@@ -905,11 +1085,11 @@
             final_copy(i, way).wait_recv()
 
 
-def grad_call(seg_row, seg_col, cosine, sine, scales, arrays):
-    x, w_qkv = arrays[0], arrays[6]
+def grad_call(first_row, cosine, sine, scales, arrays):
+    x, w_qkv = arrays[0], arrays[4]
     tokens, width = x.shape
     rows = width // 8
-    wide = arrays[8].shape[1]
+    wide = arrays[6].shape[1]
     full = jax.ShapeDtypeStruct((tokens, width), BF)
     part = jax.ShapeDtypeStruct((5, rows, wide), BF)
     outs = (
@@ -927,7 +1107,7 @@
     return pl.pallas_call(
         grad_kernel,
         out_shape=outs,
-        in_specs=[vmem] * 5 + [anywhere] * 15,
+        in_specs=[vmem] * 4 + [anywhere] * 13,
         out_specs=[anywhere] * 4 + [vmem] + [anywhere] * 2,
         scratch_shapes=[
             pltpu.VMEM(w_qkv.shape, BF),
@@ -956,7 +1136,7 @@
             dma((3, 4)),
             dma((2, 2)),
             dma((3,)),
-            dma((5,)),
+            dma((17,)),
             dma((5, 8)),
             dma((5, 8)),
             dma((5,)),
@@ -966,10 +1146,82 @@
             collective_id=2, has_side_effects=True, vmem_limit_bytes=63 * 10**6
         ),
         name="grads",
-    )(seg_row, seg_col, cosine, sine, scales, *arrays)
+    )(first_row, cosine, sine, scales, *arrays)
 
 
 def fast_device(
+    sizes,
+    inputs,
+    segment_ids,
+    positions,
+    cotangent,
+    *params,
+):
+    masters, moments = params[:11], params[11:]
+    batches, seqs, tokens, width = inputs.shape
+    assert seqs == 1
+    q_cols, k_cols = masters[0].shape[1], masters[1].shape[1]
+    width_ff = masters[4].shape[1]
+    assert k_cols == HEAD
+
+    own = masters[7].shape[0]
+    place = (lax.axis_index("dp") * sizes["ctx"] + lax.axis_index("ctx")) * own
+    low = [w.astype(BF) for w in masters[:7]]
+    owns = (jnp.concatenate(low[:3], axis=1), *low[3:])
+    gains_own = jnp.zeros((16, width), BF)
+    gains_own = lax.dynamic_update_slice(gains_own, jnp.stack(masters[7:]).astype(BF), (0, place))
+    start = lax.axis_index("ctx") * tokens
+    frequency = jnp.exp(
+        jnp.arange(HEAD // 2, dtype=F32) * (-2.0 * math.log(10000.0) / HEAD)
+    )
+    angle = positions.reshape(-1).astype(F32)[:, None] * frequency
+    cosine, sine = jnp.cos(angle), jnp.sin(angle)
+    first_row = (start + jnp.arange(tokens, dtype=jnp.int32))[None, None] - positions
+    flat = (batches * tokens, width)
+    x = inputs.reshape(flat)
+    outs = layer_call(first_row, gains_own, cosine, sine, x, cotangent.reshape(flat), owns)
+    (
+        output, ffn_in_t, hidden, d_ffn_t, d_gate, d_up, d_attn_t, d_heads, d_mid, gain_parts, scales,
+        attn_in_t, heads_out, pack, w_qkv,
+    ) = outs[:15]
+    outs = grad_call(
+        first_row, cosine, sine, scales,
+        (
+            x, d_mid, pack, d_heads, w_qkv, d_ffn_t, hidden, ffn_in_t, d_gate, d_up, d_attn_t, heads_out,
+            attn_in_t,
+        ),
+    )
+    input_grad, own_sum, by_x, by_y, gain_part = outs[:5]
+
+    def final_sum(i, cols):
+        picked = [v[i, :, :cols].astype(F32) for v in (own_sum, by_x, by_y)]
+        return picked[0] + picked[1] + picked[2]
+
+    qkv_cols = w_qkv.shape[1]
+    s_down, s_gate, s_up = [final_sum(i, width_ff) for i in range(3)]
+    s_out, s_qkv = final_sum(3, q_cols), final_sum(4, qkv_cols)
+    gain_grads = jnp.concatenate([jnp.sum(gain_part, axis=0)[None], jnp.sum(gain_parts, axis=1)])
+    gain_grads = sum_small(gain_grads, ("ctx", "dp"), sizes)
+    summed = (
+        s_qkv[:, :q_cols], s_qkv[:, q_cols : q_cols + k_cols], s_qkv[:, q_cols + k_cols :],
+        s_out, s_gate, s_up, s_down,
+    )
+    weight_sq = sum(jnp.sum(g * g) for g in (s_qkv, s_out, s_gate, s_up, s_down))
+    weight_sq = sum_small(weight_sq.reshape(1, 1), ("ctx", "dp", "mp"), sizes)[0, 0]
+    norm_value = jnp.sqrt(weight_sq + jnp.sum(gain_grads * gain_grads))
+    factor = 1.0 / jnp.maximum(norm_value, 1.0)
+    own_gains = lax.dynamic_slice_in_dim(gain_grads, place, own, 1)
+    summed += tuple(own_gains[i] for i in range(4))
+    new_moments = tuple(0.5 * m + 0.5 * factor * g for m, g in zip(moments, summed))
+    changes = tuple(-RATE * (m + 0.01 * w) for w, m in zip(masters[:7], new_moments[:7]))
+
+    return (
+        output.reshape(inputs.shape),
+        input_grad.reshape(inputs.shape), norm_value.reshape(1), *changes, *new_moments
+    )
+
+
+def per_device(
     sizes,
     inputs,
     segment_ids,
@@ -983,8 +1235,9 @@
     full_len = segment_ids.shape[2]
     q_cols, k_cols = masters[0].shape[1], masters[1].shape[1]
     heads = q_cols // HEAD
-    width_ff = masters[4].shape[1]
     assert k_cols == HEAD
+    cuts = 2 if tokens >= 512 else 1
+    unit = tokens // cuts
 
     low = [w.astype(BF) for w in masters[:7]]
     qkv_own = jnp.concatenate(low[:3], axis=1)
@@ -993,6 +1246,9 @@
     gain_one, gain_two, gain_three, gain_four = [gains[:, i] for i in range(4)]
     w_qkv, mark = gather_rows(qkv_own, sizes, None)
     w_out, mark = gather_rows(low[3], sizes, mark)
+    w_gate, mark = gather_rows(low[4], sizes, mark)
+    w_up, mark = gather_rows(low[5], sizes, mark)
+    w_down, mark = gather_rows(low[6], sizes, mark)
 
     start = lax.axis_index("ctx") * tokens
     causal = (start + jnp.arange(tokens))[:, None] >= jnp.arange(full_len)[None, :]
@@ -1027,124 +1283,6 @@
             )
         )
 
-    flat = (batches * tokens, width)
-    heads_all = jnp.concatenate([s["heads_out"] for s in state])
-    outs = ffn_call(
-        heads_all, (1.0 + gains).T, inputs.reshape(flat), cotangent.reshape(flat), w_out,
-        jnp.stack(low[4:]),
-    )
-    output, ffn_in_t, hidden, d_ffn_t, d_gate, d_up, d_attn_t, d_heads, d_mid, gain_parts = outs[:10]
-
-    def batch(key):
-        return jnp.stack([s[key] for s in state])
-
-    def tokens_of(key):
-        return jnp.concatenate([s[key] for s in state])
-
-    seg_all = segment_ids[:, 0]
-    seg_row = lax.dynamic_slice_in_dim(seg_all, start, tokens, 1)[:, None]
-    outs = grad_call(
-        seg_row, seg_all[:, :, None], tokens_of("cosine"), tokens_of("sine"), (1.0 + gains).T,
-        (
-            inputs.reshape(flat), d_mid, batch("queries").reshape(batches, heads, tokens, HEAD),
-            batch("keys"), batch("values"), d_heads, w_qkv, d_ffn_t, hidden, ffn_in_t, d_gate, d_up,
-            d_attn_t, heads_all, tokens_of("attn_in").T,
-        ),
-    )
-    input_grad, own_sum, by_x, by_y, gain_part = outs[:5]
-
-    def final_sum(i, cols):
-        picked = [v[i, :, :cols].astype(F32) for v in (own_sum, by_x, by_y)]
-        return picked[0] + picked[1] + picked[2]
-
-    qkv_cols = w_qkv.shape[1]
-    s_down, s_gate, s_up = [final_sum(i, width_ff) for i in range(3)]
-    s_out, s_qkv = final_sum(3, q_cols), final_sum(4, qkv_cols)
-    gain_grads = jnp.concatenate([jnp.sum(gain_part, axis=0)[None], jnp.sum(gain_parts, axis=1)])
-    gain_grads = sum_small(gain_grads, ("ctx", "dp"), sizes)
-    summed = (
-        s_qkv[:, :q_cols], s_qkv[:, q_cols : q_cols + k_cols], s_qkv[:, q_cols + k_cols :],
-        s_out, s_gate, s_up, s_down,
-    )
-    weight_sq = sum(jnp.sum(g * g) for g in (s_qkv, s_out, s_gate, s_up, s_down))
-    weight_sq = sum_small(weight_sq.reshape(1, 1), ("ctx", "dp", "mp"), sizes)[0, 0]
-    norm_value = jnp.sqrt(weight_sq + jnp.sum(gain_grads * gain_grads))
-    factor = 1.0 / jnp.maximum(norm_value, 1.0)
-    own = masters[7].shape[0]
-    place = (lax.axis_index("dp") * sizes["ctx"] + lax.axis_index("ctx")) * own
-    own_gains = lax.dynamic_slice_in_dim(gain_grads, place, own, 1)
-    summed += tuple(own_gains[i] for i in range(4))
-    new_moments = tuple(0.5 * m + 0.5 * factor * g for m, g in zip(moments, summed))
-    changes = tuple(-RATE * (m + 0.01 * w) for w, m in zip(masters[:7], new_moments[:7]))
-
-    return (
-        output.reshape(inputs.shape),
-        input_grad.reshape(inputs.shape), norm_value.reshape(1), *changes, *new_moments
-    )
-
-
-def per_device(
-    sizes,
-    inputs,
-    segment_ids,
-    positions,
-    cotangent,
-    *params,
-):
-    masters, moments = params[:11], params[11:]
-    batches, seqs, tokens, width = inputs.shape
-    assert seqs == 1
-    full_len = segment_ids.shape[2]
-    q_cols, k_cols = masters[0].shape[1], masters[1].shape[1]
-    heads = q_cols // HEAD
-    assert k_cols == HEAD
-    cuts = 2 if tokens >= 512 else 1
-    unit = tokens // cuts
-
-    low = [w.astype(BF) for w in masters[:7]]
-    qkv_own = jnp.concatenate(low[:3], axis=1)
-    gains_own = jnp.stack([g.astype(BF) for g in masters[7:]], axis=1)
-    gains = lax.all_gather(gains_own, ("dp", "ctx"), axis=0, tiled=True).astype(F32)
-    gain_one, gain_two, gain_three, gain_four = [gains[:, i] for i in range(4)]
-    w_qkv, mark = gather_rows(qkv_own, sizes, None)
-    w_out, mark = gather_rows(low[3], sizes, mark)
-    w_gate, mark = gather_rows(low[4], sizes, mark)
-    w_up, mark = gather_rows(low[5], sizes, mark)
-    w_down, mark = gather_rows(low[6], sizes, mark)
-
-    start = lax.axis_index("ctx") * tokens
-    causal = (start + jnp.arange(tokens))[:, None] >= jnp.arange(full_len)[None, :]
-    frequency = jnp.exp(
-        jnp.arange(HEAD // 2, dtype=F32) * (-2.0 * math.log(10000.0) / HEAD)
-    )
-
-    state = []
-    for mb in range(batches):
-        x = inputs[mb, 0].astype(F32)
-        r_one = inverse_rms(x)
-        attn_in = (x * r_one * (1.0 + gain_one)).astype(BF)
-        angles = positions[mb, 0].astype(F32)[:, None] * frequency
-        cosine, sine = jnp.cos(angles), jnp.sin(angles)
-        seg = segment_ids[mb, 0]
-        seg_local = lax.dynamic_slice_in_dim(seg, start, tokens)
-        allowed = causal & (seg_local[:, None] == seg[None, :])
-        proj = dot(attn_in, w_qkv)
-        queries = jnp.concatenate(
-            [rotate(proj[:, h * HEAD : (h + 1) * HEAD], cosine, sine) for h in range(heads)]
-        ).astype(BF)
-        keys = rotate(proj[:, q_cols : q_cols + HEAD], cosine, sine).astype(BF)
-        values = proj[:, q_cols + HEAD :].astype(BF)
-        both = swap_ctx(jnp.concatenate([keys, values], axis=1), sizes)
-        keys_all, values_all = both[:, :HEAD], both[:, HEAD:]
-        out, saved = attend(queries, keys_all, values_all, allowed)
-        heads_out = jnp.concatenate(jnp.split(out, heads, axis=0), axis=1)
-        state.append(
-            dict(
-                x=x, r_one=r_one, attn_in=attn_in, cosine=cosine, sine=sine, queries=queries,
-                keys=keys_all, values=values_all, saved=saved, heads_out=heads_out,
-            )
-        )
-
     units = [(mb, cut) for mb in range(batches) for cut in range(cuts)]
     work = []
     for mb, cut in units:

time: 845 us -> 780 us (0.923)
  Pallas kernels: 655 us -> 680 us
  local copies, waits for them, and re-layouts: 31.9 us -> 8.83 us
  other arithmetic: 76.6 us -> 54.1 us
  starting transfers between devices: 28.4 us -> 15.8 us
  matrix products: 9.93 us -> 0 us
  waiting for transfers between devices: 13.1 us -> 4.63 us
    pallas_call x2, Pallas kernels: 655 us -> 680 us  [the longest x1 459 us: layer_call(): pl.pallas_call(layer_kernel, out_shape=outs, in_specs=[vmem] * 2 + [anywh...]
    ppermute x12 -> x0, starting transfers between devices: 12.8 us -> none  [the longest x2 4.43 us: gather_rows(): from_x = lax.ppermute(own, **flip('dp', dp, 1))]
    dot_general x6 -> x0, matrix products: 9.93 us -> none  [the longest x4 7 us: dot(): lax.dot_general(a, b, (((1,), (0,)), ((), ())), preferred_element_type=F32)]
    mul x4 -> x3, other arithmetic: 22.2 us -> 21.5 us  [fast_device(): -RATE * (m + 0.01 * w)]
  transfers between devices with their start and end apart: 20 -> 8, of which waited for: 8 -> 5; matrix products, arithmetic and copies ran while one was open for 7% -> 2% of each run, Pallas kernels for 0% -> 0%
where the time goes in v4:
time: 780 us; the launch traced here: 773 us
  Pallas kernels  680 us (87%)
  other arithmetic  54.1 us (7%)
  starting transfers between devices  15.8 us (2%)
  between operations  9.61 us (1%)
  local copies, waits for them, and re-layouts  8.83 us (1%)
    pallas_call x1, Pallas kernels, layer_call(): pl.pallas_call(layer_kernel, out_shape=outs, in_specs=[vmem] * 2 + [anywh...  459 us
    pallas_call x1, Pallas kernels, grad_call(): pl.pallas_call(grad_kernel, out_shape=outs, in_specs=[vmem] * 4 + [anywhe...  220 us
    mul x3, other arithmetic, fast_device(): -RATE * (m + 0.01 * w)  21.5 us
    ppermute x8, starting transfers between devices, sum_small(): value = value + lax.ppermute(value, **flip(axis, size, step))  15.8 us
  transfers between devices with their start and end apart: 8, of which 5 were waited for; matrix products, arithmetic and copies ran while one was open for 2% of the time, Pallas kernels for 0%

profile of v4, /device:TPU:0, one launch (start us, length us, event | category | flops | bytes accessed | tf_op | source)
XLA Modules:
  0.0 772.8 jit_solution(17671292230797870040)
XLA Ops:
  0.7 0.0 copy-start
  0.7 0.8 convert.16
  1.5 0.7 convert.17
  2.2 0.7 convert.18
  2.9 0.7 convert.19
  3.6 1.0 convert_element_type.75
  4.6 1.0 convert_element_type.76
  5.6 0.0 copy-start.1
  5.6 1.3 convert_element_type.74
  6.8 1.8 convert_element_type.77.own_out
  8.7 1.2 convert_element_type.78.own_gate
  9.9 1.2 convert_element_type.79.own_up
  11.1 1.0 copy-done.2
  12.1 1.2 convert_element_type.80.own_down
  13.3 0.6 fusion.10
  13.9 3.0 multiply_sine_fusion
  16.9 0.5 dynamic_update_slice.3.gains_own
  17.4 0.0 copy-start.9
  17.5 0.9 pad_maximum_fusion.own_qkv
  18.4 459.4 %layer.1 = (bf16[1024,2304]{1,0:T(8,128)(2,1)}, bf16[2304,1024]{1,0:T(8,128)(2,1)}, bf16[1024,2304]{1,0:T(8,128)(2,1)}, bf16[2304,1024]{1,0:T(8,128)(2,1)}, bf16...) custom-call(s32[2,1,512]{2,1,0:T(1,128)} %get-tuple-element.137.firs, ...), custom_call_target="tpu_custom_call" | custom-call | tf_op jit(solution)/shard_map/layer/pallas_call | solution.py:710
  477.7 1.0 reduce_sum.78
  478.7 220.5 %grads.1 = (bf16[1024,2304]{1,0:T(8,128)(2,1)}, f32[5,288,2304]{2,1,0:T(8,128)}, bf16[5,288,2304]{2,1,0:T(8,128)(2,1)}, bf16[5,288,2304]{2,1,0:T(8,128)(2,1)}, f...) custom-call(s32[2,1,512]{2,1,0:T(1,128)} %get-tuple-element.137.first_row, ...), custom_call_target="tpu_custom_call" | custom-call | tf_op jit(solution)/shard_map/grads/pallas_call | solution.py:1107
  699.2 0.9 reduce_sum.77
  700.2 0.1 collective-permute-start.5
  700.3 7.0 multiply_reduce_fusion
  707.3 0.7 collective-permute-start.6
  708.0 3.7 multiply_reduce_fusion.3
  711.7 1.5 collective-permute-start.7
  713.2 2.0 multiply_reduce_fusion.4
  718.4 1.0 collective-permute-start
  719.4 0.3 collective-permute-done
  720.4 2.0 collective-permute-start.1
  722.3 1.7 collective-permute-done.1
  724.7 2.0 collective-permute-start.2
  726.7 1.7 collective-permute-done.2
  729.0 4.5 collective-permute-start.3
  733.6 0.3 collective-permute-done.3
  734.5 4.1 collective-permute-start.4
  738.6 0.5 collective-permute-done.4
  739.8 0.6 multiply_reduce_fusion.5
  741.2 2.6 add_multiply_fusion.5
  743.8 3.3 add_multiply_fusion.3
  747.1 15.7 %add_multiply_fusion = (f32[288,2304]{1,0:T(8,128)}, f32[288,2304]{1,0:T(8,128)}, f32[288,2304]{1,0:T(8,128)}, f32[288,2304]{1,0:T(8,128)}, f32[288,2304]{1,0:T(8,128)}, /*index=5*/f32[288,2304]{1,0:T(8,128)}) fusion(f32[288,2304]{1,0:T(8,128)} %param.35, bf16[5,288,2304]{2,1,0:T(8,128)(2,1)} %get-tuple-element.58, bf16[5,288,2304]{2,1,0:T(8,128)(2,1)S(1)} %bitcast.30, ...), kind=kLoop, calls=%fused_computation.3 | loop fusion | flops 19906560 | bytes 47775748 | tf_op jit(solution)/shard_map/mul | solution.py:1216
  762.8 0.1 fusion.3
  762.9 0.6 multiply_add_fusion
  763.5 0.6 multiply_add_fusion.2
  764.1 5.0 copy.53
  769.1 2.2 copy.54
  (51 shorter events, 0.2 us)
Async XLA Ops:
  0.7 8.0 %copy-start = (f32[288,2304]{1,0:T(8,128)S(1)}, f32[288,2304]{1,0:T(8,128)}, u32[]{:S(2)}) copy-start(f32[288,2304]{1,0:T(8,128)} %param.33) | copy-start | bytes 7962628
  5.6 4.3 copy-start.1
  9.9 2.2 copy-start.2
  12.1 1.2 copy-start.10
  17.4 0.9 copy-start.9
  700.2 7.1 collective-permute-start.5
  707.3 33.9 %copy-start.6 = (f32[288,256]{1,0:T(8,128)S(1)}, f32[288,256]{1,0:T(8,128)}, u32[]{:S(2)}) copy-start(f32[288,256]{1,0:T(8,128)} %param.31) | copy-start | bytes 884740
  707.3 4.4 collective-permute-start.6
  708.0 39.1 %slice-start = ((s8[6635520]{0:T(1024)(128)(4,1)}), s8[2441216]{0:T(1024)(128)(4,1)S(1)}, s32[]{:S(2)}) async-start(s8[6635520]{0:T(1024)(128)(4,1)} %bitcast.29), calls=%async_computation | async-start | bytes 4882432
  711.7 32.1 %copy-start.4 = (f32[288,512]{1,0:T(8,128)S(1)}, f32[288,512]{1,0:T(8,128)}, u32[]{:S(2)}) copy-start(f32[288,512]{1,0:T(8,128)} %param.29) | copy-start | bytes 1769476
  711.7 28.1 %collective-permute-start.7 = (f32[4,2304]{1,0:T(4,128)S(1)}, f32[4,2304]{1,0:T(4,128)S(1)}, u32[]{:S(2)}, u32[]{:S(2)}) collective-permute-start(f32[4,2304]{1,0:T(4,128)S(1)} %add.177), channel_id=1, source_target_pairs={{0,16},{8,24},{16,0},{24,8},{1,17},{9,25},{17,1},{25,9},{2,18},{10... | collective-permute-start | bytes 110600 | tf_op jit(solution)/shard_map/ppermute | solution.py:116
  718.4 1.3 collective-permute-start
  720.4 3.7 collective-permute-start.1
  724.7 3.7 collective-permute-start.2
  729.0 4.9 collective-permute-start.3
  734.5 4.6 collective-permute-start.4
  741.1 2.6 copy-start.3
  741.1 2.6 copy-start.5
  741.1 2.6 copy-start.7
  741.2 2.6 copy-start.8
  741.2 5.9 slice-start.1
  747.1 15.8 %copy-start.11 = (f32[288]{0:T(512)S(1)}, f32[288]{0:T(512)}, u32[]{:S(2)}) copy-start(f32[288]{0:T(512)} %param.50) | copy-start | bytes 3460
  747.1 15.8 %copy-start.12 = (f32[288]{0:T(512)S(1)}, f32[288]{0:T(512)}, u32[]{:S(2)}) copy-start(f32[288]{0:T(512)} %param.49) | copy-start | bytes 3460
  747.1 16.4 %copy-start.13 = (f32[288]{0:T(512)S(1)}, f32[288]{0:T(512)}, u32[]{:S(2)}) copy-start(f32[288]{0:T(512)} %param.48) | copy-start | bytes 3460
  747.1 16.4 %copy-start.14 = (f32[288]{0:T(512)S(1)}, f32[288]{0:T(512)}, u32[]{:S(2)}) copy-start(f32[288]{0:T(512)} %param.47) | copy-start | bytes 3460
  764.1 5.0 slice-start.2
  764.1 5.0 slice-start.3

commit v5 on v2

--- a/solution.py
+++ b/solution.py
@@ -202,16 +202,20 @@
 TILE = 256
 
 
-def ffn_kernel(
-    heads_ref, scale_ref, x_hbm, cot_hbm, w_out_hbm, own_hbm,
+def layer_kernel(
+    first_row, gains_own, cos_hbm, sin_hbm, x_hbm, cot_hbm, own_qkv, own_out, own_gate, own_up, own_down,
     out_hbm, ffn_in_hbm, hidden_hbm, d_ffn_hbm, d_gate_hbm, d_up_hbm, d_attn_hbm, d_heads_hbm,
-    d_mid_hbm, gain_ref, attn_hbm, slope_hbm, value_hbm,
-    weights, w_out, send, near, across, total, xb, cb, ab, act, stage, d_mid, d_heads,
-    line_send, line_recv, credit, local, ag_send, ag_recv, ag_local,
+    d_mid_hbm, gain_ref, scale_ref, attn_in_hbm, heads_hbm, pack_hbm, w_qkv_hbm, w_out_hbm,
+    attn_hbm, slope_hbm, value_hbm,
+    in_grad_hbm, own_hbm, by_x_hbm, by_y_hbm, core_hbm, far_hbm, kv_hbm, d_proj_hbm,
+    weights, w_qkv, send, near, across, total, xb, cb, ab, act, act_t, stage, d_heads, angle,
+    line_send, line_recv, credit, local, ag_send, ag_recv, ag_local, gain_send, gain_recv, kv_sem,
+    load_sem, rs_send, rs_recv, rs_local, kv_back, proj_sem,
 ):
     dp, core, z = lax.axis_index("dp"), lax.axis_index("ctx"), lax.axis_index("mp")
+    w_out = w_qkv.at[:, : w_out_hbm.shape[1]]
     width, units = xb.shape[1], weights.shape[2]
-    rows_own = own_hbm.shape[1]
+    rows_own = own_qkv.shape[0]
     half = rows_own // 2
     inner = (z == 1) | (z == 2)
     outer = (z == 0) | (z == 3)
@@ -221,13 +225,16 @@
     far_peer = (dp, core, 3 - z)
 
     barrier = pltpu.get_barrier_semaphore()
-    for peer in (x_peer, y_peer, core_peer, near_peer, far_peer):
+    group = [(dp ^ (m // 2), (1 - core) if m % 2 else core, z) for m in range(1, 8)]
+    for peer in (*group, near_peer, far_peer):
         pl.semaphore_signal(barrier, inc=1, device_id=peer, device_id_type=MESH)
-    pl.semaphore_wait(barrier, 5)
 
     def block(mask, other=False, low=0, size=rows_own):
         owner = (dp ^ mask) * 2 + ((1 - core) if other else core)
         return pl.ds(pl.multiple_of(owner * rows_own + low, 16), size)
+
+    owns = (own_qkv, own_out, own_gate, own_up, own_down)
+    wholes = (w_qkv, w_out_hbm, weights.at[0], weights.at[1], weights.at[2])
 
     def gather(w, name, recv=False):
         table = {
@@ -243,14 +250,14 @@
         }
         index, out_rows, peer, in_rows = table[name]
         rows = in_rows if recv else out_rows
-        src = own_hbm.at[w] if name in ("x", "y", "own_c") else weights.at[w, rows]
+        src = owns[w] if name in ("x", "y", "own_c") else wholes[w].at[rows]
         return pltpu.make_async_remote_copy(
-            src_ref=src, dst_ref=weights.at[w, rows], send_sem=ag_send.at[w, index],
+            src_ref=src, dst_ref=wholes[w].at[rows], send_sem=ag_send.at[w, index],
             recv_sem=ag_recv.at[w, index], device_id=peer, device_id_type=MESH,
         )
 
     def own_copy(w):
-        return pltpu.make_async_copy(own_hbm.at[w], weights.at[w, block(0)], ag_local.at[w])
+        return pltpu.make_async_copy(owns[w], wholes[w].at[block(0)], ag_local.at[w])
 
     def gather_first(w):
         for name in ("x", "y", "own_c"):
@@ -292,38 +299,33 @@
             rows = pl.ds(pl.multiple_of(r * 16, 16), 16)
             dst[rows] = (a[rows].astype(F32) + b[rows].astype(F32)).astype(BF)
 
-    def boundary(k, up=True, cross=True, back=True, done=True):
+    def boundary(up=None, cross=None, back=None, done=None):
         @pl.when(outer)
         def _():
-            if done:
-                hop(2, k - 3).wait_recv()
-            if cross:
-                hop(0, k - 1).wait_send()
-            if up:
-                hop(0, k).start()
+            if done is not None:
+                hop(2, done).wait_recv()
+            if cross is not None:
+                hop(0, cross).wait_send()
+            if up is not None:
+                hop(0, up).start()
 
         @pl.when(inner)
         def _():
-            if cross:
-                i = k - 1
-                hop(0, i).wait_recv()
-                add_rows(send.at[i % 3], send.at[i % 3], near.at[i % 3])
-                if isinstance(i, int):
-                    if i >= 2:
-                        pl.semaphore_wait(credit, 1)
-                else:
+            if cross is not None:
+                hop(0, cross).wait_recv()
+                add_rows(send.at[cross % 3], send.at[cross % 3], near.at[cross % 3])
+                if not isinstance(cross, int) or cross >= 2:
                     pl.semaphore_wait(credit, 1)
-                hop(1, i).start()
-            if back:
-                i = k - 2
-                hop(1, i).wait_recv()
-                hop(1, i).wait_send()
-                add_rows(total.at[i % 4], send.at[i % 3], across.at[i % 2])
-                if not isinstance(i, int) or i < 10:
+                hop(1, cross).start()
+            if back is not None:
+                hop(1, back).wait_recv()
+                hop(1, back).wait_send()
+                add_rows(total.at[back % 4], send.at[back % 3], across.at[back % 2])
+                if not isinstance(back, int) or back < 14:
                     pl.semaphore_signal(credit, inc=1, device_id=far_peer, device_id_type=MESH)
-                hop(2, i).start()
-            if done:
-                hop(2, k - 3).wait_send()
+                hop(2, back).start()
+            if done is not None:
+                hop(2, done).wait_send()
 
     def rows_of(u):
         return pl.ds(pl.multiple_of(u * UNIT, UNIT), UNIT)
@@ -333,6 +335,16 @@
 
     def store(src, ref, u, sem):
         return pltpu.make_async_copy(src, ref.at[rows_of(u)], local.at[sem])
+
+    def store_t(ref, u, sem):
+        return pltpu.make_async_copy(act_t, ref.at[:, rows_of(u)], local.at[sem])
+
+    def turn(source=None):
+        source = act if source is None else source
+
+        @pl.loop(0, width // TILE)
+        def _(n):
+            act_t[tile(n)] = source[:, tile(n)].T
 
     def tile(n):
         return pl.ds(pl.multiple_of(n * TILE, TILE), TILE)
@@ -353,14 +365,14 @@
 
         @pl.loop(0, width // TILE)
         def _(n):
-            dst[:, tile(n)] = dot_t(heads_ref[rows_of(u)], w_out[tile(n)]).astype(BF)
+            dst[:, tile(n)] = dot_t(act[:, 2 * HEAD * u : 2 * HEAD * (u + 1)], w_out[tile(n)]).astype(BF)
 
     def middle(rows, u4):
         attn = total[u4, rows].astype(F32) if u4 is not None else ab[rows].astype(F32)
         r_two = inverse_rms(attn)
         return attn, r_two, xb[rows].astype(F32) + attn * r_two * scale(1)
 
-    def forward(u, k):
+    def forward(u, k, ready=None):
         load(x_hbm, u, xb, 0).start()
         store(total.at[u], attn_hbm, u, 1).start()
         load(x_hbm, u, xb, 0).wait()
@@ -370,7 +382,8 @@
             act[rows] = (mid * inverse_rms(mid) * scale(2)).astype(BF)
 
         each_rows(body)
-        store(act, ffn_in_hbm, u, 2).start()
+        turn()
+        store_t(ffn_in_hbm, u, 2).start()
 
         @pl.loop(0, units // TILE)
         def _(f):
@@ -384,6 +397,8 @@
         saves = ((0, hidden_hbm), (1, slope_hbm), (2, value_hbm))
         for i, ref in saves:
             store(stage.at[i], ref, u, 3 + i).start()
+        if ready is not None:
+            ready()
         dst = send.at[k % 3]
 
         @pl.loop(0, width // TILE)
@@ -393,7 +408,7 @@
         for i, ref in saves:
             store(stage.at[i], ref, u, 3 + i).wait()
         store(total.at[u], attn_hbm, u, 1).wait()
-        store(act, ffn_in_hbm, u, 2).wait()
+        store_t(ffn_in_hbm, u, 2).wait()
 
     def backward(u, k):
         loads = (
@@ -418,7 +433,8 @@
 
         each_rows(body)
         store(xb, out_hbm, u, 0).start()
-        store(act, d_ffn_hbm, u, 1).start()
+        turn()
+        store_t(d_ffn_hbm, u, 1).start()
 
         @pl.loop(0, units // TILE)
         def _(f):
@@ -436,7 +452,7 @@
             dst[:, tile(n)] = part.astype(BF)
 
         store(xb, out_hbm, u, 0).wait()
-        store(act, d_ffn_hbm, u, 1).wait()
+        store_t(d_ffn_hbm, u, 1).wait()
         store(stage.at[1], d_gate_hbm, u, 4).wait()
         store(stage.at[2], d_up_hbm, u, 5).wait()
 
@@ -455,85 +471,562 @@
             mean = jnp.mean(scaled * mid, axis=-1, keepdims=True)
             grad = cb[rows].astype(F32) + r * scaled - mid * (r * r * r) * mean
             add_gain(1, mid * r * dy)
-            d_mid[rows] = grad
+            cb[rows] = grad.astype(BF)
             scaled = scale(1) * grad
             mean = jnp.mean(scaled * attn, axis=-1, keepdims=True)
             act[rows] = (r_two * scaled - attn * (r_two * r_two * r_two) * mean).astype(BF)
             add_gain(0, attn * r_two * grad)
 
         each_rows(body)
-        store(d_mid, d_mid_hbm, u, 0).start()
-        store(act, d_attn_hbm, u, 1).start()
+        store(cb, d_mid_hbm, u, 0).start()
+        turn()
+        store_t(d_attn_hbm, u, 1).start()
         for h in range(w_out.shape[1] // TILE):
             columns = slice(h * TILE, (h + 1) * TILE)
             d_heads[:, columns] = dot(act[...], w_out[:, columns]).astype(BF)
         store(d_heads, d_heads_hbm, u, 2).start()
-        store(d_mid, d_mid_hbm, u, 0).wait()
-        store(act, d_attn_hbm, u, 1).wait()
+        store(cb, d_mid_hbm, u, 0).wait()
+        store_t(d_attn_hbm, u, 1).wait()
         store(d_heads, d_heads_hbm, u, 2).wait()
 
+    def gain_copy(m, recv=False):
+        peer = group[m - 1]
+        owner = (peer[0] * 2 + peer[1]) if recv else (dp * 2 + core)
+        return pltpu.make_async_remote_copy(
+            src_ref=gains_own, dst_ref=send.at[2, pl.ds(pl.multiple_of(owner * 16, 16), 16)],
+            send_sem=gain_send.at[m], recv_sem=gain_recv.at[m], device_id=peer, device_id_type=MESH,
+        )
+
+    def gains_sum():
+        whole = gains_own[...].astype(F32)
+        for m in range(1, 8):
+            gain_copy(m, True).wait_recv()
+        for m in range(1, 8):
+            owner = group[m - 1][0] * 2 + group[m - 1][1]
+            whole += send[2, pl.ds(pl.multiple_of(owner * 16, 16), 16)].astype(F32)
+        scale_ref[...] = 1.0 + whole[:8]
+        for m in range(1, 8):
+            gain_copy(m).wait_send()
+
+    loaded = (stage.at[0], stage.at[1], stage.at[2], act)
+
+    def first_norm(u):
+        load(x_hbm, u, loaded[u], u).wait()
+
+        def body(rows):
+            x = loaded[u][rows].astype(F32)
+            total[u, rows] = (x * inverse_rms(x) * scale(0)).astype(BF)
+
+        each_rows(body)
+
+    def first_turn(u):
+        if u:
+            store_t(attn_in_hbm, u - 1, 4).wait()
+        turn(total.at[u])
+        store_t(attn_in_hbm, u, 4).start()
+
+    def angles(u):
+        rows = rows_of(u)
+        return (
+            pltpu.make_async_copy(cos_hbm.at[rows], angle.at[u % 2, 0], local.at[2 * (u % 2)]),
+            pltpu.make_async_copy(sin_hbm.at[rows], angle.at[u % 2, 1], local.at[2 * (u % 2) + 1]),
+        )
+
+    packs = (cb, ab)
+
+    def kv_columns(kind, peer=False):
+        side = (1 - core) if peer else core
+        return pl.ds(pl.multiple_of(kind * 4 * HEAD + side * 2 * HEAD, HEAD), 2 * HEAD)
+
+    def kv_copy(mb, kind, recv=False):
+        part = packs[mb].at[:, kv_columns(kind, recv)]
+        return pltpu.make_async_remote_copy(
+            src_ref=part, dst_ref=part, send_sem=kv_sem.at[0, mb, kind], recv_sem=kv_sem.at[1, mb, kind],
+            device_id=core_peer, device_id_type=MESH,
+        )
+
+    def projections(u):
+        mb, b = divmod(u, 2)
+        for copy in angles(u):
+            copy.wait()
+        if u < 3:
+            for copy in angles(u + 1):
+                copy.start()
+        c, s = angle[u % 2, 0], angle[u % 2, 1]
+        for j in range(4):
+            v = dot(total[u], w_qkv[:, j * HEAD : (j + 1) * HEAD])
+            if j < 2:
+                xb[:, (mb * 4 + j * 2 + b) * HEAD : (mb * 4 + j * 2 + b + 1) * HEAD] = rotate(v, c, s).astype(BF)
+            else:
+                place = pl.multiple_of((j - 2) * 4 * HEAD + (core * 2 + b) * HEAD, HEAD)
+                packs[mb][:, pl.ds(place, HEAD)] = (rotate(v, c, s) if j == 2 else v).astype(BF)
+
+    def attention(mb):
+        for kind in (0, 1):
+            kv_copy(mb, kind, True).wait_recv()
+
+        @pl.loop(0, 4)
+        def _(i):
+            h, b = i // 2, i % 2
+            query = xb[:, pl.ds(pl.multiple_of(mb * 4 * HEAD + i * HEAD, HEAD), HEAD)]
+            lowest = first_row[mb, :, pl.ds(pl.multiple_of(b * UNIT, UNIT), UNIT)]
+            query_at = lax.broadcasted_iota(jnp.int32, (UNIT, UNIT), 1) + core * 2 * UNIT + b * UNIT
+            weight, length = [], 0.0
+            for j in range(4):
+                key_at = lax.broadcasted_iota(jnp.int32, (UNIT, UNIT), 0) + j * UNIT
+                score = dot_t(packs[mb][:, j * HEAD : (j + 1) * HEAD], query) * (SCALE / CAP)
+                ok = (key_at <= query_at) & (key_at >= lowest)
+                weight.append(jnp.where(ok, jnp.exp(CAP * jnp.tanh(score)), 0.0))
+                length = length + jnp.sum(weight[j], axis=0, keepdims=True)
+            inverse = 1.0 / length
+            out = 0.0
+            for j in range(4):
+                value = packs[mb][:, (4 + j) * HEAD : (5 + j) * HEAD]
+                out = out + t_dot((weight[j] * inverse).astype(BF), value)
+            place = pl.multiple_of((mb * 2 + b) * 2 * HEAD + h * HEAD, HEAD)
+            act[:, pl.ds(place, HEAD)] = out.astype(BF)
+
+    def heads_store(u):
+        return pltpu.make_async_copy(
+            act.at[:, 2 * HEAD * u : 2 * HEAD * (u + 1)], heads_hbm.at[rows_of(u)], local.at[u]
+        )
+
+    def pack_store(i):
+        return pltpu.make_async_copy((xb, cb, ab)[i], pack_hbm.at[i], ag_local.at[5 + i])
+
+    for u in range(4):
+        load(x_hbm, u, loaded[u], u).start()
+    gain_ref[...] = jnp.zeros_like(gain_ref)
+    pl.semaphore_wait(barrier, 9)
+    for m in range(1, 8):
+        gain_copy(m).start()
     gather_first(0)
-    pltpu.make_async_copy(w_out_hbm, w_out, local.at[0]).start()
-    gain_ref[...] = jnp.zeros_like(gain_ref)
-    pltpu.make_async_copy(w_out_hbm, w_out, local.at[0]).wait()
-    project_out(0, 0)
-    boundary(0, cross=False, back=False, done=False)
-    project_out(1, 1)
-    project_out(2, 2)
-    boundary(1, back=False, done=False)
+    gains_sum()
+    for u in range(4):
+        first_norm(u)
+    for copy in angles(0):
+        copy.start()
+    first_turn(0)
     gather_second(0)
+    first_turn(1)
+    first_turn(2)
+    gather_third(0)
     gather_first(1)
-    boundary(2, done=False)
-    project_out(3, 3)
-    gather_third(0)
+    first_turn(3)
+    gather_end(0)
+    qkv_store = pltpu.make_async_copy(w_qkv, w_qkv_hbm, local.at[5])
+    qkv_store.start()
+    for u in range(4):
+        projections(u)
+        if u % 2:
+            for kind in (0, 1):
+                kv_copy(u // 2, kind).start()
     gather_second(1)
     gather_first(2)
-    boundary(3)
+    attention(0)
     gather_third(1)
+    gather_end(1)
+    qkv_store.wait()
+    store_t(attn_in_hbm, 3, 4).wait()
+    out_load = pltpu.make_async_copy(w_out_hbm, w_out, local.at[4])
+    out_load.start()
+    out_load.wait()
+    project_out(0, 0)
+    boundary(0)
+    project_out(1, 1)
+    attention(1)
+    project_out(2, 2)
+    for i in range(3):
+        pack_store(i).start()
+    for u in range(4):
+        heads_store(u).start()
     gather_second(2)
+    gather_first(3)
+    boundary(1, 0)
     gather_third(2)
-    for w in range(3):
-        gather_end(w)
-    forward(0, 4)
+    for kind in (0, 1):
+        for mb in (0, 1):
+            kv_copy(mb, kind).wait_send()
+    for i in range(3):
+        pack_store(i).wait()
+    for u in range(4):
+        heads_store(u).wait()
+    boundary(2, 1, 0)
+    project_out(3, 3)
+    gather_second(3)
+    gather_first(4)
+    boundary(3, 2, 1, 0)
+    gather_third(3)
+    gather_end(2)
+    gather_end(3)
+
+    def ready():
+        gather_second(4)
+        gather_third(4)
+        gather_end(4)
+
+    forward(0, 4, ready)
 
     @pl.loop(4, 7)
     def _(k):
-        boundary(k)
+        boundary(k, k - 1, k - 2, k - 3)
         forward(k - 3, k + 1)
 
     @pl.loop(7, 11)
     def _(k):
-        boundary(k)
+        boundary(k, k - 1, k - 2, k - 3)
         backward(k - 7, k + 1)
 
-    for k in (11, 12, 13, 14):
-        boundary(k, up=k < 12, cross=k < 13, back=k < 14)
-        last(k - 11)
-
-
-def ffn_call(heads_out, scales, x, cot, w_out, own):
+    left, w_back = weights.at[0, :, : 4 * UNIT], weights.at[0, :, 4 * UNIT : 8 * UNIT]
+    queries = weights.at[0, : 4 * UNIT, 8 * UNIT :]
+    d_out = weights.at[0, 4 * UNIT : 8 * UNIT, 8 * UNIT :]
+    right = weights.at[1, : 4 * UNIT]
+    jobs = (
+        (d_ffn_hbm, hidden_hbm), (ffn_in_hbm, d_gate_hbm), (ffn_in_hbm, d_up_hbm),
+        (d_attn_hbm, heads_hbm), (attn_in_hbm, d_proj_hbm),
+    )
+
+    def columns(i):
+        return jobs[i][1].shape[1]
+
+    def core_out(m):
+        low = 4 * UNIT + (m % 2) * rows_own
+        return weights.at[1, low : low + rows_own]
+
+    def arrived(m):
+        low = 4 * UNIT + (2 + m % 2) * rows_own
+        return weights.at[1, low : low + rows_own]
+
+    def sums(i, m):
+        low = ((i % 2) * 3 + m - 1) * rows_own
+        return weights.at[2, low : low + rows_own]
+
+    packed = weights.at[2, 6 * rows_own : 6 * rows_own + UNIT]
+    own_sum = weights.at[2, 6 * rows_own + UNIT : 7 * rows_own + UNIT]
+
+    def remote(src, dst, index, peer):
+        return pltpu.make_async_remote_copy(
+            src_ref=src, dst_ref=dst, send_sem=rs_send.at[index], recv_sem=rs_recv.at[index],
+            device_id=peer, device_id_type=MESH,
+        )
+
+    def operands(i):
+        pair = [pltpu.make_async_copy(jobs[i][1], right.at[:, : columns(i)], rs_local.at[1])]
+        if i != 2:
+            pair.append(pltpu.make_async_copy(jobs[i][0], left, rs_local.at[0]))
+        return pair
+
+    def core_copy(i, m):
+        n = columns(i)
+        return remote(core_out(m).at[:, :n], core_hbm.at[i, m, :, :n], (i, m), core_peer)
+
+    def arrive(i, m):
+        n = columns(i)
+        return pltpu.make_async_copy(core_hbm.at[i, m, :, :n], arrived(m).at[:, :n], rs_local.at[2 + m % 2])
+
+    def far_copy(i, way):
+        n = columns(i)
+        rows = slice(0, half) if way == 0 else slice(half, rows_own)
+        peer = (x_peer, y_peer)[way]
+        return remote(sums(i, 3).at[rows, :n], far_hbm.at[i, rows, :n], (i, 4 + way), peer)
+
+    def final_copy(i, way):
+        n = columns(i)
+        dst = (by_x_hbm, by_y_hbm)[way]
+        peer = (x_peer, y_peer)[way]
+        return remote(sums(i, way + 1).at[:, :n], dst.at[i, :, :n], (i, 6 + way), peer)
+
+    def own_store(i):
+        n = columns(i)
+        return pltpu.make_async_copy(own_sum.at[:, :n], own_hbm.at[i, :, :n], rs_local.at[5])
+
+    def block_rows(mask, other):
+        owner = (dp ^ mask) * 2 + ((1 - core) if other else core)
+        return pl.ds(pl.multiple_of(owner * rows_own, 16), rows_own)
+
+    def scatter_start(i):
+        for copy in operands(i):
+            copy.wait()
+        steps = columns(i) // TILE
+
+        for m in (3, 2, 1, 0):
+            if m < 2:
+                core_copy(i, m + 2).wait_send()
+            elif i > 0:
+                core_copy(i - 1, m - 2).wait_send()
+            dst = core_out(m)
+
+            @pl.loop(0, steps)
+            def _(n):
+                dst[:, tile(n)] = dot(left[block_rows(m, True)], right[:, tile(n)]).astype(BF)
+
+            core_copy(i, m).start()
+        if i > 1:
+            for way in (0, 1):
+                far_copy(i - 2, way).wait_send()
+                final_copy(i - 2, way).wait_send()
+        if i > 0:
+            own_store(i - 1).wait()
+        core_copy(i, 3).wait_recv()
+        arrive(i, 3).start()
+        for m in (3, 2, 1, 0):
+            if m:
+                core_copy(i, m - 1).wait_recv()
+                arrive(i, m - 1).start()
+            arrive(i, m).wait()
+            dst, extra = (sums(i, m) if m else own_sum), arrived(m)
+
+            @pl.loop(0, steps)
+            def _(n):
+                part = dot(left[block_rows(m, False)], right[:, tile(n)])
+                dst[:, tile(n)] = (part + extra[:, tile(n)].astype(F32)).astype(BF)
+
+            if m == 3:
+                far_copy(i, 0).start()
+                far_copy(i, 1).start()
+        own_store(i).start()
+
+    def operands_start(i):
+        for copy in operands(i):
+            copy.start()
+
+    def scatter_end(i):
+        n = columns(i)
+        for way in (0, 1):
+            far_copy(i, way).wait_recv()
+        added = arrived(0)
+        copy = pltpu.make_async_copy(far_hbm.at[i, :, :n], added.at[:, :n], rs_local.at[4])
+        copy.start()
+        copy.wait()
+        for way in (1, 0):
+            base = 0 if way == 1 else half
+            dst = sums(i, way + 1)
+
+            @pl.loop(0, half // 16)
+            def _(r):
+                rows = pl.ds(pl.multiple_of(base + r * 16, 16), 16)
+                dst[rows, :n] = (dst[rows, :n].astype(F32) + added[rows, :n].astype(F32)).astype(BF)
+
+            final_copy(i, way).start()
+
+    def back_loads(mb):
+        copies = [pltpu.make_async_copy(pack_hbm.at[1 + mb], packed, load_sem.at[8])]
+        for i in range(4):
+            h, b = divmod(i, 2)
+            rows = pl.ds(i * UNIT, UNIT)
+            query = pack_hbm.at[0, :, (mb * 4 + i) * HEAD : (mb * 4 + i + 1) * HEAD]
+            grad = d_heads_hbm.at[pl.ds((2 * mb + b) * UNIT, UNIT), h * HEAD : (h + 1) * HEAD]
+            copies.append(pltpu.make_async_copy(query, queries.at[rows], load_sem.at[i]))
+            copies.append(pltpu.make_async_copy(grad, d_out.at[rows], load_sem.at[4 + i]))
+        return [*copies, *angles(2 * mb), *angles(2 * mb + 1)]
+
+    def unrotate(v, b):
+        c, s = angle[b, 0], angle[b, 1]
+        v, w = v[:, : HEAD // 2], v[:, HEAD // 2 :]
+        return jnp.concatenate([v * c + w * s, w * c - v * s], axis=1)
+
+    def kv_out(mb):
+        return pltpu.make_async_remote_copy(
+            src_ref=act_t.at[: 4 * UNIT], dst_ref=kv_hbm.at[mb], send_sem=kv_back.at[0, mb],
+            recv_sem=kv_back.at[1, mb], device_id=core_peer, device_id_type=MESH,
+        )
+
+    def proj_store(u):
+        part = stage.at[u // 2, :, (u % 2) * 4 * HEAD : (u % 2 + 1) * 4 * HEAD]
+        return pltpu.make_async_copy(part, d_proj_hbm.at[rows_of(u)], proj_sem.at[u])
+
+    def attention_back(mb):
+        for copy in back_loads(mb):
+            copy.start()
+        for copy in back_loads(mb):
+            copy.wait()
+        d_scores, weights_of = (xb, ab), (act, cb)
+
+        @pl.loop(0, 4)
+        def _(i):
+            h, b = i // 2, i % 2
+            rows = pl.ds(pl.multiple_of(i * UNIT, UNIT), UNIT)
+            query, grad = queries[rows], d_out[rows]
+            lowest = first_row[mb, :, pl.ds(pl.multiple_of(b * UNIT, UNIT), UNIT)]
+            query_at = lax.broadcasted_iota(jnp.int32, (UNIT, UNIT), 1) + core * 2 * UNIT + b * UNIT
+            tanh, weight, d_probs, length, mean = [], [], [], 0.0, 0.0
+            for j in range(4):
+                key_at = lax.broadcasted_iota(jnp.int32, (UNIT, UNIT), 0) + j * UNIT
+                ok = (key_at <= query_at) & (key_at >= lowest)
+                score = dot_t(packed[:, j * HEAD : (j + 1) * HEAD], query) * (SCALE / CAP)
+                tanh.append(jnp.tanh(score))
+                weight.append(jnp.where(ok, jnp.exp(CAP * tanh[j]), 0.0))
+                d_probs.append(dot_t(packed[:, (4 + j) * HEAD : (5 + j) * HEAD], grad))
+                length = length + jnp.sum(weight[j], axis=0, keepdims=True)
+                mean = mean + jnp.sum(weight[j] * d_probs[j], axis=0, keepdims=True)
+            inverse = 1.0 / length
+            mean = mean * inverse
+            d_query = 0.0
+            for j in range(4):
+                probs = weight[j] * inverse
+                d_raw = (probs * (d_probs[j] - mean) * (1.0 - tanh[j] * tanh[j])).astype(BF)
+                place = pl.ds(pl.multiple_of((j % 2) * 4 * HEAD + i * HEAD, HEAD), HEAD)
+                d_scores[j // 2][:, place] = d_raw
+                weights_of[j // 2][:, place] = probs.astype(BF)
+                d_query = d_query + t_dot(d_raw, packed[:, j * HEAD : (j + 1) * HEAD])
+            place = pl.ds(pl.multiple_of(b * 4 * HEAD + h * HEAD, HEAD), HEAD)
+            stage[mb, :, place] = unrotate(d_query * SCALE, b).astype(BF)
+
+        def block_grads(j):
+            place = slice((j % 2) * 4 * HEAD, (j % 2 + 1) * 4 * HEAD)
+            d_key = dot(d_scores[j // 2][:, place], queries[...]) * SCALE
+            return d_key, dot(weights_of[j // 2][:, place], d_out[...])
+
+        for side in (0, 1):
+
+            @pl.when(core == side)
+            def _():
+                for t in (0, 1):
+                    d_key, d_value = block_grads((1 - side) * 2 + t)
+                    act_t[t * UNIT : (t + 1) * UNIT] = d_key.astype(BF)
+                    act_t[(2 + t) * UNIT : (3 + t) * UNIT] = d_value.astype(BF)
+
+        kv_out(mb).start()
+        kv_out(mb).wait_recv()
+        copy = pltpu.make_async_copy(kv_hbm.at[mb], act_t.at[4 * UNIT : 8 * UNIT], rs_local.at[6])
+        copy.start()
+        copy.wait()
+        for side in (0, 1):
+
+            @pl.when(core == side)
+            def _():
+                for t in (0, 1):
+                    d_key, d_value = block_grads(side * 2 + t)
+                    d_key = d_key + act_t[(4 + t) * UNIT : (5 + t) * UNIT].astype(F32)
+                    d_value = d_value + act_t[(6 + t) * UNIT : (7 + t) * UNIT].astype(F32)
+                    low = t * 4 * HEAD
+                    stage[mb, :, low + 2 * HEAD : low + 3 * HEAD] = unrotate(d_key, t).astype(BF)
+                    stage[mb, :, low + 3 * HEAD : low + 4 * HEAD] = d_value.astype(BF)
+
+        proj_store(2 * mb).start()
+        proj_store(2 * mb + 1).start()
+        kv_out(mb).wait_send()
+
+    def project_back(u):
+        dst = send.at[(12 + u) % 3]
+        low = (u % 2) * 4 * HEAD
+
+        @pl.loop(0, width // TILE)
+        def _(n):
+            dst[:, tile(n)] = dot_t(stage[u // 2, :, low : low + 4 * HEAD], w_back[tile(n)]).astype(BF)
+
+    def first_back(u):
+        loads = (load(x_hbm, u, xb, 0), load(d_mid_hbm, u, ab, 1))
+        for copy in loads:
+            copy.start()
+        for copy in loads:
+            copy.wait()
+
+        def body(rows):
+            x = xb[rows].astype(F32)
+            r_one = inverse_rms(x)
+            dy = total[u, rows].astype(F32)
+            scaled = scale(0) * dy
+            mean = jnp.mean(scaled * x, axis=-1, keepdims=True)
+            back = r_one * scaled - x * (r_one * r_one * r_one) * mean
+            ab[rows] = (ab[rows].astype(F32) + back).astype(BF)
+            add_gain(3, x * r_one * dy)
+
+        each_rows(body)
+        store(ab, in_grad_hbm, u, 2).start()
+        store(ab, in_grad_hbm, u, 2).wait()
+
+    w_load = pltpu.make_async_copy(w_qkv_hbm, w_back, rs_local.at[7])
+    operands_start(0)
+    w_load.start()
+    boundary(11, 10, 9, 8)
+    scatter_start(0)
+    operands_start(1)
+    last(0)
+    boundary(None, 11, 10, 9)
+    scatter_end(0)
+    last(1)
+    attention_back(0)
+    w_load.wait()
+    project_back(0)
+    boundary(12, None, 11, 10)
+    project_back(1)
+    last(2)
+    scatter_start(1)
+    operands_start(2)
+    boundary(13, 12, None, 11)
+    scatter_end(1)
+    last(3)
+    attention_back(1)
+    project_back(2)
+    boundary(14, 13, 12)
+    project_back(3)
+    scatter_start(2)
+    operands_start(3)
+    boundary(15, 14, 13, 12)
+    scatter_end(2)
+    first_back(0)
+    scatter_start(3)
+    for u in range(4):
+        proj_store(u).wait()
+    operands_start(4)
+    boundary(None, 15, 14, 13)
+    scatter_end(3)
+    scatter_start(4)
+    first_back(1)
+    boundary(None, None, 15, 14)
+    scatter_end(4)
+    first_back(2)
+    boundary(None, None, None, 15)
+    first_back(3)
+    own_store(4).wait()
+    for m in range(2):
+        core_copy(4, m).wait_send()
+    for i in range(5):
+        for way in (0, 1):
+            if i > 2:
+                far_copy(i, way).wait_send()
+                final_copy(i, way).wait_send()
+            final_copy(i, way).wait_recv()
+
+
+def layer_call(first_row, gains_own, cosine, sine, x, cot, owns):
     tokens, width = x.shape
-    units = own.shape[2]
+    units = owns[2].shape[1]
+    qkv_cols, out_cols = owns[0].shape[1], owns[1].shape[1]
     assert tokens == 4 * UNIT
     full = jax.ShapeDtypeStruct((tokens, width), BF)
     wide = jax.ShapeDtypeStruct((tokens, units), BF)
+    flipped = jax.ShapeDtypeStruct((width, tokens), BF)
+    rows = owns[0].shape[0]
+    part = jax.ShapeDtypeStruct((5, rows, units), BF)
+    heads = jax.ShapeDtypeStruct((tokens, out_cols), BF)
     outs = (
-        full, full, wide, full, wide, wide, full,
-        jax.ShapeDtypeStruct((tokens, w_out.shape[1]), BF),
-        jax.ShapeDtypeStruct((tokens, width), F32),
-        jax.ShapeDtypeStruct((3, 8, width), F32),
+        full, flipped, wide, flipped, wide, wide, flipped, heads, full,
+        jax.ShapeDtypeStruct((4, 8, width), F32),
+        jax.ShapeDtypeStruct((8, width), F32),
+        flipped,
+        heads,
+        jax.ShapeDtypeStruct((3, UNIT, width), BF),
+        jax.ShapeDtypeStruct((width, qkv_cols), BF),
+        jax.ShapeDtypeStruct((width, out_cols), BF),
         full, wide, wide,
+        full, part, part, part,
+        jax.ShapeDtypeStruct((5, 4, rows, units), BF),
+        part,
+        jax.ShapeDtypeStruct((2, tokens, HEAD), BF),
+        jax.ShapeDtypeStruct((tokens, qkv_cols), BF),
     )
     anywhere, vmem = pl.BlockSpec(memory_space=pl.ANY), pl.BlockSpec(memory_space=pltpu.VMEM)
     dma = pltpu.SemaphoreType.DMA
     return pl.pallas_call(
-        ffn_kernel,
+        layer_kernel,
         out_shape=outs,
-        in_specs=[vmem, vmem, anywhere, anywhere, anywhere, anywhere],
-        out_specs=[anywhere] * 9 + [vmem] + [anywhere] * 3,
+        in_specs=[vmem] * 2 + [anywhere] * 9,
+        out_specs=[anywhere] * 9 + [vmem] * 2 + [anywhere] * 16,
         scratch_shapes=[
             pltpu.VMEM((3, width, units), BF),
-            pltpu.VMEM(w_out.shape, BF),
+            pltpu.VMEM((width, qkv_cols), BF),
             pltpu.VMEM((3, UNIT, width), BF),
             pltpu.VMEM((3, UNIT, width), BF),
             pltpu.VMEM((2, UNIT, width), BF),
@@ -542,22 +1035,32 @@
             pltpu.VMEM((UNIT, width), BF),
             pltpu.VMEM((UNIT, width), BF),
             pltpu.VMEM((UNIT, width), BF),
+            pltpu.VMEM((width, UNIT), BF),
             pltpu.VMEM((3, UNIT, units), BF),
-            pltpu.VMEM((UNIT, width), F32),
-            pltpu.VMEM((UNIT, w_out.shape[1]), BF),
+            pltpu.VMEM((UNIT, out_cols), BF),
+            pltpu.VMEM((2, 2, UNIT, HEAD // 2), F32),
             dma((3, 4)),
             dma((3, 4)),
             pltpu.SemaphoreType.REGULAR,
             dma((6,)),
-            dma((3, 9)),
-            dma((3, 9)),
-            dma((3,)),
+            dma((5, 9)),
+            dma((5, 9)),
+            dma((8,)),
+            dma((8,)),
+            dma((8,)),
+            dma((2, 2, 2)),
+            dma((9,)),
+            dma((5, 8)),
+            dma((5, 8)),
+            dma((8,)),
+            dma((2, 2)),
+            dma((4,)),
         ],
         compiler_params=pltpu.CompilerParams(
-            collective_id=1, has_side_effects=True, vmem_limit_bytes=60 * 2**20
+            collective_id=1, has_side_effects=True, vmem_limit_bytes=63 * 2**20
         ),
-        name="ffn",
-    )(heads_out, scales, x, cot, w_out, own)
+        name="layer",
+    )(first_row, gains_own, cosine, sine, x, cot, *owns)
 
 
 def fast_device(
@@ -571,106 +1074,37 @@
     masters, moments = params[:11], params[11:]
     batches, seqs, tokens, width = inputs.shape
     assert seqs == 1
-    full_len = segment_ids.shape[2]
     q_cols, k_cols = masters[0].shape[1], masters[1].shape[1]
-    heads = q_cols // HEAD
+    width_ff = masters[4].shape[1]
     assert k_cols == HEAD
-    cuts = 2 if tokens >= 512 else 1
-    unit = tokens // cuts
-
+
+    own = masters[7].shape[0]
+    place = (lax.axis_index("dp") * sizes["ctx"] + lax.axis_index("ctx")) * own
     low = [w.astype(BF) for w in masters[:7]]
-    qkv_own = jnp.concatenate(low[:3], axis=1)
-    gains_own = jnp.stack([g.astype(BF) for g in masters[7:]], axis=1)
-    gains = lax.all_gather(gains_own, ("dp", "ctx"), axis=0, tiled=True).astype(F32)
-    gain_one, gain_two, gain_three, gain_four = [gains[:, i] for i in range(4)]
-    w_qkv, mark = gather_rows(qkv_own, sizes, None)
-    w_out, mark = gather_rows(low[3], sizes, mark)
-
+    owns = (jnp.concatenate(low[:3], axis=1), *low[3:])
+    gains_own = jnp.zeros((16, width), BF)
+    gains_own = lax.dynamic_update_slice(gains_own, jnp.stack(masters[7:]).astype(BF), (0, place))
     start = lax.axis_index("ctx") * tokens
-    causal = (start + jnp.arange(tokens))[:, None] >= jnp.arange(full_len)[None, :]
     frequency = jnp.exp(
         jnp.arange(HEAD // 2, dtype=F32) * (-2.0 * math.log(10000.0) / HEAD)
     )
-
-    state = []
-    for mb in range(batches):
-        x = inputs[mb, 0].astype(F32)
-        r_one = inverse_rms(x)
-        attn_in = (x * r_one * (1.0 + gain_one)).astype(BF)
-        angles = positions[mb, 0].astype(F32)[:, None] * frequency
-        cosine, sine = jnp.cos(angles), jnp.sin(angles)
-        seg = segment_ids[mb, 0]
-        seg_local = lax.dynamic_slice_in_dim(seg, start, tokens)
-        allowed = causal & (seg_local[:, None] == seg[None, :])
-        proj = dot(attn_in, w_qkv)
-        queries = jnp.concatenate(
-            [rotate(proj[:, h * HEAD : (h + 1) * HEAD], cosine, sine) for h in range(heads)]
-        ).astype(BF)
-        keys = rotate(proj[:, q_cols : q_cols + HEAD], cosine, sine).astype(BF)
-        values = proj[:, q_cols + HEAD :].astype(BF)
-        both = swap_ctx(jnp.concatenate([keys, values], axis=1), sizes)
-        keys_all, values_all = both[:, :HEAD], both[:, HEAD:]
-        out, saved = attend(queries, keys_all, values_all, allowed)
-        heads_out = jnp.concatenate(jnp.split(out, heads, axis=0), axis=1)
-        state.append(
-            dict(
-                x=x, r_one=r_one, attn_in=attn_in, cosine=cosine, sine=sine, queries=queries,
-                keys=keys_all, values=values_all, saved=saved, heads_out=heads_out,
-            )
-        )
-
+    angle = positions.reshape(-1).astype(F32)[:, None] * frequency
+    cosine, sine = jnp.cos(angle), jnp.sin(angle)
+    first_row = (start + jnp.arange(tokens, dtype=jnp.int32))[None, None] - positions
     flat = (batches * tokens, width)
-    heads_all = jnp.concatenate([s["heads_out"] for s in state])
-    outs = ffn_call(
-        heads_all, (1.0 + gains).T, inputs.reshape(flat), cotangent.reshape(flat), w_out,
-        jnp.stack(low[4:]),
-    )
-    output, ffn_in, hidden, d_ffn, d_gate, d_up, d_attn, d_heads_all, d_mid, gain_parts = outs[:10]
-    units = [(mb, cut) for mb in range(batches) for cut in range(cuts)]
-    work = []
-    for i, (mb, cut) in enumerate(units):
-        work.append(dict(rows=slice(cut * unit, (cut + 1) * unit), mb=mb, all=slice(i * unit, (i + 1) * unit)))
-
-    g_down = t_dot(d_ffn, hidden)
-    g_gate = t_dot(ffn_in, d_gate)
-    g_up = t_dot(ffn_in, d_up)
-    s_down, mark = scatter_rows(g_down, sizes, None)
-    s_gate, mark = scatter_rows(g_gate, sizes, mark)
-    s_up, mark = scatter_rows(g_up, sizes, mark)
-
-    for mb in range(batches):
-        s = state[mb]
-        d_heads = d_heads_all[mb * tokens : (mb + 1) * tokens]
-        d_out = jnp.concatenate(jnp.split(d_heads, heads, axis=1))
-        d_queries, d_keys, d_values = attend_back(
-            s["saved"], s["queries"], s["keys"], s["values"], d_out
-        )
-        d_kv = scatter_ctx(jnp.concatenate([d_keys, d_values], axis=1), sizes)
-        pieces = [rotate(q, s["cosine"], -s["sine"]) for q in jnp.split(d_queries, heads)]
-        pieces += [rotate(d_kv[:, :HEAD], s["cosine"], -s["sine"]), d_kv[:, HEAD:]]
-        s["d_proj"] = jnp.concatenate(pieces, axis=1).astype(BF)
-    for w in work:
-        part = dot_t(state[w["mb"]]["d_proj"][w["rows"]], w_qkv).astype(BF)
-        w["d_attn_in"] = sum_mp(part, sizes)
-
-    g_out = t_dot(d_attn, heads_all)
-    g_qkv = t_dot(
-        jnp.concatenate([s["attn_in"] for s in state]),
-        jnp.concatenate([s["d_proj"] for s in state]),
-    )
-    s_out, mark = scatter_rows(g_out, sizes, mark)
-    s_qkv, mark = scatter_rows(g_qkv, sizes, mark)
-
-    for w in work:
-        s = state[w["mb"]]
-        back, w["g_one"] = norm_back(
-            s["x"][w["rows"]], s["r_one"][w["rows"]], gain_one, w["d_attn_in"].astype(F32)
-        )
-        w["input_grad"] = (d_mid[w["all"]] + back).astype(BF)
-
-    gain_grads = jnp.concatenate(
-        [sum(w["g_one"] for w in work)[None], jnp.sum(gain_parts, axis=1)]
-    )
+    x = inputs.reshape(flat)
+    outs = layer_call(first_row, gains_own, cosine, sine, x, cotangent.reshape(flat), owns)
+    output, gain_parts = outs[0], outs[9]
+    input_grad, own_sum, by_x, by_y = outs[19:23]
+
+    def final_sum(i, cols):
+        picked = [v[i, :, :cols].astype(F32) for v in (own_sum, by_x, by_y)]
+        return picked[0] + picked[1] + picked[2]
+
+    qkv_cols = owns[0].shape[1]
+    s_down, s_gate, s_up = [final_sum(i, width_ff) for i in range(3)]
+    s_out, s_qkv = final_sum(3, q_cols), final_sum(4, qkv_cols)
+    gain_grads = jnp.sum(gain_parts, axis=1)
     gain_grads = sum_small(gain_grads, ("ctx", "dp"), sizes)
     summed = (
         s_qkv[:, :q_cols], s_qkv[:, q_cols : q_cols + k_cols], s_qkv[:, q_cols + k_cols :],
@@ -680,16 +1114,14 @@
     weight_sq = sum_small(weight_sq.reshape(1, 1), ("ctx", "dp", "mp"), sizes)[0, 0]
     norm_value = jnp.sqrt(weight_sq + jnp.sum(gain_grads * gain_grads))
     factor = 1.0 / jnp.maximum(norm_value, 1.0)
-    own = masters[7].shape[0]
-    place = (lax.axis_index("dp") * sizes["ctx"] + lax.axis_index("ctx")) * own
     own_gains = lax.dynamic_slice_in_dim(gain_grads, place, own, 1)
-    summed += tuple(own_gains[i] for i in range(4))
+    summed += tuple(own_gains[i] for i in (3, 0, 1, 2))
     new_moments = tuple(0.5 * m + 0.5 * factor * g for m, g in zip(moments, summed))
     changes = tuple(-RATE * (m + 0.01 * w) for w, m in zip(masters[:7], new_moments[:7]))
 
     return (
         output.reshape(inputs.shape),
-        jnp.concatenate([w["input_grad"] for w in work]).reshape(inputs.shape), norm_value.reshape(1), *changes, *new_moments
+        input_grad.reshape(inputs.shape), norm_value.reshape(1), *changes, *new_moments
     )
 
 

time: 1160 us -> 724 us (0.62)
  waiting for transfers between devices: 356 us -> 6.58 us
  Pallas kernels: 432 us -> 631 us
  other arithmetic: 156 us -> 47.6 us
  matrix products: 90.1 us -> 0 us
  starting transfers between devices: 63.2 us -> 12.7 us
  local copies, waits for them, and re-layouts: 41 us -> 9.41 us
    ppermute x51 -> x0, waiting for transfers between devices: 350 us -> none  [the longest x5 85.5 us: scatter_rows(): far_low = lax.ppermute(part(3, half, rows).astype(BF), **flip('dp', dp, 2))]
    pallas_call x1, Pallas kernels: 432 us -> 631 us  [layer_call(): pl.pallas_call(layer_kernel, out_shape=outs, in_specs=[vmem] * 2 + [anywh...]
    dot_general x23 -> x0, matrix products: 90.1 us -> none  [the longest x9 62.8 us: t_dot(): lax.dot_general(a, b, (((0,), (0,)), ((), ())), preferred_element_type=F32)]
    ppermute x51 -> x0, starting transfers between devices: 51.6 us -> none  [the longest x4 6.91 us: sum_mp(): across = lax.ppermute(pair, 'mp', [(1, 2), (2, 1)])]
    convert_element_type x26 -> x1, other arithmetic: 38.3 us -> 0.6 us  [fast_device(): angle = positions.reshape(-1).astype(F32)[:, None] * frequency]
    another operation x15 -> x5, other arithmetic: 26.2 us -> 2.9 us
    unnamed x25 -> x2, other arithmetic: 18.1 us -> 0.01 us
    squeeze x5 -> x0, local copies, waits for them, and re-layouts: 12.9 us -> none  [scatter_rows(): send = lax.dynamic_index_in_dim(blocks, 1 - core, 1, keepdims=False)]
  transfers between devices with their start and end apart: 59 -> 8, of which waited for: 28 -> 5; matrix products, arithmetic and copies ran while one was open for 18% -> 2% of each run, Pallas kernels for 0% -> 0%
where the time goes in v5:
time: 724 us; the launch traced here: 717 us
  Pallas kernels  631 us (87%)
  other arithmetic  47.6 us (7%)
  starting transfers between devices  12.7 us (2%)
  between operations  9.55 us (1%)
  local copies, waits for them, and re-layouts  9.41 us (1%)
    pallas_call x1, Pallas kernels, layer_call(): pl.pallas_call(layer_kernel, out_shape=outs, in_specs=[vmem] * 2 + [anywh...  631 us
    mul x3, other arithmetic, fast_device(): -RATE * (m + 0.01 * w)  19.7 us
  transfers between devices with their start and end apart: 8, of which 5 were waited for; matrix products, arithmetic and copies ran while one was open for 2% of the time, Pallas kernels for 0%

profile of v5, /device:TPU:0, one launch (start us, length us, event | category | flops | bytes accessed | tf_op | source)
XLA Modules:
  0.0 716.6 jit_solution(9729245750249791658)
XLA Ops:
  0.7 0.0 copy-start
  0.7 0.8 convert.16
  1.5 0.7 convert.17
  2.2 0.7 convert.18
  2.9 0.7 convert.19
  3.6 2.9 convert_element_type.100.own_down
  6.6 1.2 convert_element_type.98.own_gate
  7.8 1.0 copy-done.2
  8.8 0.0 copy-start.10
  8.8 1.2 convert_element_type.99.own_up
  10.1 0.1 copy-done.8
  10.2 0.3 copy-done.7
  10.5 0.2 copy-done.5
  10.7 0.8 convert_element_type.97.own_out
  11.4 0.6 fusion.10
  12.0 3.0 multiply_sine_fusion
  15.1 0.5 dynamic_update_slice.3.gains_own
  15.6 0.0 copy-start.9
  15.6 0.9 pad_maximum_fusion.own_qkv
  16.5 630.8 %layer.1 = (bf16[1024,2304]{1,0:T(8,128)(2,1)}, bf16[2304,1024]{1,0:T(8,128)(2,1)}, bf16[1024,2304]{1,0:T(8,128)(2,1)}, bf16[2304,1024]{1,0:T(8,128)(2,1)}, bf16...) custom-call(s32[2,1,512]{2,1,0:T(1,128)} %get-tuple-element.109.firs, ...), custom_call_target="tpu_custom_call" | custom-call | tf_op jit(solution)/shard_map/layer/pallas_call | solution.py:1022
  647.3 1.0 reduce_sum.68
  648.4 0.1 collective-permute-start.5
  648.5 5.9 multiply_reduce_fusion
  654.4 1.0 collective-permute-start.6
  655.4 3.5 multiply_reduce_fusion.3
  658.9 1.2 collective-permute-start.7
  660.1 1.9 multiply_reduce_fusion.4
  665.2 1.0 collective-permute-start
  666.2 0.3 collective-permute-done
  667.2 2.3 collective-permute-start.1
  669.5 1.4 collective-permute-done.1
  671.5 2.3 collective-permute-start.2
  673.8 1.4 collective-permute-done.2
  675.8 1.4 collective-permute-start.3
  677.2 2.3 collective-permute-done.3
  680.2 3.5 collective-permute-start.4
  683.7 1.1 collective-permute-done.4
  685.4 0.6 multiply_reduce_fusion.5
  686.8 2.6 add_multiply_fusion.5
  689.4 3.3 add_multiply_fusion.3
  692.7 0.0 copy-start.13
  692.7 0.0 copy-start.14
  692.8 13.8 %add_multiply_fusion = (f32[288,2304]{1,0:T(8,128)}, f32[288,2304]{1,0:T(8,128)}, f32[288,2304]{1,0:T(8,128)}, f32[288,2304]{1,0:T(8,128)}, f32[288,2304]{1,0:T(8,128)}, /*index=5*/f32[288,2304]{1,0:T(8,128)}) fusion(f32[288,2304]{1,0:T(8,128)} %param.35, bf16[5,288,2304]{2,1,0:T(8,128)(2,1)} %get-tuple-element.31, ...), kind=kLoop, calls=%fused_computation.3 | loop fusion | flops 21897216 | bytes 43794436 | tf_op jit(solution)/shard_map/mul | solution.py:1120
  706.6 0.1 fusion.3
  706.7 0.6 multiply_add_fusion
  707.3 0.6 multiply_add_fusion.2
  707.9 5.0 copy.53
  712.9 2.2 copy.54
  (47 shorter events, 0.2 us)
Async XLA Ops:
  0.7 5.9 copy-start
  6.6 2.2 copy-start.2
  8.8 1.2 copy-start.4
  8.8 1.4 copy-start.8
  8.8 1.7 copy-start.7
  8.8 1.9 copy-start.5
  8.8 2.6 copy-start.10
  15.6 0.9 copy-start.9
  648.4 6.0 collective-permute-start.5
  654.4 4.5 collective-permute-start.6
  655.4 37.3 %slice-start = ((s8[6635520]{0:T(1024)(128)(4,1)}), s8[2441216]{0:T(1024)(128)(4,1)S(1)}, s32[]{:S(2)}) async-start(s8[6635520]{0:T(1024)(128)(4,1)} %bitcast.27), calls=%async_computation | async-start | bytes 4882432
  658.9 26.5 %collective-permute-start.7 = (f32[4,2304]{1,0:T(4,128)S(1)}, f32[4,2304]{1,0:T(4,128)S(1)}, u32[]{:S(2)}, u32[]{:S(2)}) collective-permute-start(f32[4,2304]{1,0:T(4,128)S(1)} %add.177), channel_id=1, source_target_pairs={{0,16},{8,24},{16,0},{24,8},{1,17},{9,25},{17,1},{25,9},{2,18},{10... | collective-permute-start | bytes 110600 | tf_op jit(solution)/shard_map/ppermute | solution.py:116
  665.2 1.3 collective-permute-start
  667.2 3.7 collective-permute-start.1
  671.5 3.7 collective-permute-start.2
  675.8 3.7 collective-permute-start.3
  680.2 4.6 collective-permute-start.4
  686.8 2.6 copy-start.3
  686.8 2.6 copy-start.6
  686.8 5.9 slice-start.1
  689.4 3.3 copy-start.1
  692.7 14.0 %copy-start.11 = (f32[288]{0:T(512)S(1)}, f32[288]{0:T(512)}, u32[]{:S(2)}) copy-start(f32[288]{0:T(512)} %param.50) | copy-start | bytes 3460
  692.7 14.0 %copy-start.12 = (f32[288]{0:T(512)S(1)}, f32[288]{0:T(512)}, u32[]{:S(2)}) copy-start(f32[288]{0:T(512)} %param.49) | copy-start | bytes 3460
  692.7 14.6 %copy-start.13 = (f32[288]{0:T(512)S(1)}, f32[288]{0:T(512)}, u32[]{:S(2)}) copy-start(f32[288]{0:T(512)} %param.48) | copy-start | bytes 3460
  692.7 14.6 %copy-start.14 = (f32[288]{0:T(512)S(1)}, f32[288]{0:T(512)}, u32[]{:S(2)}) copy-start(f32[288]{0:T(512)} %param.47) | copy-start | bytes 3460
  707.9 5.0 slice-start.2
  707.9 5.0 slice-start.3

commit v6 on v5

--- a/solution.py
+++ b/solution.py
@@ -205,12 +205,13 @@
 def layer_kernel(
     first_row, gains_own, cos_hbm, sin_hbm, x_hbm, cot_hbm, own_qkv, own_out, own_gate, own_up, own_down,
     out_hbm, ffn_in_hbm, hidden_hbm, d_ffn_hbm, d_gate_hbm, d_up_hbm, d_attn_hbm, d_heads_hbm,
-    d_mid_hbm, gain_ref, scale_ref, attn_in_hbm, heads_hbm, pack_hbm, w_qkv_hbm, w_out_hbm,
+    d_mid_hbm, gains_out, norm_out, attn_in_hbm, heads_hbm, pack_hbm, w_qkv_hbm, w_out_hbm,
     attn_hbm, slope_hbm, value_hbm,
     in_grad_hbm, own_hbm, by_x_hbm, by_y_hbm, core_hbm, far_hbm, kv_hbm, d_proj_hbm,
     weights, w_qkv, send, near, across, total, xb, cb, ab, act, act_t, stage, d_heads, angle,
     line_send, line_recv, credit, local, ag_send, ag_recv, ag_local, gain_send, gain_recv, kv_sem,
     load_sem, rs_send, rs_recv, rs_local, kv_back, proj_sem,
+    gain_ref, scale_ref, cast, squares, cast_sem, fin_sem, tail_send, tail_recv, z_send, z_recv,
 ):
     dp, core, z = lax.axis_index("dp"), lax.axis_index("ctx"), lax.axis_index("mp")
     w_out = w_qkv.at[:, : w_out_hbm.shape[1]]
@@ -226,7 +227,8 @@
 
     barrier = pltpu.get_barrier_semaphore()
     group = [(dp ^ (m // 2), (1 - core) if m % 2 else core, z) for m in range(1, 8)]
-    for peer in (*group, near_peer, far_peer):
+    line = [(dp, core, z ^ m) for m in range(1, 4)]
+    for peer in (*group, *line):
         pl.semaphore_signal(barrier, inc=1, device_id=peer, device_id_type=MESH)
 
     def block(mask, other=False, low=0, size=rows_own):
@@ -250,7 +252,8 @@
         }
         index, out_rows, peer, in_rows = table[name]
         rows = in_rows if recv else out_rows
-        src = owns[w] if name in ("x", "y", "own_c") else wholes[w].at[rows]
+        direct = w < 2 and name in ("x", "y", "own_c")
+        src = owns[w] if direct else wholes[w].at[rows]
         return pltpu.make_async_remote_copy(
             src_ref=src, dst_ref=wholes[w].at[rows], send_sem=ag_send.at[w, index],
             recv_sem=ag_recv.at[w, index], device_id=peer, device_id_type=MESH,
@@ -259,10 +262,25 @@
     def own_copy(w):
         return pltpu.make_async_copy(owns[w], wholes[w].at[block(0)], ag_local.at[w])
 
+    def round_own(w):
+        size = cast.shape[1]
+        steps = rows_own // size
+        copies = [
+            pltpu.make_async_copy(owns[w].at[pl.ds(c * size, size)], cast.at[c % 2], cast_sem.at[c % 2])
+            for c in range(steps)
+        ]
+        copies[0].start()
+        for c in range(steps):
+            if c + 1 < steps:
+                copies[c + 1].start()
+            copies[c].wait()
+            weights[w - 2, block(0, False, c * size, size)] = cast[c % 2].astype(BF)
+
     def gather_first(w):
         for name in ("x", "y", "own_c"):
             gather(w, name).start()
-        own_copy(w).start()
+        if w < 2:
+            own_copy(w).start()
 
     def gather_second(w):
         gather(w, "x", True).wait_recv()
@@ -280,7 +298,8 @@
     def gather_end(w):
         for name in ("own_c", "x_c", "y_c", "top_c", "low_c"):
             gather(w, name, True).wait_recv()
-        own_copy(w).wait()
+        if w < 2:
+            own_copy(w).wait()
         for name in ("x", "y", "top", "low", "own_c", "x_c", "y_c", "top_c", "low_c"):
             gather(w, name).wait_send()
 
@@ -456,11 +475,15 @@
         store(stage.at[1], d_gate_hbm, u, 4).wait()
         store(stage.at[2], d_up_hbm, u, 5).wait()
 
+    def last_loads(u):
+        return (load(x_hbm, u, xb, 0), load(attn_hbm, u, ab, 1), load(cot_hbm, u, cb, 2))
+
+    def start_all(copies):
+        for copy in copies:
+            copy.start()
+
     def last(u):
-        loads = (load(x_hbm, u, xb, 0), load(attn_hbm, u, ab, 1), load(cot_hbm, u, cb, 2))
-        for copy in loads:
-            copy.start()
-        for copy in loads:
+        for copy in last_loads(u):
             copy.wait()
 
         def body(rows):
@@ -489,16 +512,19 @@
         store_t(d_attn_hbm, u, 1).wait()
         store(d_heads, d_heads_hbm, u, 2).wait()
 
+    own_rows = pl.ds(pl.multiple_of((dp * 2 + core) * 16, 16), 16)
+
     def gain_copy(m, recv=False):
         peer = group[m - 1]
         owner = (peer[0] * 2 + peer[1]) if recv else (dp * 2 + core)
         return pltpu.make_async_remote_copy(
-            src_ref=gains_own, dst_ref=send.at[2, pl.ds(pl.multiple_of(owner * 16, 16), 16)],
+            src_ref=send.at[2, own_rows],
+            dst_ref=send.at[2, own_rows if not recv else pl.ds(pl.multiple_of(owner * 16, 16), 16)],
             send_sem=gain_send.at[m], recv_sem=gain_recv.at[m], device_id=peer, device_id_type=MESH,
         )
 
     def gains_sum():
-        whole = gains_own[...].astype(F32)
+        whole = send[2, own_rows].astype(F32)
         for m in range(1, 8):
             gain_copy(m, True).wait_recv()
         for m in range(1, 8):
@@ -597,7 +623,8 @@
     for u in range(4):
         load(x_hbm, u, loaded[u], u).start()
     gain_ref[...] = jnp.zeros_like(gain_ref)
-    pl.semaphore_wait(barrier, 9)
+    send[2, own_rows] = gains_own[...].astype(BF)
+    pl.semaphore_wait(barrier, 10)
     for m in range(1, 8):
         gain_copy(m).start()
     gather_first(0)
@@ -613,6 +640,7 @@
     gather_third(0)
     gather_first(1)
     first_turn(3)
+    round_own(2)
     gather_end(0)
     qkv_store = pltpu.make_async_copy(w_qkv, w_qkv_hbm, local.at[5])
     qkv_store.start()
@@ -640,10 +668,12 @@
         pack_store(i).start()
     for u in range(4):
         heads_store(u).start()
+    round_own(3)
     gather_second(2)
     gather_first(3)
     boundary(1, 0)
     gather_third(2)
+    round_own(4)
     for kind in (0, 1):
         for mb in (0, 1):
             kv_copy(mb, kind).wait_send()
@@ -747,7 +777,11 @@
     def scatter_start(i):
         for copy in operands(i):
             copy.wait()
-        steps = columns(i) // TILE
+        piece = 768 if columns(i) % 768 == 0 else 512
+        steps = columns(i) // piece
+
+        def piece_at(n):
+            return pl.ds(pl.multiple_of(n * piece, TILE), piece)
 
         for m in (3, 2, 1, 0):
             if m < 2:
@@ -758,7 +792,7 @@
 
             @pl.loop(0, steps)
             def _(n):
-                dst[:, tile(n)] = dot(left[block_rows(m, True)], right[:, tile(n)]).astype(BF)
+                dst[:, piece_at(n)] = dot(left[block_rows(m, True)], right[:, piece_at(n)]).astype(BF)
 
             core_copy(i, m).start()
         if i > 1:
@@ -778,8 +812,8 @@
 
             @pl.loop(0, steps)
             def _(n):
-                part = dot(left[block_rows(m, False)], right[:, tile(n)])
-                dst[:, tile(n)] = (part + extra[:, tile(n)].astype(F32)).astype(BF)
+                part = dot(left[block_rows(m, False)], right[:, piece_at(n)])
+                dst[:, piece_at(n)] = (part + extra[:, piece_at(n)].astype(F32)).astype(BF)
 
             if m == 3:
                 far_copy(i, 0).start()
@@ -915,11 +949,11 @@
         def _(n):
             dst[:, tile(n)] = dot_t(stage[u // 2, :, low : low + 4 * HEAD], w_back[tile(n)]).astype(BF)
 
+    def first_loads(u):
+        return (load(x_hbm, u, xb, 0), load(d_mid_hbm, u, ab, 1))
+
     def first_back(u):
-        loads = (load(x_hbm, u, xb, 0), load(d_mid_hbm, u, ab, 1))
-        for copy in loads:
-            copy.start()
-        for copy in loads:
+        for copy in first_loads(u):
             copy.wait()
 
         def body(rows):
@@ -935,29 +969,103 @@
         each_rows(body)
         store(ab, in_grad_hbm, u, 2).start()
         store(ab, in_grad_hbm, u, 2).wait()
+        if u < 3:
+            start_all(first_loads(u + 1))
+
+    def finish(i):
+        n = columns(i)
+        for way in (0, 1):
+            final_copy(i, way).wait_recv()
+        for low in (0, half):
+            pairs = ((own_hbm, cb), (by_x_hbm, act), (by_y_hbm, stage.at[2]))
+            copies = [
+                pltpu.make_async_copy(ref.at[i, low : low + half, :n], dst.at[:half, :n], fin_sem.at[j])
+                for j, (ref, dst) in enumerate(pairs)
+            ]
+            start_all(copies)
+            for copy in copies:
+                copy.wait()
+
+            @pl.loop(0, half // 16)
+            def _(r):
+                rows = pl.ds(pl.multiple_of(r * 16, 16), 16)
+                v = cb[rows, :n].astype(F32) + act[rows, :n].astype(F32) + stage[2, rows, :n].astype(F32)
+                v = v * v
+                gain_ref[4, :, :n] += v[:8] + v[8:]
+
+    table = weights.at[1, 4 * UNIT + 4 * rows_own :]
+
+    def table_copy(m, recv=False):
+        peer = group[m - 1]
+        owner = (peer[0] * 2 + peer[1]) if recv else (dp * 2 + core)
+        rows = pl.ds(pl.multiple_of(owner * 16, 16), 16)
+        return pltpu.make_async_remote_copy(
+            src_ref=table.at[own_rows], dst_ref=table.at[rows], send_sem=tail_send.at[m],
+            recv_sem=tail_recv.at[m], device_id=peer, device_id_type=MESH,
+        )
+
+    def square_copy(m, recv=False):
+        place = (z ^ m) if recv else z
+        return pltpu.make_async_remote_copy(
+            src_ref=squares.at[z], dst_ref=squares.at[place], send_sem=z_send.at[m],
+            recv_sem=z_recv.at[m], device_id=line[m - 1], device_id_type=MESH,
+        )
+
+    def agree():
+        rows = [jnp.sum(gain_ref[i], axis=0, keepdims=True) for i in (3, 0, 1, 2, 4)]
+        high = [v.astype(BF).astype(F32) for v in rows]
+        low = [v - h for v, h in zip(rows, high)]
+        blank = jnp.zeros((6, rows[0].shape[1]), F32)
+        table[own_rows] = jnp.concatenate([*high, *low, blank], axis=0).astype(BF)
+        for m in range(1, 8):
+            table_copy(m).start()
+        for m in range(1, 8):
+            table_copy(m, True).wait_recv()
+        whole = jnp.zeros((16, rows[0].shape[1]), F32)
+        for owner in range(8):
+            whole = whole + table[owner * 16 : owner * 16 + 16].astype(F32)
+        gains = whole[0:4] + whole[5:9]
+        squares[z] = jnp.broadcast_to(jnp.sum(whole[4:5] + whole[9:10], axis=1, keepdims=True), (8, 128))
+        for m in range(1, 4):
+            square_copy(m).start()
+        gains_out[0:4] = gains
+        gains_out[4:8] = jnp.zeros_like(gains)
+        gain_square = jnp.sum(jnp.sum(gains * gains, axis=1, keepdims=True), axis=0, keepdims=True)
+        for m in range(1, 4):
+            square_copy(m, True).wait_recv()
+        norm_out[...] = jnp.sqrt(squares[0] + squares[1] + squares[2] + squares[3] + gain_square)
+        for m in range(1, 8):
+            table_copy(m).wait_send()
+        for m in range(1, 4):
+            square_copy(m).wait_send()
 
     w_load = pltpu.make_async_copy(w_qkv_hbm, w_back, rs_local.at[7])
     operands_start(0)
     w_load.start()
+    start_all(last_loads(0))
     boundary(11, 10, 9, 8)
     scatter_start(0)
     operands_start(1)
     last(0)
+    start_all(last_loads(1))
     boundary(None, 11, 10, 9)
     scatter_end(0)
     last(1)
     attention_back(0)
+    start_all(last_loads(2))
     w_load.wait()
     project_back(0)
     boundary(12, None, 11, 10)
     project_back(1)
     last(2)
+    start_all(last_loads(3))
     scatter_start(1)
     operands_start(2)
     boundary(13, 12, None, 11)
     scatter_end(1)
     last(3)
     attention_back(1)
+    start_all(first_loads(0))
     project_back(2)
     boundary(14, 13, 12)
     project_back(3)
@@ -970,24 +1078,28 @@
     for u in range(4):
         proj_store(u).wait()
     operands_start(4)
+    finish(0)
+    finish(1)
     boundary(None, 15, 14, 13)
     scatter_end(3)
     scatter_start(4)
     first_back(1)
     boundary(None, None, 15, 14)
     scatter_end(4)
+    own_store(4).wait()
     first_back(2)
+    finish(2)
+    finish(3)
     boundary(None, None, None, 15)
     first_back(3)
-    own_store(4).wait()
+    finish(4)
+    agree()
     for m in range(2):
         core_copy(4, m).wait_send()
-    for i in range(5):
+    for i in range(3, 5):
         for way in (0, 1):
-            if i > 2:
-                far_copy(i, way).wait_send()
-                final_copy(i, way).wait_send()
-            final_copy(i, way).wait_recv()
+            far_copy(i, way).wait_send()
+            final_copy(i, way).wait_send()
 
 
 def layer_call(first_row, gains_own, cosine, sine, x, cot, owns):
@@ -1003,8 +1115,8 @@
     heads = jax.ShapeDtypeStruct((tokens, out_cols), BF)
     outs = (
         full, flipped, wide, flipped, wide, wide, flipped, heads, full,
-        jax.ShapeDtypeStruct((4, 8, width), F32),
         jax.ShapeDtypeStruct((8, width), F32),
+        jax.ShapeDtypeStruct((8, 128), F32),
         flipped,
         heads,
         jax.ShapeDtypeStruct((3, UNIT, width), BF),
@@ -1055,6 +1167,16 @@
             dma((8,)),
             dma((2, 2)),
             dma((4,)),
+            pltpu.VMEM((5, 8, width), F32),
+            pltpu.VMEM((8, width), F32),
+            pltpu.VMEM((2, 32, units), F32),
+            pltpu.VMEM((4, 8, 128), F32),
+            dma((2,)),
+            dma((3,)),
+            dma((8,)),
+            dma((8,)),
+            dma((4,)),
+            dma((4,)),
         ],
         compiler_params=pltpu.CompilerParams(
             collective_id=1, has_side_effects=True, vmem_limit_bytes=63 * 2**20
@@ -1080,10 +1202,10 @@
 
     own = masters[7].shape[0]
     place = (lax.axis_index("dp") * sizes["ctx"] + lax.axis_index("ctx")) * own
-    low = [w.astype(BF) for w in masters[:7]]
-    owns = (jnp.concatenate(low[:3], axis=1), *low[3:])
-    gains_own = jnp.zeros((16, width), BF)
-    gains_own = lax.dynamic_update_slice(gains_own, jnp.stack(masters[7:]).astype(BF), (0, place))
+    low = [w.astype(BF) for w in masters[:4]]
+    owns = (jnp.concatenate(low[:3], axis=1), low[3], *masters[4:7])
+    gains_own = jnp.zeros((16, width), F32)
+    gains_own = lax.dynamic_update_slice(gains_own, jnp.stack(masters[7:]), (0, place))
     start = lax.axis_index("ctx") * tokens
     frequency = jnp.exp(
         jnp.arange(HEAD // 2, dtype=F32) * (-2.0 * math.log(10000.0) / HEAD)
@@ -1094,7 +1216,7 @@
     flat = (batches * tokens, width)
     x = inputs.reshape(flat)
     outs = layer_call(first_row, gains_own, cosine, sine, x, cotangent.reshape(flat), owns)
-    output, gain_parts = outs[0], outs[9]
+    output, gain_grads, norm_tile = outs[0], outs[9], outs[10]
     input_grad, own_sum, by_x, by_y = outs[19:23]
 
     def final_sum(i, cols):
@@ -1104,18 +1226,14 @@
     qkv_cols = owns[0].shape[1]
     s_down, s_gate, s_up = [final_sum(i, width_ff) for i in range(3)]
     s_out, s_qkv = final_sum(3, q_cols), final_sum(4, qkv_cols)
-    gain_grads = jnp.sum(gain_parts, axis=1)
-    gain_grads = sum_small(gain_grads, ("ctx", "dp"), sizes)
     summed = (
         s_qkv[:, :q_cols], s_qkv[:, q_cols : q_cols + k_cols], s_qkv[:, q_cols + k_cols :],
         s_out, s_gate, s_up, s_down,
     )
-    weight_sq = sum(jnp.sum(g * g) for g in (s_qkv, s_out, s_gate, s_up, s_down))
-    weight_sq = sum_small(weight_sq.reshape(1, 1), ("ctx", "dp", "mp"), sizes)[0, 0]
-    norm_value = jnp.sqrt(weight_sq + jnp.sum(gain_grads * gain_grads))
+    norm_value = norm_tile[0, 0]
     factor = 1.0 / jnp.maximum(norm_value, 1.0)
     own_gains = lax.dynamic_slice_in_dim(gain_grads, place, own, 1)
-    summed += tuple(own_gains[i] for i in (3, 0, 1, 2))
+    summed += tuple(own_gains[i] for i in range(4))
     new_moments = tuple(0.5 * m + 0.5 * factor * g for m, g in zip(moments, summed))
     changes = tuple(-RATE * (m + 0.01 * w) for w, m in zip(masters[:7], new_moments[:7]))
 

time: 724 us -> 670 us (0.925)
  other arithmetic: 47.6 us -> 31.9 us
  Pallas kernels: 631 us -> 618 us
  starting transfers between devices: 12.7 us -> 0 us
  between operations: 9.55 us -> 2.08 us
    pallas_call x1, Pallas kernels: 631 us -> 618 us  [layer_call(): pl.pallas_call(layer_kernel, out_shape=outs, in_specs=[vmem] * 2 + [anywh...]
    reduce_sum x5 -> x0, other arithmetic: 13 us -> none  [the longest x3 11.3 us: fast_device(): jnp.sum(g * g)]
    ppermute x8 -> x0, starting transfers between devices: 12.7 us -> none  [sum_small(): value = value + lax.ppermute(value, **flip(axis, size, step))]
  transfers between devices with their start and end apart: 8 -> 0, of which waited for: 5 -> 0; matrix products, arithmetic and copies ran while one was open for 2% -> 0% of each run, Pallas kernels for 0% -> 0%
where the time goes in v6:
time: 670 us; the launch traced here: 662 us
  Pallas kernels  618 us (92%)
  other arithmetic  31.9 us (5%)
  local copies, waits for them, and re-layouts  10.9 us (2%)
    pallas_call x1, Pallas kernels, layer_call(): pl.pallas_call(layer_kernel, out_shape=outs, in_specs=[vmem] * 2 + [anywh...  618 us
    mul x3, other arithmetic, fast_device(): -RATE * (m + 0.01 * w)  19.7 us

profile of v6, /device:TPU:0, one launch (start us, length us, event | category | flops | bytes accessed | tf_op | source)
XLA Modules:
  0.0 662.4 jit_solution(4227464260553558620)
XLA Ops:
  0.7 0.0 copy-start.3
  0.7 0.0 copy-start.2
  0.7 0.8 stack.15
  1.4 0.7 stack.16
  2.1 0.7 stack.17
  2.8 0.7 stack.18
  3.5 0.6 dynamic_update_slice.3.gains_own
  4.1 0.0 copy-start.5
  4.2 1.4 fusion.10
  5.6 3.0 multiply_sine_fusion
  8.6 1.1 convert_element_type.84
  9.7 1.0 convert_element_type.85
  10.7 0.0 copy-done.3
  10.7 0.9 pad_maximum_fusion.own_qkv
  11.6 0.0 copy-done.5
  11.6 0.0 copy-done.2
  11.6 0.8 convert_element_type.87.own_out
  12.4 617.6 %layer.1 = (bf16[1024,2304]{1,0:T(8,128)(2,1)}, bf16[2304,1024]{1,0:T(8,128)(2,1)}, bf16[1024,2304]{1,0:T(8,128)(2,1)}, bf16[2304,1024]{1,0:T(8,128)(2,1)}, bf16...) custom-call(s32[2,1,512]{2,1,0:T(1,128)} %get-tuple-element.83.first, ...), custom_call_target="tpu_custom_call" | custom-call | tf_op jit(solution)/shard_map/layer/pallas_call | solution.py:1134
  629.9 1.2 slice.69
  631.8 1.0 fusion.3
  632.8 0.0 copy-done.10
  632.8 0.0 copy-done.11
  632.8 0.6 multiply_add_fusion
  633.4 0.0 copy-done.12
  633.4 0.0 copy-done.13
  633.4 0.6 multiply_add_fusion.2
  634.0 15.6 %add_multiply_fusion = (f32[288,2304]{1,0:T(8,128)}, f32[288,2304]{1,0:T(8,128)}, f32[288,2304]{1,0:T(8,128)}, f32[288,2304]{1,0:T(8,128)}, f32[288,2304]{1,0:T(8,128)}, /*index=5*/f32[288,2304]{1,0:T(8,128)}) fusion(f32[288,2304]{1,0:T(8,128)} %own_down.1, bf16[5,288,2304]{2,1,0:T(8,128)(2,1)} %get-tuple-element.33, ...), kind=kLoop, calls=%fused_computation.3 | loop fusion | flops 21897216 | bytes 43794436 | tf_op jit(solution)/shard_map/mul | solution.py:1238
  649.6 0.0 copy-start.4
  649.7 0.0 copy-start.8
  649.7 0.0 copy-start.9
  649.7 0.0 copy-start.1
  649.7 0.0 copy-start.6
  649.7 0.0 copy-start.7
  649.7 1.9 add_bitcast_fusion
  651.6 0.0 copy-done.4
  651.6 0.0 copy-done.8
  651.6 0.0 copy-done.9
  651.6 1.1 add_multiply_fusion.5
  652.7 0.0 copy-done.1
  652.7 0.0 copy-done.6
  652.7 0.0 copy-done.7
  652.7 0.0 copy-start
  652.7 2.9 add_multiply_fusion.3
  655.7 0.0 copy-done
  655.7 2.4 copy.51
  658.1 1.5 slice-done
  659.6 0.1 slice-done.1
  659.7 2.2 copy.52
  (12 shorter events, 0.1 us)
Async XLA Ops:
  0.7 10.0 %copy-start.3 = (f32[288,256]{1,0:T(8,128)S(1)}, f32[288,256]{1,0:T(8,128)}, u32[]{:S(2)}) copy-start(f32[288,256]{1,0:T(8,128)} %param.31) | copy-start | bytes 884740
  0.7 11.0 %copy-start.2 = (f32[288,512]{1,0:T(8,128)S(1)}, f32[288,512]{1,0:T(8,128)}, u32[]{:S(2)}) copy-start(f32[288,512]{1,0:T(8,128)} %param.32) | copy-start | bytes 1769476
  4.1 7.5 %copy-start.5 = (f32[16,2304]{1,0:T(8,128)}, f32[16,2304]{1,0:T(8,128)S(1)}, u32[]{:S(2)}) copy-start(f32[16,2304]{1,0:T(8,128)S(1)} %dynamic_update_slice.3.gains_own) | copy-start | bytes 442372
  12.4 620.4 %copy-start.10 = (f32[288]{0:T(512)S(1)}, f32[288]{0:T(512)}, u32[]{:S(2)}) copy-start(f32[288]{0:T(512)} %param.50) | copy-start | bytes 3460
  12.4 620.5 %copy-start.11 = (f32[288]{0:T(512)S(1)}, f32[288]{0:T(512)}, u32[]{:S(2)}) copy-start(f32[288]{0:T(512)} %param.49) | copy-start | bytes 3460
  12.4 621.0 %copy-start.12 = (f32[288]{0:T(512)S(1)}, f32[288]{0:T(512)}, u32[]{:S(2)}) copy-start(f32[288]{0:T(512)} %param.48) | copy-start | bytes 3460
  12.4 621.0 %copy-start.13 = (f32[288]{0:T(512)S(1)}, f32[288]{0:T(512)}, u32[]{:S(2)}) copy-start(f32[288]{0:T(512)} %param.47) | copy-start | bytes 3460
  649.6 2.0 copy-start.4
  649.7 2.0 copy-start.8
  649.7 1.9 copy-start.9
  649.7 3.0 copy-start.1
  649.7 3.0 copy-start.6
  649.7 3.0 copy-start.7
  652.7 3.0 copy-start
  655.7 3.9 slice-start
  655.7 4.0 slice-start.1

commit v7 on v6

--- a/solution.py
+++ b/solution.py
@@ -208,7 +208,7 @@
     d_mid_hbm, gains_out, norm_out, attn_in_hbm, heads_hbm, pack_hbm, w_qkv_hbm, w_out_hbm,
     attn_hbm, slope_hbm, value_hbm,
     in_grad_hbm, own_hbm, by_x_hbm, by_y_hbm, core_hbm, far_hbm, kv_hbm, d_proj_hbm,
-    weights, w_qkv, send, near, across, total, xb, cb, ab, act, act_t, stage, d_heads, angle,
+    weights, w_qkv, send, near, across, total, xb, cb, ab, act, act_t, stage, angle,
     line_send, line_recv, credit, local, ag_send, ag_recv, ag_local, gain_send, gain_recv, kv_sem,
     load_sem, rs_send, rs_recv, rs_local, kv_back, proj_sem,
     gain_ref, scale_ref, cast, squares, cast_sem, fin_sem, tail_send, tail_recv, z_send, z_recv,
@@ -313,7 +313,7 @@
         )
 
     def add_rows(dst, a, b):
-        @pl.loop(0, UNIT // 16)
+        @pl.loop(0, UNIT // 16, unroll=4)
         def _(r):
             rows = pl.ds(pl.multiple_of(r * 16, 16), 16)
             dst[rows] = (a[rows].astype(F32) + b[rows].astype(F32)).astype(BF)
@@ -361,7 +361,7 @@
     def turn(source=None):
         source = act if source is None else source
 
-        @pl.loop(0, width // TILE)
+        @pl.loop(0, width // TILE, unroll=3)
         def _(n):
             act_t[tile(n)] = source[:, tile(n)].T
 
@@ -369,7 +369,7 @@
         return pl.ds(pl.multiple_of(n * TILE, TILE), TILE)
 
     def each_rows(body):
-        @pl.loop(0, UNIT // 16)
+        @pl.loop(0, UNIT // 16, unroll=4)
         def _(r):
             body(pl.ds(pl.multiple_of(r * 16, 16), 16))
 
@@ -382,7 +382,7 @@
     def project_out(u, k):
         dst = send.at[k % 3]
 
-        @pl.loop(0, width // TILE)
+        @pl.loop(0, width // TILE, unroll=3)
         def _(n):
             dst[:, tile(n)] = dot_t(act[:, 2 * HEAD * u : 2 * HEAD * (u + 1)], w_out[tile(n)]).astype(BF)
 
@@ -404,7 +404,7 @@
         turn()
         store_t(ffn_in_hbm, u, 2).start()
 
-        @pl.loop(0, units // TILE)
+        @pl.loop(0, units // TILE, unroll=3)
         def _(f):
             gate = dot(act[...], weights[0, :, tile(f)])
             up = dot(act[...], weights[1, :, tile(f)])
@@ -420,7 +420,7 @@
             ready()
         dst = send.at[k % 3]
 
-        @pl.loop(0, width // TILE)
+        @pl.loop(0, width // TILE, unroll=3)
         def _(n):
             dst[:, tile(n)] = dot_t(stage[0], weights[2, tile(n)]).astype(BF)
 
@@ -455,7 +455,7 @@
         turn()
         store_t(d_ffn_hbm, u, 1).start()
 
-        @pl.loop(0, units // TILE)
+        @pl.loop(0, units // TILE, unroll=3)
         def _(f):
             d_hidden = dot(act[...], weights[2, :, tile(f)])
             stage[1, :, tile(f)] = (d_hidden * stage[1, :, tile(f)].astype(F32)).astype(BF)
@@ -465,7 +465,7 @@
         store(stage.at[2], d_up_hbm, u, 5).start()
         dst = send.at[k % 3]
 
-        @pl.loop(0, width // TILE)
+        @pl.loop(0, width // TILE, unroll=3)
         def _(n):
             part = dot_t(stage[1], weights[0, tile(n)]) + dot_t(stage[2], weights[1, tile(n)])
             dst[:, tile(n)] = part.astype(BF)
@@ -474,6 +474,8 @@
         store_t(d_ffn_hbm, u, 1).wait()
         store(stage.at[1], d_gate_hbm, u, 4).wait()
         store(stage.at[2], d_up_hbm, u, 5).wait()
+
+    d_heads = stage.at[2, :, : w_out_hbm.shape[1]]
 
     def last_loads(u):
         return (load(x_hbm, u, xb, 0), load(attn_hbm, u, ab, 1), load(cot_hbm, u, cb, 2))
@@ -836,7 +838,7 @@
             base = 0 if way == 1 else half
             dst = sums(i, way + 1)
 
-            @pl.loop(0, half // 16)
+            @pl.loop(0, half // 16, unroll=3)
             def _(r):
                 rows = pl.ds(pl.multiple_of(base + r * 16, 16), 16)
                 dst[rows, :n] = (dst[rows, :n].astype(F32) + added[rows, :n].astype(F32)).astype(BF)
@@ -945,7 +947,7 @@
         dst = send.at[(12 + u) % 3]
         low = (u % 2) * 4 * HEAD
 
-        @pl.loop(0, width // TILE)
+        @pl.loop(0, width // TILE, unroll=3)
         def _(n):
             dst[:, tile(n)] = dot_t(stage[u // 2, :, low : low + 4 * HEAD], w_back[tile(n)]).astype(BF)
 
@@ -986,12 +988,17 @@
             for copy in copies:
                 copy.wait()
 
-            @pl.loop(0, half // 16)
+            @pl.loop(0, half // 16, unroll=3)
             def _(r):
                 rows = pl.ds(pl.multiple_of(r * 16, 16), 16)
                 v = cb[rows, :n].astype(F32) + act[rows, :n].astype(F32) + stage[2, rows, :n].astype(F32)
+                cb[rows, :n] = v.astype(BF)
                 v = v * v
                 gain_ref[4, :, :n] += v[:8] + v[8:]
+
+            copy = pltpu.make_async_copy(cb.at[:half, :n], own_hbm.at[i, low : low + half, :n], fin_sem.at[0])
+            copy.start()
+            copy.wait()
 
     table = weights.at[1, 4 * UNIT + 4 * rows_own :]
 
@@ -1049,25 +1056,28 @@
     last(0)
     start_all(last_loads(1))
     boundary(None, 11, 10, 9)
-    scatter_end(0)
     last(1)
     attention_back(0)
     start_all(last_loads(2))
     w_load.wait()
     project_back(0)
-    boundary(12, None, 11, 10)
+    boundary(12)
+    scatter_end(0)
     project_back(1)
+    boundary(None, None, 11, 10)
     last(2)
     start_all(last_loads(3))
     scatter_start(1)
     operands_start(2)
-    boundary(13, 12, None, 11)
-    scatter_end(1)
+    boundary(13, 12)
+    boundary(None, None, None, 11)
     last(3)
     attention_back(1)
     start_all(first_loads(0))
     project_back(2)
-    boundary(14, 13, 12)
+    boundary(14)
+    scatter_end(1)
+    boundary(None, 13, 12)
     project_back(3)
     scatter_start(2)
     operands_start(3)
@@ -1149,7 +1159,6 @@
             pltpu.VMEM((UNIT, width), BF),
             pltpu.VMEM((width, UNIT), BF),
             pltpu.VMEM((3, UNIT, units), BF),
-            pltpu.VMEM((UNIT, out_cols), BF),
             pltpu.VMEM((2, 2, UNIT, HEAD // 2), F32),
             dma((3, 4)),
             dma((3, 4)),
@@ -1205,7 +1214,7 @@
     low = [w.astype(BF) for w in masters[:4]]
     owns = (jnp.concatenate(low[:3], axis=1), low[3], *masters[4:7])
     gains_own = jnp.zeros((16, width), F32)
-    gains_own = lax.dynamic_update_slice(gains_own, jnp.stack(masters[7:]), (0, place))
+    gains_own = lax.dynamic_update_slice(gains_own, jnp.concatenate(masters[7:]).reshape(4, own), (0, place))
     start = lax.axis_index("ctx") * tokens
     frequency = jnp.exp(
         jnp.arange(HEAD // 2, dtype=F32) * (-2.0 * math.log(10000.0) / HEAD)
@@ -1217,11 +1226,10 @@
     x = inputs.reshape(flat)
     outs = layer_call(first_row, gains_own, cosine, sine, x, cotangent.reshape(flat), owns)
     output, gain_grads, norm_tile = outs[0], outs[9], outs[10]
-    input_grad, own_sum, by_x, by_y = outs[19:23]
+    input_grad, grad_sum = outs[19:21]
 
     def final_sum(i, cols):
-        picked = [v[i, :, :cols].astype(F32) for v in (own_sum, by_x, by_y)]
-        return picked[0] + picked[1] + picked[2]
+        return grad_sum[i, :, :cols].astype(F32)
 
     qkv_cols = owns[0].shape[1]
     s_down, s_gate, s_up = [final_sum(i, width_ff) for i in range(3)]

time: 670 us -> 656 us (0.979)
  Pallas kernels: 618 us -> 608 us
    pallas_call x1, Pallas kernels: 618 us -> 608 us  [layer_call(): pl.pallas_call(layer_kernel, out_shape=outs, in_specs=[vmem] * 2 + [anywh...]
where the time goes in v7:
time: 656 us; the launch traced here: 647 us
  Pallas kernels  608 us (93%)
  other arithmetic  27 us (4%)
  local copies, waits for them, and re-layouts  9.65 us (1%)
    pallas_call x1, Pallas kernels, layer_call(): pl.pallas_call(layer_kernel, out_shape=outs, in_specs=[vmem] * 2 + [anywh...  608 us
    mul x3, other arithmetic, fast_device(): -RATE * (m + 0.01 * w)  15.5 us

profile of v7, /device:TPU:0, one launch (start us, length us, event | category | flops | bytes accessed | tf_op | source)
XLA Modules:
  0.0 646.8 jit_solution(15009546295603210893)
XLA Ops:
  0.7 0.0 copy-start.4
  0.7 0.0 copy-start.3
  0.7 0.9 concatenate.6
  1.6 0.1 reshape.103
  1.7 0.6 dynamic_update_slice.3.gains_own
  2.3 0.0 copy-start.6
  2.3 1.4 fusion.10
  3.7 3.0 multiply_sine_fusion
  6.7 0.0 copy-done.6
  6.7 1.1 convert_element_type.46
  7.8 1.0 convert_element_type.47
  8.8 0.0 copy-done.4
  8.9 0.9 pad_maximum_fusion.own_qkv
  9.8 0.0 copy-done.3
  9.8 0.8 convert_element_type.49.own_out
  10.5 0.0 copy-start.9
  10.5 0.0 copy-start.10
  10.5 0.0 copy-start.11
  10.5 0.0 copy-start.12
  10.5 0.0 copy-start.2
  10.5 608.2 %layer.1 = (bf16[1024,2304]{1,0:T(8,128)(2,1)}, bf16[2304,1024]{1,0:T(8,128)(2,1)}, bf16[1024,2304]{1,0:T(8,128)(2,1)}, bf16[2304,1024]{1,0:T(8,128)(2,1)}, bf16...) custom-call(s32[2,1,512]{2,1,0:T(1,128)} %get-tuple-element.79.first, ...), custom_call_target="tpu_custom_call" | custom-call | tf_op jit(solution)/shard_map/layer/pallas_call | solution.py:1144
  618.7 1.2 slice.39
  620.6 1.0 fusion.3
  621.6 0.0 copy-done.9
  621.6 0.0 copy-done.10
  621.6 0.6 multiply_add_fusion
  622.2 0.0 copy-done.11
  622.2 0.0 copy-done.12
  622.2 0.6 multiply_add_fusion.2
  622.8 1.2 bitcast_convert_fusion
  624.0 0.0 copy-done.2
  624.0 0.0 copy-start
  624.0 0.0 copy-start.1
  624.0 3.3 add_multiply_fusion.3
  627.3 0.0 copy-done
  627.3 0.6 copy-done.1
  627.9 11.1 %add_multiply_fusion = (f32[288,2304]{1,0:T(8,128)}, f32[288,2304]{1,0:T(8,128)}, f32[288,2304]{1,0:T(8,128)}, f32[288,2304]{1,0:T(8,128)}, f32[288,2304]{1,0:T(8,128)}, /*index=5*/f32[288,2304]{1,0:T(8,128)}) fusion(f32[288,2304]{1,0:T(8,128)} %own_down.1, bf16[5,288,2304]{2,1,0:T(8,128)(2,1)} %get-tuple-element.29, f32[]{:T(128)} %bitcast.8, ...), kind=kLoop, calls=%fused_computation.3 | loop fusion | flops 13934592 | bytes 35831812 | tf_op jit(solution)/shard_map/mul | solution.py:1246
  639.0 0.0 copy-done.5
  639.0 0.0 copy-done.7
  639.1 0.0 copy-done.8
  639.1 1.1 add_multiply_fusion.5
  640.2 0.0 slice-done.2
  640.2 0.0 slice-done.3
  640.2 0.0 slice-start.1
  640.2 2.4 copy.51
  642.6 1.5 slice-done
  644.1 0.1 slice-done.1
  644.2 2.2 copy.52
  (12 shorter events, 0.1 us)
Async XLA Ops:
  0.7 8.2 %copy-start.4 = (f32[288,256]{1,0:T(8,128)S(1)}, f32[288,256]{1,0:T(8,128)}, u32[]{:S(2)}) copy-start(f32[288,256]{1,0:T(8,128)} %param.31) | copy-start | bytes 884740
  0.7 9.1 %copy-start.3 = (f32[288,512]{1,0:T(8,128)S(1)}, f32[288,512]{1,0:T(8,128)}, u32[]{:S(2)}) copy-start(f32[288,512]{1,0:T(8,128)} %param.32) | copy-start | bytes 1769476
  2.3 4.4 copy-start.6
  10.5 611.1 %copy-start.9 = (f32[288]{0:T(512)S(1)}, f32[288]{0:T(512)}, u32[]{:S(2)}) copy-start(f32[288]{0:T(512)} %param.50) | copy-start | bytes 3460
  10.5 611.1 %copy-start.10 = (f32[288]{0:T(512)S(1)}, f32[288]{0:T(512)}, u32[]{:S(2)}) copy-start(f32[288]{0:T(512)} %param.49) | copy-start | bytes 3460
  10.5 611.7 %copy-start.11 = (f32[288]{0:T(512)S(1)}, f32[288]{0:T(512)}, u32[]{:S(2)}) copy-start(f32[288]{0:T(512)} %param.48) | copy-start | bytes 3460
  10.5 611.7 %copy-start.12 = (f32[288]{0:T(512)S(1)}, f32[288]{0:T(512)}, u32[]{:S(2)}) copy-start(f32[288]{0:T(512)} %param.47) | copy-start | bytes 3460
  10.5 613.5 %copy-start.2 = (f32[288,512]{1,0:T(8,128)S(1)}, f32[288,512]{1,0:T(8,128)}, u32[]{:S(2)}) copy-start(f32[288,512]{1,0:T(8,128)} %param.29) | copy-start | bytes 1769476
  624.0 3.3 copy-start
  624.0 3.9 copy-start.1
  627.3 12.9 %slice-start.2 = ((s8[4718592]{0:T(1024)(128)(4,1)}), s8[4194304]{0:T(1024)(128)(4,1)S(1)}, s32[]{:S(2)}) async-start(s8[4718592]{0:T(1024)(128)(4,1)} %bitcast.29), calls=%async_computation.2 | async-start | bytes 8388608
  627.9 11.1 %copy-start.5 = (f32[288,256]{1,0:T(8,128)S(1)}, f32[288,256]{1,0:T(8,128)}, u32[]{:S(2)}) copy-start(f32[288,256]{1,0:T(8,128)} %param.30) | copy-start | bytes 884740
  627.9 11.1 %copy-start.7 = (f32[288,256]{1,0:T(8,128)S(1)}, f32[288,256]{1,0:T(8,128)}, u32[]{:S(2)}) copy-start(f32[288,256]{1,0:T(8,128)} %param.42) | copy-start | bytes 884740
  627.9 11.1 %copy-start.8 = (f32[288,256]{1,0:T(8,128)S(1)}, f32[288,256]{1,0:T(8,128)}, u32[]{:S(2)}) copy-start(f32[288,256]{1,0:T(8,128)} %param.41) | copy-start | bytes 884740
  627.9 12.2 %slice-start.3 = ((s8[4718592]{0:T(1024)(128)(4,1)}), s8[524288]{0:T(1024)(128)(4,1)S(1)}, s32[]{:S(2)}) async-start(s8[4718592]{0:T(1024)(128)(4,1)} %bitcast.29), calls=%async_computation.3 | async-start | bytes 1048576
  640.2 3.9 slice-start
  640.2 4.0 slice-start.1

commit v8 on v7

--- a/solution.py
+++ b/solution.py
@@ -776,14 +776,14 @@
         owner = (dp ^ mask) * 2 + ((1 - core) if other else core)
         return pl.ds(pl.multiple_of(owner * rows_own, 16), rows_own)
 
-    def scatter_start(i):
+    def pieces(i):
+        piece = 768 if columns(i) % 768 == 0 else 512
+        return columns(i) // piece, lambda n: pl.ds(pl.multiple_of(n * piece, TILE), piece)
+
+    def scatter_theirs(i):
         for copy in operands(i):
             copy.wait()
-        piece = 768 if columns(i) % 768 == 0 else 512
-        steps = columns(i) // piece
-
-        def piece_at(n):
-            return pl.ds(pl.multiple_of(n * piece, TILE), piece)
+        steps, piece_at = pieces(i)
 
         for m in (3, 2, 1, 0):
             if m < 2:
@@ -797,6 +797,9 @@
                 dst[:, piece_at(n)] = dot(left[block_rows(m, True)], right[:, piece_at(n)]).astype(BF)
 
             core_copy(i, m).start()
+
+    def scatter_mine(i):
+        steps, piece_at = pieces(i)
         if i > 1:
             for way in (0, 1):
                 far_copy(i - 2, way).wait_send()
@@ -821,6 +824,10 @@
                 far_copy(i, 0).start()
                 far_copy(i, 1).start()
         own_store(i).start()
+
+    def scatter_start(i):
+        scatter_theirs(i)
+        scatter_mine(i)
 
     def operands_start(i):
         for copy in operands(i):
@@ -1057,42 +1064,43 @@
     start_all(last_loads(1))
     boundary(None, 11, 10, 9)
     last(1)
+    scatter_end(0)
     attention_back(0)
     start_all(last_loads(2))
     w_load.wait()
     project_back(0)
     boundary(12)
-    scatter_end(0)
     project_back(1)
     boundary(None, None, 11, 10)
+    scatter_start(1)
+    operands_start(2)
     last(2)
     start_all(last_loads(3))
-    scatter_start(1)
-    operands_start(2)
     boundary(13, 12)
     boundary(None, None, None, 11)
     last(3)
+    scatter_end(1)
     attention_back(1)
     start_all(first_loads(0))
     project_back(2)
     boundary(14)
-    scatter_end(1)
+    scatter_theirs(2)
     boundary(None, 13, 12)
     project_back(3)
-    scatter_start(2)
+    scatter_mine(2)
     operands_start(3)
     boundary(15, 14, 13, 12)
     scatter_end(2)
-    first_back(0)
     scatter_start(3)
     for u in range(4):
         proj_store(u).wait()
     operands_start(4)
+    first_back(0)
     finish(0)
     finish(1)
     boundary(None, 15, 14, 13)
+    scatter_start(4)
     scatter_end(3)
-    scatter_start(4)
     first_back(1)
     boundary(None, None, 15, 14)
     scatter_end(4)

time: 656 us -> 653 us (level)
  no operation moved by 1% of the time
where the time goes in v8:
time: 653 us; the launch traced here: 644 us
  Pallas kernels  605 us (93%)
  other arithmetic  27 us (4%)
  local copies, waits for them, and re-layouts  9.65 us (1%)
    pallas_call x1, Pallas kernels, layer_call(): pl.pallas_call(layer_kernel, out_shape=outs, in_specs=[vmem] * 2 + [anywh...  605 us
    mul x3, other arithmetic, fast_device(): -RATE * (m + 0.01 * w)  15.5 us

profile of v8, /device:TPU:0, one launch (start us, length us, event | category | flops | bytes accessed | tf_op | source)
XLA Modules:
  0.0 644.0 jit_solution(1661366377169403001)
XLA Ops:
  0.7 0.0 copy-start.4
  0.7 0.0 copy-start.3
  0.7 0.9 concatenate.6
  1.6 0.1 reshape.103
  1.7 0.6 dynamic_update_slice.3.gains_own
  2.3 0.0 copy-start.6
  2.3 1.4 fusion.10
  3.7 3.0 multiply_sine_fusion
  6.7 0.0 copy-done.6
  6.7 1.1 convert_element_type.46
  7.8 1.0 convert_element_type.47
  8.8 0.0 copy-done.4
  8.9 0.9 pad_maximum_fusion.own_qkv
  9.8 0.0 copy-done.3
  9.8 0.8 convert_element_type.49.own_out
  10.5 0.0 copy-start.9
  10.5 0.0 copy-start.10
  10.5 0.0 copy-start.11
  10.5 0.0 copy-start.12
  10.5 0.0 copy-start.2
  10.5 605.4 %layer.1 = (bf16[1024,2304]{1,0:T(8,128)(2,1)}, bf16[2304,1024]{1,0:T(8,128)(2,1)}, bf16[1024,2304]{1,0:T(8,128)(2,1)}, bf16[2304,1024]{1,0:T(8,128)(2,1)}, bf16...) custom-call(s32[2,1,512]{2,1,0:T(1,128)} %get-tuple-element.79.first, ...), custom_call_target="tpu_custom_call" | custom-call | tf_op jit(solution)/shard_map/layer/pallas_call | solution.py:1152
  616.0 1.2 slice.39
  617.8 1.0 fusion.3
  618.8 0.0 copy-done.9
  618.8 0.0 copy-done.10
  618.9 0.6 multiply_add_fusion
  619.4 0.0 copy-done.11
  619.4 0.0 copy-done.12
  619.4 0.6 multiply_add_fusion.2
  620.0 1.2 bitcast_convert_fusion
  621.2 0.0 copy-done.2
  621.2 0.0 copy-start
  621.2 0.0 copy-start.1
  621.2 3.3 add_multiply_fusion.3
  624.5 0.0 copy-done
  624.5 0.6 copy-done.1
  625.2 11.1 %add_multiply_fusion = (f32[288,2304]{1,0:T(8,128)}, f32[288,2304]{1,0:T(8,128)}, f32[288,2304]{1,0:T(8,128)}, f32[288,2304]{1,0:T(8,128)}, f32[288,2304]{1,0:T(8,128)}, /*index=5*/f32[288,2304]{1,0:T(8,128)}) fusion(f32[288,2304]{1,0:T(8,128)} %own_down.1, bf16[5,288,2304]{2,1,0:T(8,128)(2,1)} %get-tuple-element.29, f32[]{:T(128)} %bitcast.8, ...), kind=kLoop, calls=%fused_computation.3 | loop fusion | flops 13934592 | bytes 35831812 | tf_op jit(solution)/shard_map/mul | solution.py:1254
  636.3 0.0 copy-done.5
  636.3 0.0 copy-done.7
  636.3 0.0 copy-done.8
  636.3 1.1 add_multiply_fusion.5
  637.4 0.0 slice-done.2
  637.4 0.0 slice-done.3
  637.4 0.0 slice-start.1
  637.4 2.4 copy.51
  639.8 1.5 slice-done
  641.3 0.1 slice-done.1
  641.4 2.2 copy.52
  (12 shorter events, 0.1 us)
Async XLA Ops:
  0.7 8.2 %copy-start.4 = (f32[288,256]{1,0:T(8,128)S(1)}, f32[288,256]{1,0:T(8,128)}, u32[]{:S(2)}) copy-start(f32[288,256]{1,0:T(8,128)} %param.31) | copy-start | bytes 884740
  0.7 9.1 %copy-start.3 = (f32[288,512]{1,0:T(8,128)S(1)}, f32[288,512]{1,0:T(8,128)}, u32[]{:S(2)}) copy-start(f32[288,512]{1,0:T(8,128)} %param.32) | copy-start | bytes 1769476
  2.3 4.4 copy-start.6
  10.5 608.3 %copy-start.9 = (f32[288]{0:T(512)S(1)}, f32[288]{0:T(512)}, u32[]{:S(2)}) copy-start(f32[288]{0:T(512)} %param.50) | copy-start | bytes 3460
  10.5 608.3 %copy-start.10 = (f32[288]{0:T(512)S(1)}, f32[288]{0:T(512)}, u32[]{:S(2)}) copy-start(f32[288]{0:T(512)} %param.49) | copy-start | bytes 3460
  10.5 608.9 %copy-start.11 = (f32[288]{0:T(512)S(1)}, f32[288]{0:T(512)}, u32[]{:S(2)}) copy-start(f32[288]{0:T(512)} %param.48) | copy-start | bytes 3460
  10.5 608.9 %copy-start.12 = (f32[288]{0:T(512)S(1)}, f32[288]{0:T(512)}, u32[]{:S(2)}) copy-start(f32[288]{0:T(512)} %param.47) | copy-start | bytes 3460
  10.5 610.7 %copy-start.2 = (f32[288,512]{1,0:T(8,128)S(1)}, f32[288,512]{1,0:T(8,128)}, u32[]{:S(2)}) copy-start(f32[288,512]{1,0:T(8,128)} %param.29) | copy-start | bytes 1769476
  621.2 3.3 copy-start
  621.2 3.9 copy-start.1
  624.5 12.9 %slice-start.2 = ((s8[4718592]{0:T(1024)(128)(4,1)}), s8[4194304]{0:T(1024)(128)(4,1)S(1)}, s32[]{:S(2)}) async-start(s8[4718592]{0:T(1024)(128)(4,1)} %bitcast.29), calls=%async_computation.2 | async-start | bytes 8388608
  625.2 11.1 %copy-start.5 = (f32[288,256]{1,0:T(8,128)S(1)}, f32[288,256]{1,0:T(8,128)}, u32[]{:S(2)}) copy-start(f32[288,256]{1,0:T(8,128)} %param.30) | copy-start | bytes 884740
  625.2 11.1 %copy-start.7 = (f32[288,256]{1,0:T(8,128)S(1)}, f32[288,256]{1,0:T(8,128)}, u32[]{:S(2)}) copy-start(f32[288,256]{1,0:T(8,128)} %param.42) | copy-start | bytes 884740
  625.2 11.1 %copy-start.8 = (f32[288,256]{1,0:T(8,128)S(1)}, f32[288,256]{1,0:T(8,128)}, u32[]{:S(2)}) copy-start(f32[288,256]{1,0:T(8,128)} %param.41) | copy-start | bytes 884740
  625.2 12.2 %slice-start.3 = ((s8[4718592]{0:T(1024)(128)(4,1)}), s8[524288]{0:T(1024)(128)(4,1)S(1)}, s32[]{:S(2)}) async-start(s8[4718592]{0:T(1024)(128)(4,1)} %bitcast.29), calls=%async_computation.3 | async-start | bytes 1048576
  637.4 3.9 slice-start
  637.4 4.0 slice-start.1
